TPU v7x, 32 devices: a whole 2x2x4 slice. The times are simulated.
32 devices in a mesh: fsdp: 8 (over z, x), rep: 4 (over y, core).
Axes of the slice: x: 2, y: 2, z: 4, core: 2. Of those that a mesh axis runs over, the one named last changes fastest.
Arguments:
- inputs: bfloat16 [32, 512, 768], P(('fsdp', 'rep')), may hold values from -6 to 6
- lengths: int32 [32], P(('fsdp', 'rep')), may hold values from 128 to 512, as said below
- cotangent: bfloat16 [32, 512, 768], P(('fsdp', 'rep')), may hold values from -6 to 6
- query_weight: bfloat16 [768, 768], P('fsdp'), may hold values from -0.02734375 to 0.02734375
- key_weight: bfloat16 [768, 768], P('fsdp'), may hold values from -0.21875 to 0.21875
- value_weight: bfloat16 [768, 768], P('fsdp'), may hold values from -0.21875 to 0.21875
- output_weight: bfloat16 [768, 768], P('fsdp'), may hold values from -6 to 6
- attention_gain: bfloat16 [768], P('fsdp'), may hold values from 0.099609375 to 1.8984375
- bias_table: bfloat16 [32, 12], P('fsdp'), may hold values from -4 to 4
- inner_weight: bfloat16 [768, 3072], P('fsdp'), may hold values from -0.21875 to 0.21875
- outer_weight: bfloat16 [3072, 768], P('fsdp'), may hold values from -0.109375 to 0.109375
- feedforward_gain: bfloat16 [768], P('fsdp'), may hold values from 0.099609375 to 1.8984375
Outputs:
- block_output: bfloat16 [32, 512, 768], P(('fsdp', 'rep'))
- input_grad: float32 [32, 512, 768], P(('fsdp', 'rep'))
- query_grad: float32 [768, 768], P('fsdp')
- key_grad: float32 [768, 768], P('fsdp')
- value_grad: float32 [768, 768], P('fsdp')
- output_grad: float32 [768, 768], P('fsdp')
- attention_gain_grad: float32 [768], P('fsdp')
- bias_table_grad: float32 [32, 12], P('fsdp')
- inner_grad: float32 [768, 3072], P('fsdp')
- outer_grad: float32 [3072, 768], P('fsdp')
- feedforward_gain_grad: float32 [768], P('fsdp')
Inputs may be any that keep to these rules, and one draw needn't show every extreme that they name: `lengths`: positions below a pair's entry hold the pair, the rest of its 512 slots is padding; some pair has exactly 512 and some exactly 128.
All inputs are finite; a program needn't handle non-finite values.
Results may differ from a plain program's by a relative error of at most 0.02.
Values may be sent and summed in bfloat16 or wider, within the bound.
A program may use at most 192 MiB of HBM per device.

v0:
```python
import math

import jax
import jax.numpy as jnp
from jax import lax
from jax.sharding import PartitionSpec as P

NB = 32


epsilon = 1e-06
highest = lax.Precision.HIGHEST
gelu_coeff = 0.7978845608028654
masked_score = -1e30


def bucket_of(offset):
    half_count = NB // 2
    exact_count = half_count // 2
    distance = jnp.abs(offset)
    beyond = jnp.full(offset.shape, exact_count, jnp.int32)
    for exponent in range(1, half_count - exact_count):
        beyond = beyond + (distance * distance >= exact_count * exact_count * 2**exponent).astype(
            jnp.int32
        )
    nearby = jnp.where(distance < exact_count, distance, beyond)
    return jnp.where(offset > 0, half_count, 0).astype(jnp.int32) + nearby


def rms_norm(values, gain_vector):
    inverse_rms = lax.rsqrt(jnp.mean(values * values, axis=-1, keepdims=True) + epsilon)
    return values * inverse_rms * gain_vector


def gelu(values):
    return (
        0.5 * values * (1.0 + jnp.tanh(gelu_coeff * (values + 0.044715 * values * values * values)))
    )


def toeplitz(relative, seq_len):
    tiled_rows = jnp.tile(relative, (1, seq_len + 1))[:, : seq_len * (2 * seq_len - 1)]
    return tiled_rows.reshape(relative.shape[0], seq_len, 2 * seq_len - 1)[:, :, :seq_len]


def diagonal_sums(grad_block, seq_len):
    head_here = grad_block.shape[0]
    padded = jnp.pad(grad_block, ((0, 0), (0, 0), (0, seq_len - 1))).reshape(
        head_here, seq_len * (2 * seq_len - 1)
    )
    padded = jnp.pad(padded, ((0, 0), (0, seq_len)))
    return jnp.sum(padded.reshape(head_here, seq_len, 2 * seq_len), axis=1)


def to_items(block, layout):
    pairs_here, seq_len, groups, per_item, head_size = layout
    shaped = block.reshape(pairs_here, seq_len, groups, per_item, head_size)
    return jnp.transpose(shaped, (0, 2, 3, 1, 4)).reshape(
        pairs_here * groups, per_item, seq_len, head_size
    )


def from_items(block, layout):
    pairs_here, seq_len, groups, per_item, head_size = layout
    shaped = block.reshape(pairs_here, groups, per_item, seq_len, head_size)
    return jnp.transpose(shaped, (0, 3, 1, 2, 4)).reshape(
        pairs_here * seq_len, groups * per_item * head_size
    )


def item_scores(queries, key_rows, relative, length):
    seq_len = queries.shape[1]
    scores = jnp.einsum("gid,gjd->gij", queries, key_rows, preferred_element_type=jnp.float32)
    scores = scores + toeplitz(relative, seq_len)
    key_valid = jnp.arange(seq_len, dtype=jnp.int32) < length
    return jnp.where(key_valid[None, None, :], scores, masked_score)


def item_forward(packed):
    queries, key_rows, value_rows, relative, length = packed
    scores = item_scores(queries, key_rows, relative, length)
    row_peak = jnp.max(scores, axis=-1, keepdims=True)
    exp_scores = jnp.exp(scores - row_peak)
    row_total = jnp.sum(exp_scores, axis=-1, keepdims=True)
    soft_probs = (exp_scores / row_total).astype(jnp.bfloat16)
    attended = jnp.einsum(
        "gij,gjd->gid", soft_probs, value_rows, preferred_element_type=jnp.float32
    )
    return (attended.astype(jnp.bfloat16), (row_peak + jnp.log(row_total))[:, :, 0])


def item_backward(packed):
    queries, key_rows, value_rows, relative, length, log_total, grad_attended = packed
    seq_len = queries.shape[1]
    scores = item_scores(queries, key_rows, relative, length)
    soft_probs = jnp.exp(scores - log_total[:, :, None])
    grad_probs = jnp.einsum(
        "gid,gjd->gij", grad_attended, value_rows, preferred_element_type=jnp.float32
    )
    centre = jnp.sum(soft_probs * grad_probs, axis=-1, keepdims=True)
    grad_scores = (soft_probs * (grad_probs - centre)).astype(jnp.bfloat16)
    grad_queries = jnp.einsum(
        "gij,gjd->gid", grad_scores, key_rows, preferred_element_type=jnp.float32
    ).astype(jnp.bfloat16)
    grad_keys = jnp.einsum(
        "gij,gid->gjd", grad_scores, queries, preferred_element_type=jnp.float32
    ).astype(jnp.bfloat16)
    grad_values = jnp.einsum(
        "gij,gid->gjd",
        soft_probs.astype(jnp.bfloat16),
        grad_attended,
        preferred_element_type=jnp.float32,
    ).astype(jnp.bfloat16)
    return (
        grad_queries,
        grad_keys,
        grad_values,
        diagonal_sums(grad_scores.astype(jnp.float32), seq_len),
    )


def contract_rows(left, right):
    return lax.dot_general(
        left, right, (((0,), (0,)), ((), ())), preferred_element_type=jnp.float32
    )


def contract_cols(left, right):
    return lax.dot_general(
        left, right, (((1,), (1,)), ((), ())), preferred_element_type=jnp.float32
    )


def local(
    inputs,
    lengths,
    cotangent,
    query_weight,
    key_weight,
    value_weight,
    output_weight,
    attention_gain,
    bias_table,
    inner_weight,
    outer_weight,
    feedforward_gain,
):
    pairs_here, seq_len, model_width = inputs.shape
    row_count = pairs_here * seq_len
    full_query, full_key, full_value, full_output, full_gain, full_table = (
        lax.all_gather(query_weight, "fsdp", axis=0, tiled=True),
        lax.all_gather(key_weight, "fsdp", axis=0, tiled=True),
        lax.all_gather(value_weight, "fsdp", axis=0, tiled=True),
        lax.all_gather(output_weight, "fsdp", axis=0, tiled=True),
        lax.all_gather(attention_gain, "fsdp", axis=0, tiled=True),
        lax.all_gather(bias_table, "fsdp", axis=0, tiled=True),
    )
    head_count = full_table.shape[1]
    head_size = model_width // head_count
    per_item = math.gcd(head_count, 4)
    groups = head_count // per_item
    item_count = pairs_here * groups
    layout = (pairs_here, seq_len, groups, per_item, head_size)
    slot_ids = jnp.arange(2 * seq_len, dtype=jnp.int32)
    offsets = jnp.where(slot_ids < seq_len, slot_ids, slot_ids - 2 * seq_len)
    bucket_hits = (bucket_of(offsets)[:, None] == jnp.arange(NB, dtype=jnp.int32)[None, :]).astype(
        jnp.float32
    )
    relative = jnp.dot(bucket_hits, full_table.astype(jnp.float32), precision=highest).T
    relative_items = relative.reshape(1, groups, per_item, 2 * seq_len).reshape(
        item_count, per_item, 2 * seq_len
    )
    length_items = jnp.repeat(lengths, groups)
    flat_inputs = inputs.reshape(row_count, model_width).astype(jnp.float32)
    normed = rms_norm(flat_inputs, full_gain.astype(jnp.float32)).astype(jnp.bfloat16)
    joined = jnp.concatenate((full_query, full_key, full_value), axis=1)
    projected = jnp.dot(normed, joined, preferred_element_type=jnp.float32).astype(jnp.bfloat16)
    queries = to_items(projected[:, :model_width], layout)
    key_rows = to_items(projected[:, model_width : 2 * model_width], layout)
    value_rows = to_items(projected[:, 2 * model_width :], layout)
    attended_items, log_totals = lax.map(
        item_forward, (queries, key_rows, value_rows, relative_items, length_items)
    )
    attended = from_items(attended_items, layout)
    middle = flat_inputs + jnp.dot(attended, full_output, preferred_element_type=jnp.float32)
    full_inner, full_outer, full_ffn_gain = (
        lax.all_gather(inner_weight, "fsdp", axis=0, tiled=True),
        lax.all_gather(outer_weight, "fsdp", axis=0, tiled=True),
        lax.all_gather(feedforward_gain, "fsdp", axis=0, tiled=True),
    )
    normed_ffn = rms_norm(middle, full_ffn_gain.astype(jnp.float32)).astype(jnp.bfloat16)
    raised = jnp.dot(normed_ffn, full_inner, preferred_element_type=jnp.float32)
    active = gelu(raised).astype(jnp.bfloat16)
    lowered = jnp.dot(active, full_outer, preferred_element_type=jnp.float32)
    block_output = (middle + lowered).astype(jnp.bfloat16).reshape(pairs_here, seq_len, model_width)
    positions = jnp.arange(seq_len, dtype=jnp.int32)
    row_live = (positions[None, :] < lengths[:, None]).astype(jnp.float32)
    seed_rows = (cotangent.astype(jnp.float32) * row_live[:, :, None]).reshape(
        row_count, model_width
    )
    full_inner, full_outer, full_ffn_gain = (
        lax.all_gather(inner_weight, "fsdp", axis=0, tiled=True),
        lax.all_gather(outer_weight, "fsdp", axis=0, tiled=True),
        lax.all_gather(feedforward_gain, "fsdp", axis=0, tiled=True),
    )
    seed_low = seed_rows.astype(jnp.bfloat16)
    grad_active = contract_cols(seed_low, full_outer)
    grad_outer = contract_rows(active, seed_low)
    grad_raised = jax.vjp(gelu, raised)[1](grad_active)[0].astype(jnp.bfloat16)
    grad_inner = contract_rows(normed_ffn, grad_raised)
    grad_normed_ffn = contract_cols(grad_raised, full_inner)
    ffn_pull = jax.vjp(rms_norm, middle, full_ffn_gain.astype(jnp.float32))[1]
    grad_middle_part, grad_ffn_gain = ffn_pull(grad_normed_ffn)
    grad_middle = seed_rows + grad_middle_part
    full_query, full_key, full_value, full_output, full_gain, full_table = (
        lax.all_gather(query_weight, "fsdp", axis=0, tiled=True),
        lax.all_gather(key_weight, "fsdp", axis=0, tiled=True),
        lax.all_gather(value_weight, "fsdp", axis=0, tiled=True),
        lax.all_gather(output_weight, "fsdp", axis=0, tiled=True),
        lax.all_gather(attention_gain, "fsdp", axis=0, tiled=True),
        lax.all_gather(bias_table, "fsdp", axis=0, tiled=True),
    )
    joined = jnp.concatenate((full_query, full_key, full_value), axis=1)
    middle_low = grad_middle.astype(jnp.bfloat16)
    grad_attended = contract_cols(middle_low, full_output).astype(jnp.bfloat16)
    grad_output = contract_rows(attended, middle_low)
    grad_query_items, grad_key_items, grad_value_items, grad_rel_items = lax.map(
        item_backward,
        (
            queries,
            key_rows,
            value_rows,
            relative_items,
            length_items,
            log_totals,
            to_items(grad_attended, layout),
        ),
    )
    grad_projected = jnp.concatenate(
        (
            from_items(grad_query_items, layout),
            from_items(grad_key_items, layout),
            from_items(grad_value_items, layout),
        ),
        axis=1,
    )
    grad_joined = contract_rows(normed, grad_projected)
    grad_normed = contract_cols(grad_projected, joined)
    attention_pull = jax.vjp(rms_norm, flat_inputs, full_gain.astype(jnp.float32))[1]
    grad_inputs_part, grad_attention_gain = attention_pull(grad_normed)
    input_grad = (grad_middle + grad_inputs_part).reshape(pairs_here, seq_len, model_width)
    grad_relative = jnp.sum(grad_rel_items.reshape(pairs_here, head_count, 2 * seq_len), axis=0)
    grad_table = jnp.dot(bucket_hits.T, grad_relative.T, precision=highest)
    gradients = (
        grad_joined[:, :model_width],
        grad_joined[:, model_width : 2 * model_width],
        grad_joined[:, 2 * model_width :],
        grad_output,
        grad_attention_gain,
        grad_table,
        grad_inner,
        grad_outer,
        grad_ffn_gain,
    )
    shard_inner, shard_outer, shard_ffn_gain = (
        lax.psum_scatter(
            gradients[6].astype(jnp.bfloat16), "fsdp", scatter_dimension=0, tiled=True
        ).astype(jnp.float32),
        lax.psum_scatter(
            gradients[7].astype(jnp.bfloat16), "fsdp", scatter_dimension=0, tiled=True
        ).astype(jnp.float32),
        lax.psum_scatter(
            gradients[8].astype(jnp.bfloat16), "fsdp", scatter_dimension=0, tiled=True
        ).astype(jnp.float32),
    )
    shard_query, shard_key, shard_value, shard_output, shard_attention_gain, shard_table = (
        lax.psum_scatter(
            gradients[0].astype(jnp.bfloat16), "fsdp", scatter_dimension=0, tiled=True
        ).astype(jnp.float32),
        lax.psum_scatter(
            gradients[1].astype(jnp.bfloat16), "fsdp", scatter_dimension=0, tiled=True
        ).astype(jnp.float32),
        lax.psum_scatter(
            gradients[2].astype(jnp.bfloat16), "fsdp", scatter_dimension=0, tiled=True
        ).astype(jnp.float32),
        lax.psum_scatter(
            gradients[3].astype(jnp.bfloat16), "fsdp", scatter_dimension=0, tiled=True
        ).astype(jnp.float32),
        lax.psum_scatter(
            gradients[4].astype(jnp.bfloat16), "fsdp", scatter_dimension=0, tiled=True
        ).astype(jnp.float32),
        lax.psum_scatter(
            gradients[5].astype(jnp.bfloat16), "fsdp", scatter_dimension=0, tiled=True
        ).astype(jnp.float32),
    )
    summed = (
        lax.psum(shard_query.astype(jnp.bfloat16), "rep").astype(jnp.float32),
        lax.psum(shard_key.astype(jnp.bfloat16), "rep").astype(jnp.float32),
        lax.psum(shard_value.astype(jnp.bfloat16), "rep").astype(jnp.float32),
        lax.psum(shard_output.astype(jnp.bfloat16), "rep").astype(jnp.float32),
        lax.psum(shard_attention_gain.astype(jnp.bfloat16), "rep").astype(jnp.float32),
        lax.psum(shard_table.astype(jnp.bfloat16), "rep").astype(jnp.float32),
        lax.psum(shard_inner.astype(jnp.bfloat16), "rep").astype(jnp.float32),
        lax.psum(shard_outer.astype(jnp.bfloat16), "rep").astype(jnp.float32),
        lax.psum(shard_ffn_gain.astype(jnp.bfloat16), "rep").astype(jnp.float32),
    )
    return (
        block_output,
        input_grad,
        summed[0],
        summed[1],
        summed[2],
        summed[3],
        summed[4],
        summed[5],
        summed[6],
        summed[7],
        summed[8],
    )


def solution(mesh):
    placed = (
        P(("fsdp", "rep"), None, None),
        P(("fsdp", "rep")),
        P(("fsdp", "rep"), None, None),
        P("fsdp", None),
        P("fsdp", None),
        P("fsdp", None),
        P("fsdp", None),
        P("fsdp"),
        P("fsdp", None),
        P("fsdp", None),
        P("fsdp", None),
        P("fsdp"),
    )
    return jax.shard_map(
        local,
        mesh=mesh,
        in_specs=placed,
        out_specs=(
            P(("fsdp", "rep"), None, None),
            P(("fsdp", "rep"), None, None),
            P("fsdp", None),
            P("fsdp", None),
            P("fsdp", None),
            P("fsdp", None),
            P("fsdp"),
            P("fsdp", None),
            P("fsdp", None),
            P("fsdp", None),
            P("fsdp"),
        ),
        check_vma=False,
    )
```

profile of v0, /device:TPU:1, one launch (start us, length us, event | category | flops | bytes accessed | tf_op | source)
XLA Modules:
  0.0 1144.9 jit_solution(16237137596634835096)
XLA Ops:
  18.2 18.7 %all-reduce.8 = (bf16[768]{0:T(1024)(128)(2,1)S(1)}, bf16[768]{0:T(1024)(128)(2,1)S(1)}) all-reduce(bf16[768]{0:T(1024)(128)(2,1)S(1)} %dynamic-update-slice, bf16[768]{0:T(1024)(128)(2,1)S(1)} %dynamic-update-slice.1), channel_id=1, replica_groups=mesh['fsdp'=8,'rep'=4] {'fsdp'}, use_global_device_ids=true, to_apply=%add.2 | all-reduce | flops 1536 | bytes 6144
  37.5 13.2 %all-gather = bf16[8,4,12]{2,1,0:T(4,128)(2,1)S(1)} all-gather(bf16[1,4,12]{2,1,0:T(4,128)(2,1)} %bitcast.228), channel_id=1, replica_groups=mesh['fsdp'=8,'rep'=4] {'fsdp'}, dimensions={0}, use_global_device_ids=true | all-gather | bytes 864 | tf_op jit(solution)/shard_map/all_gather | solution.py:156
  54.7 39.6 %all-gather.10.cloned.1.call-done = bf16[768,768]{1,0:T(8,128)(2,1)} async-done(((bf16[96,768]{1,0:T(8,128)(2,1)}), bf16[768,768]{1,0:T(8,128)(2,1)}) %all-gather.10.cloned.1.call-update) | async-done | bytes 1179664 | tf_op jit(solution)/shard_map/all_gather | solution.py:152
  96.7 39.6 %all-gather.12.cloned.1.call-done = bf16[768,768]{1,0:T(8,128)(2,1)} async-done(((bf16[96,768]{1,0:T(8,128)(2,1)}), bf16[768,768]{1,0:T(8,128)(2,1)}) %all-gather.12.cloned.1.call-update) | async-done | bytes 1179664 | tf_op jit(solution)/shard_map/all_gather | solution.py:153
  146.8 180.3 %while.30 = (s32[]{:T(128)}, bf16[3,4,512,64]{2,3,1,0:T(8,128)(2,1)}, f32[3,4,512]{2,1,0:T(4,128)S(1)}, s32[3]{0:T(128)S(1)}, bf16[3,4,512,64]{2,3,1,0:T(8,128)(...) while((s32[]{:T(128)}, ...), condition=%wide.region_4.5_spmd, body=%wide.region_1.4_spmd.sunk | while | flops 276953600 | bytes 93457520 | solution.py:181
  164.3 12.1 %copy.70 = f32[1,4,513,1024]{3,1,2,0:T(4,128)} copy(f32[1,4,513,1024]{3,2,1,0:T(8,128)} %broadcast_bitcast_fusion.4) | data formatting | bytes 16809984 | tf_op jit(solution)/shard_map/while
  176.4 7.1 slice.65
  183.5 15.7 %reshape.296 = f32[4,512,1023]{2,1,0:T(8,128)} reshape(f32[4,523776]{1,0:T(4,128)} %slice.65) | data formatting | bytes 16760832 | tf_op jit(solution)/shard_map/while/body/eval_jaxpr/reshape | solution.py:43
  203.8 5.2 copy.71
  220.1 12.1 %copy.70 = f32[1,4,513,1024]{3,1,2,0:T(4,128)} copy(f32[1,4,513,1024]{3,2,1,0:T(8,128)} %broadcast_bitcast_fusion.4) | data formatting | bytes 16809984 | tf_op jit(solution)/shard_map/while
  232.2 7.1 slice.65
  239.4 15.7 %reshape.296 = f32[4,512,1023]{2,1,0:T(8,128)} reshape(f32[4,523776]{1,0:T(4,128)} %slice.65) | data formatting | bytes 16760832 | tf_op jit(solution)/shard_map/while/body/eval_jaxpr/reshape | solution.py:43
  276.0 12.1 %copy.70 = f32[1,4,513,1024]{3,1,2,0:T(4,128)} copy(f32[1,4,513,1024]{3,2,1,0:T(8,128)} %broadcast_bitcast_fusion.4) | data formatting | bytes 16809984 | tf_op jit(solution)/shard_map/while
  288.1 7.1 slice.65
  295.2 16.3 %reshape.296 = f32[4,512,1023]{2,1,0:T(8,128)} reshape(f32[4,523776]{1,0:T(4,128)} %slice.65) | data formatting | bytes 16760832 | tf_op jit(solution)/shard_map/while/body/eval_jaxpr/reshape | solution.py:43
  316.1 5.2 copy.71
  331.2 8.2 fusion.89
  339.4 9.8 fusion.51
  364.0 314.9 %while.31 = (s32[]{:T(128)}, bf16[3,4,512,64]{2,3,1,0:T(8,128)(2,1)}, bf16[3,4,512,64]{2,3,1,0:T(8,128)(2,1)}, bf16[3,4,512,64]{2,3,1,0:T(8,128)(2,1)}, f32[3,4,...) while((s32[]{:T(128)}, ...), condition=%wide.region_10.11_spmd, body=%wide.region_7.10_spmd.sunk | while | flops 685107712 | bytes 191502656 | solution.py:227
  392.8 12.2 %copy.73 = f32[1,4,513,1024]{3,1,2,0:T(4,128)} copy(f32[1,4,513,1024]{3,2,1,0:T(8,128)} %broadcast_bitcast_fusion.5) | data formatting | bytes 16809984 | tf_op jit(solution)/shard_map/while
  404.9 7.1 slice.67
  412.0 15.9 %reshape.298 = f32[4,512,1023]{2,1,0:T(8,128)} reshape(f32[4,523776]{1,0:T(4,128)} %slice.67) | data formatting | bytes 16760832 | tf_op jit(solution)/shard_map/while/body/eval_jaxpr/reshape | solution.py:43
  432.5 5.2 copy.74
  456.7 8.5 reshape.299
  465.1 5.8 reshape.300
  488.9 12.1 %copy.73 = f32[1,4,513,1024]{3,1,2,0:T(4,128)} copy(f32[1,4,513,1024]{3,2,1,0:T(8,128)} %broadcast_bitcast_fusion.5) | data formatting | bytes 16809984 | tf_op jit(solution)/shard_map/while
  501.0 7.1 slice.67
  508.1 15.7 %reshape.298 = f32[4,512,1023]{2,1,0:T(8,128)} reshape(f32[4,523776]{1,0:T(4,128)} %slice.67) | data formatting | bytes 16760832 | tf_op jit(solution)/shard_map/while/body/eval_jaxpr/reshape | solution.py:43
  528.4 5.2 copy.74
  552.6 8.5 reshape.299
  561.1 5.8 reshape.300
  584.9 12.1 %copy.73 = f32[1,4,513,1024]{3,1,2,0:T(4,128)} copy(f32[1,4,513,1024]{3,2,1,0:T(8,128)} %broadcast_bitcast_fusion.5) | data formatting | bytes 16809984 | tf_op jit(solution)/shard_map/while
  597.0 7.1 slice.67
  604.0 15.7 %reshape.298 = f32[4,512,1023]{2,1,0:T(8,128)} reshape(f32[4,523776]{1,0:T(4,128)} %slice.67) | data formatting | bytes 16760832 | tf_op jit(solution)/shard_map/while/body/eval_jaxpr/reshape | solution.py:43
  624.4 5.2 copy.74
  648.6 8.5 reshape.299
  657.0 5.8 reshape.300
  686.4 6.3 convolution_convert_fusion.3
  693.8 8.2 convolution_convert_fusion.2
  704.1 6.4 fusion.57
  710.5 28.4 %all-reduce.7 = (bf16[768]{0:T(1024)(128)(2,1)S(1)}, bf16[32,12]{1,0:T(8,128)(2,1)S(1)}, bf16[768]{0:T(1024)(128)(2,1)S(1)}) all-reduce(bf16[768]{0:T(1024)(128)(2,1)S(1)} %get-tuple-element.214, bf16[32,12]{1,0:T(8,128)(2,1)S(1)} %convolution_convert_fusion.8, ...), channel_id=6, replica_groups=mesh['fsdp'=8,'rep'=4] {'fsdp'}, use_global_device_ids=true, to_apply=%region_21.22.clone | all-reduce | flops 1920 | bytes 7680
  739.1 13.9 %all-reduce.9 = (bf16[96]{0:T(256)(128)(2,1)S(1)}, bf16[4,12]{1,0:T(4,128)(2,1)S(1)}, bf16[96]{0:T(256)(128)(2,1)S(1)}) all-reduce(bf16[96]{0:T(256)(128)(2,1)S(1)} %dynamic-slice.3, bf16[4,12]{1,0:T(4,128)(2,1)S(1)} %constant_dynamic-slice_fusion, bf16[96]{0:T(256)(128)(2,1)S(1)} %dynamic-slice.7), channel_id=1, replica_groups=mesh['fsdp'=8,'rep'=4] {'rep'}, use_global_device_ids=true, to_apply=%region_22.23 | all-reduce | flops 240 | bytes 960 | tf_op jit(solution)/shard_map/psum | solution.py:301
  757.8 56.9 %reduce-scatter.9.cloned.1.call-done = bf16[96,768]{1,0:T(8,128)(2,1)} async-done(((bf16[768,768]{1,0:T(8,128)(2,1)}), bf16[96,768]{1,0:T(8,128)(2,1)}) %reduce-scatter.9.cloned.1.call-update) | async-done | bytes 147472 | tf_op jit(solution)/shard_map/reduce_scatter | solution.py:280
  814.7 66.3 %reduce-scatter.7.cloned.1.call-done = bf16[96,768]{1,0:T(8,128)(2,1)} async-done(((bf16[768,768]{1,0:T(8,128)(2,1)}), bf16[96,768]{1,0:T(8,128)(2,1)}) %reduce-scatter.7.cloned.1.call-update) | async-done | bytes 147472 | tf_op jit(solution)/shard_map/reduce_scatter | solution.py:277
  881.0 99.5 %reduce-scatter.15.cloned.1.call-done = bf16[96,3072]{1,0:T(8,128)(2,1)} async-done(((bf16[768,3072]{1,0:T(8,128)(2,1)}), bf16[96,3072]{1,0:T(8,128)(2,1)}) %reduce-scatter.15.cloned.1.call-update) | async-done | bytes 589840 | tf_op jit(solution)/shard_map/reduce_scatter | solution.py:266
  980.4 98.5 %reduce-scatter.17.cloned.1.call-done = bf16[384,768]{1,0:T(8,128)(2,1)} async-done(((bf16[3072,768]{1,0:T(8,128)(2,1)}), bf16[384,768]{1,0:T(8,128)(2,1)}) %reduce-scatter.17.cloned.1.call-update) | async-done | bytes 589840 | tf_op jit(solution)/shard_map/reduce_scatter | solution.py:269
  1079.0 8.8 fusion.63
  1087.8 40.4 %all-reduce.13.cloned.1.call-done = (bf16[96,768]{1,0:T(8,128)(2,1)}, bf16[96,768]{1,0:T(8,128)(2,1)}, bf16[96,768]{1,0:T(8,128)(2,1)}, bf16[96,768]{1,0:T(8,128...) async-done(((bf16[96,768]{1,0:T(8,128)(2,1)}, bf16[96,768]{1,0:T(8,128)(2,1)}, bf16[96,768]{1,0:T(8,128)(2,1)}, bf16[96,768]{1,0:T(8,128)(2,1)}, ...) | async-done | bytes 1769488 | tf_op jit(solution)/shard_map/psum | solution.py:297
  (251 shorter events, 246.1 us)
Async XLA Ops:
  7.2 45.1 %all-gather.8.cloned.1.call-start = ((), (), s32[]{:S(2)}) async-start(), calls=%async_computation.6 | async-start | bytes 1327104 | tf_op jit(solution)/shard_map/all_gather | solution.py:151
  7.9 86.3 %all-gather.10.cloned.1.call-start = ((), (), s32[]{:S(2)}) async-start(), calls=%async_computation.7 | async-start | bytes 1327104 | tf_op jit(solution)/shard_map/all_gather | solution.py:152
  8.7 127.6 %all-gather.12.cloned.1.call-start = ((), (), s32[]{:S(2)}) async-start(), calls=%async_computation.8 | async-start | bytes 1327104 | tf_op jit(solution)/shard_map/all_gather | solution.py:153
  9.4 317.7 %all-gather.14.cloned.1.call-start = ((), (), s32[]{:S(2)}) async-start(), calls=%async_computation.9 | async-start | bytes 1327104 | tf_op jit(solution)/shard_map/all_gather | solution.py:154
  10.0 321.2 %all-gather.16.cloned.1.call-start = ((), (), s32[]{:S(2)}) async-start(), calls=%async_computation.10 | async-start | bytes 5308416 | tf_op jit(solution)/shard_map/all_gather | solution.py:187
  10.6 328.8 %all-gather.18.cloned.1.call-start = ((), (), s32[]{:S(2)}) async-start(), calls=%async_computation.11 | async-start | bytes 5308416 | tf_op jit(solution)/shard_map/all_gather | solution.py:188
  11.1 746.7 %reduce-scatter.13.cloned.1.call-start = ((), (), s32[]{:S(2)}) async-start(), calls=%async_computation.15 | async-start | bytes 1327104 | tf_op jit(solution)/shard_map/reduce_scatter | solution.py:286
  11.2 39.8 %copy-start.29 = (s32[1024]{0:T(1024)}, s32[1024]{0:T(1024)S(1)}, u32[]{:S(2)}) copy-start(s32[1024]{0:T(1024)S(1)} %fusion.74) | copy-start | bytes 12292
  14.4 124.3 %copy-start.27 = (f32[512]{0:T(512)}, f32[512]{0:T(512)S(1)}, u32[]{:S(2)}) copy-start(f32[512]{0:T(512)S(1)} %fusion.85) | copy-start | bytes 6148
  36.9 101.8 %copy-start.23 = (f32[768]{0:T(1024)}, f32[768]{0:T(1024)S(1)}, u32[]{:S(2)}) copy-start(f32[768]{0:T(1024)S(1)} %convert_element_type.232) | copy-start | bytes 9220
  51.0 87.7 %copy-start.12 = (bf16[1,512,768]{2,1,0:T(8,128)(2,1)S(1)}, bf16[1,512,768]{2,1,0:T(8,128)(2,1)}, u32[]{:S(2)}) copy-start(bf16[1,512,768]{2,1,0:T(8,128)(2,1)} %param.16) | copy-start | bytes 2359300
  327.1 12.3 %copy-start.9 = (bf16[3,4,512,64]{2,3,1,0:T(8,128)(2,1)}, bf16[3,4,512,64]{2,3,1,0:T(8,128)(2,1)S(1)}, u32[]{:S(2)}) copy-start(bf16[3,4,512,64]{2,3,1,0:T(8,128)(2,1)S(1)} %get-tuple-element.511) | copy-start | bytes 2359300
  327.1 4.0 copy-start.16
  331.1 21.6 %copy-start.19 = (f32[512]{0:T(512)}, f32[512]{0:T(512)S(1)}, u32[]{:S(2)}) copy-start(f32[512]{0:T(512)S(1)} %fusion.86) | copy-start | bytes 6148
  331.1 8.2 copy-start.25
  339.4 9.9 copy-start.7
  339.4 9.9 copy-start.10
  349.3 3.4 copy-start.32
  349.3 3.4 copy-start.13
  352.6 1.7 copy-start.11
  356.1 7.8 copy-start.18
  361.0 396.8 %reduce-scatter.11.cloned.1.call-start = ((), (), s32[]{:S(2)}) async-start(), calls=%async_computation.14 | async-start | bytes 1327104 | tf_op jit(solution)/shard_map/reduce_scatter | solution.py:283
  364.0 314.9 %copy-start.24 = (f32[768]{0:T(1024)S(1)}, f32[768]{0:T(1024)}, u32[]{:S(2)}) copy-start(f32[768]{0:T(1024)} %copy-done.23) | copy-start | bytes 9220
  364.0 314.9 %copy-start.28 = (f32[512]{0:T(512)S(1)}, f32[512]{0:T(512)}, u32[]{:S(2)}) copy-start(f32[512]{0:T(512)} %copy-done.27) | copy-start | bytes 6148
  383.2 9.6 copy-start.3
  383.2 54.5 %copy-start.1 = (bf16[3,4,512,64]{2,3,1,0:T(8,128)(2,1)}, bf16[3,4,512,64]{2,3,1,0:T(8,128)(2,1)S(1)}, u32[]{:S(2)}) copy-start(bf16[3,4,512,64]{2,3,1,0:T(8,128)(2,1)S(1)} %get-tuple-element.477) | copy-start | bytes 2359300 | tf_op jit(solution)/shard_map/while
  437.7 5.2 copy-start
  474.9 4.4 copy-start.2
  474.9 4.4 copy-start.4
  479.3 9.6 copy-start.3
  479.3 54.4 %copy-start.1 = (bf16[3,4,512,64]{2,3,1,0:T(8,128)(2,1)}, bf16[3,4,512,64]{2,3,1,0:T(8,128)(2,1)S(1)}, u32[]{:S(2)}) copy-start(bf16[3,4,512,64]{2,3,1,0:T(8,128)(2,1)S(1)} %get-tuple-element.477) | copy-start | bytes 2359300 | tf_op jit(solution)/shard_map/while
  533.7 5.2 copy-start
  570.8 4.4 copy-start.2
  570.8 4.4 copy-start.4
  575.3 9.6 copy-start.3
  575.3 54.4 %copy-start.1 = (bf16[3,4,512,64]{2,3,1,0:T(8,128)(2,1)}, bf16[3,4,512,64]{2,3,1,0:T(8,128)(2,1)S(1)}, u32[]{:S(2)}) copy-start(bf16[3,4,512,64]{2,3,1,0:T(8,128)(2,1)S(1)} %get-tuple-element.477) | copy-start | bytes 2359300 | tf_op jit(solution)/shard_map/while
  629.6 5.2 copy-start
  666.8 4.4 copy-start.2
  666.8 4.4 copy-start.4
  685.0 129.7 %reduce-scatter.9.cloned.1.call-start = ((), (), s32[]{:S(2)}) async-start(), calls=%async_computation.13 | async-start | bytes 1327104 | tf_op jit(solution)/shard_map/reduce_scatter | solution.py:280
  685.7 195.2 %reduce-scatter.7.cloned.1.call-start = ((), (), s32[]{:S(2)}) async-start(), calls=%async_computation.12 | async-start | bytes 1327104 | tf_op jit(solution)/shard_map/reduce_scatter | solution.py:277
  686.3 294.2 %reduce-scatter.15.cloned.1.call-start = ((), (), s32[]{:S(2)}) async-start(), calls=%async_computation.16 | async-start | bytes 5308416 | tf_op jit(solution)/shard_map/reduce_scatter | solution.py:266
  692.7 386.2 %reduce-scatter.17.cloned.1.call-start = ((), (), s32[]{:S(2)}) async-start(), calls=%async_computation.17 | async-start | bytes 5308416 | tf_op jit(solution)/shard_map/reduce_scatter | solution.py:269
  702.1 426.1 %all-reduce.13.cloned.1.call-start = ((), (), s32[]{:S(2)}) async-start(), calls=%async_computation.18 | async-start | bytes 3538944 | tf_op jit(solution)/shard_map/psum | solution.py:297
  704.0 6.4 copy-start.31
  704.0 50.6 %copy-start.22 = (f32[512]{0:T(512)S(1)}, f32[512]{0:T(512)}, u32[]{:S(2)}) copy-start(f32[512]{0:T(512)} %copy-done.21) | copy-start | bytes 6148
  704.1 50.6 %copy-start.6 = (f32[512,768]{1,0:T(8,128)S(1)}, f32[512,768]{1,0:T(8,128)}, u32[]{:S(2)}) copy-start(f32[512,768]{1,0:T(8,128)} %copy-done.5) | copy-start | bytes 4718596
  1128.2 8.8 copy-start.15
  (8 other events, 9.6 us)
Sparse Core Ops, SparseCore 0:
  10.2 42.0 all-gather.7
  54.4 39.7 all-gather.9
  96.4 39.8 all-gather.11
  138.3 39.8 all-gather.13
  180.2 78.9 all-gather.15
  261.3 77.9 all-gather.17
  361.2 62.5 reduce-scatter.12
  685.1 62.7 reduce-scatter.10
  751.8 62.8 reduce-scatter.8
  817.9 62.9 reduce-scatter.6
  884.6 95.7 reduce-scatter.14
  983.9 94.9 reduce-scatter.16
  1081.8 46.4 all-reduce.12
where the time goes:
time: 1150 us; the launch traced here: 1140 us
  waiting for transfers between devices  447 us (39%)
  local copies, waits for them, and re-layouts  386 us (34%)
  matrix products  129 us (11%)
  blocking collectives  74.3 us (6%)
  other arithmetic  51.8 us (5%)
  loops' own time  39.5 us (3%)
  between operations  17.1 us (1%)
    while x54, local copies, waits for them, and re-layouts  163 us
    reduce_scatter x1, waiting for transfers between devices, local(): lax.psum_scatter(gradients[6].astype(jnp.bfloat16), 'fsdp', scatter_dimen...  99.5 us
    reduce_scatter x1, waiting for transfers between devices, local(): lax.psum_scatter(gradients[7].astype(jnp.bfloat16), 'fsdp', scatter_dimen...  98.5 us
    reshape x6, local copies, waits for them, and re-layouts, toeplitz(): tiled_rows.reshape(relative.shape[0], seq_len, 2 * seq_len - 1)  95.1 us
    reduce_scatter x1, waiting for transfers between devices, local(): lax.psum_scatter(gradients[0].astype(jnp.bfloat16), 'fsdp', scatter_dimen...  66.3 us
    reduce_scatter x1, waiting for transfers between devices, local(): lax.psum_scatter(gradients[1].astype(jnp.bfloat16), 'fsdp', scatter_dimen...  56.9 us
    unnamed x2, blocking collectives  47.2 us
    slice x6, local copies, waits for them, and re-layouts, toeplitz(): jnp.tile(relative, (1, seq_len + 1))[:, :seq_len * (2 * seq_len - 1)]  42.5 us
  transfers between devices with their start and end apart: 13, of which 8 were waited for; matrix products, arithmetic and copies ran while one was open for 47% of the time, Pallas kernels for 0%

commit v1 on v0

--- a/solution.py
+++ b/solution.py
@@ -1,8 +1,10 @@
-import math
+import functools
 
 import jax
 import jax.numpy as jnp
 from jax import lax
+import jax.experimental.pallas as pl
+import jax.experimental.pallas.tpu as pltpu
 from jax.sharding import PartitionSpec as P
 
 NB = 32
@@ -38,86 +40,116 @@
     )
 
 
-def toeplitz(relative, seq_len):
-    tiled_rows = jnp.tile(relative, (1, seq_len + 1))[:, : seq_len * (2 * seq_len - 1)]
-    return tiled_rows.reshape(relative.shape[0], seq_len, 2 * seq_len - 1)[:, :, :seq_len]
-
-
-def diagonal_sums(grad_block, seq_len):
-    head_here = grad_block.shape[0]
-    padded = jnp.pad(grad_block, ((0, 0), (0, 0), (0, seq_len - 1))).reshape(
-        head_here, seq_len * (2 * seq_len - 1)
-    )
-    padded = jnp.pad(padded, ((0, 0), (0, seq_len)))
-    return jnp.sum(padded.reshape(head_here, seq_len, 2 * seq_len), axis=1)
-
-
-def to_items(block, layout):
-    pairs_here, seq_len, groups, per_item, head_size = layout
-    shaped = block.reshape(pairs_here, seq_len, groups, per_item, head_size)
-    return jnp.transpose(shaped, (0, 2, 3, 1, 4)).reshape(
-        pairs_here * groups, per_item, seq_len, head_size
-    )
-
-
-def from_items(block, layout):
-    pairs_here, seq_len, groups, per_item, head_size = layout
-    shaped = block.reshape(pairs_here, groups, per_item, seq_len, head_size)
-    return jnp.transpose(shaped, (0, 3, 1, 2, 4)).reshape(
-        pairs_here * seq_len, groups * per_item * head_size
-    )
-
-
-def item_scores(queries, key_rows, relative, length):
-    seq_len = queries.shape[1]
-    scores = jnp.einsum("gid,gjd->gij", queries, key_rows, preferred_element_type=jnp.float32)
-    scores = scores + toeplitz(relative, seq_len)
-    key_valid = jnp.arange(seq_len, dtype=jnp.int32) < length
-    return jnp.where(key_valid[None, None, :], scores, masked_score)
-
-
-def item_forward(packed):
-    queries, key_rows, value_rows, relative, length = packed
-    scores = item_scores(queries, key_rows, relative, length)
-    row_peak = jnp.max(scores, axis=-1, keepdims=True)
-    exp_scores = jnp.exp(scores - row_peak)
-    row_total = jnp.sum(exp_scores, axis=-1, keepdims=True)
-    soft_probs = (exp_scores / row_total).astype(jnp.bfloat16)
-    attended = jnp.einsum(
-        "gij,gjd->gid", soft_probs, value_rows, preferred_element_type=jnp.float32
-    )
-    return (attended.astype(jnp.bfloat16), (row_peak + jnp.log(row_total))[:, :, 0])
-
-
-def item_backward(packed):
-    queries, key_rows, value_rows, relative, length, log_total, grad_attended = packed
-    seq_len = queries.shape[1]
-    scores = item_scores(queries, key_rows, relative, length)
-    soft_probs = jnp.exp(scores - log_total[:, :, None])
-    grad_probs = jnp.einsum(
-        "gid,gjd->gij", grad_attended, value_rows, preferred_element_type=jnp.float32
-    )
-    centre = jnp.sum(soft_probs * grad_probs, axis=-1, keepdims=True)
-    grad_scores = (soft_probs * (grad_probs - centre)).astype(jnp.bfloat16)
-    grad_queries = jnp.einsum(
-        "gij,gjd->gid", grad_scores, key_rows, preferred_element_type=jnp.float32
-    ).astype(jnp.bfloat16)
-    grad_keys = jnp.einsum(
-        "gij,gid->gjd", grad_scores, queries, preferred_element_type=jnp.float32
-    ).astype(jnp.bfloat16)
-    grad_values = jnp.einsum(
-        "gij,gid->gjd",
-        soft_probs.astype(jnp.bfloat16),
-        grad_attended,
-        preferred_element_type=jnp.float32,
-    ).astype(jnp.bfloat16)
-    return (
-        grad_queries,
-        grad_keys,
-        grad_values,
-        diagonal_sums(grad_scores.astype(jnp.float32), seq_len),
-    )
-
+def dot(a,b): return jnp.dot(a,b,preferred_element_type=jnp.float32)
+def dot_t(a,b): return lax.dot_general(a,b,(((1,),(1,)),((),())),preferred_element_type=jnp.float32)
+def dot_c(a,b): return lax.dot_general(a,b,(((0,),(0,)),((),())),preferred_element_type=jnp.float32)
+
+def fwd_kernel(T, len_ref, q_ref, k_ref, v_ref, rel_ref, o_ref, p_ref, strip):
+    hp=pl.program_id(0)
+    seq=q_ref.shape[0]; nb=seq//T
+    lane=lax.broadcasted_iota(jnp.int32,(1,128),1)
+    kcol=lax.broadcasted_iota(jnp.int32,(1,seq),1)
+    mask=jnp.where(kcol<len_ref[0],0.0,-1e30)
+    k=k_ref[...]; v=v_ref[...]
+    for hh in range(2):
+        mine=(lane>=64) if hh else (lane<64)
+        rel=rel_ref[pl.ds(hh,1),:]
+        W=4*T
+        rolled=pltpu.roll(jnp.broadcast_to(rel,(T,W)),0,axis=1,stride=1,stride_axis=0)
+        strip[:, 2*T:5*T]=rolled[:, :3*T]
+        far_neg=rel[:, 0:1]; far_pos=rel[:, 3*T-1:3*T]
+        strip[:, 0:2*T]=jnp.broadcast_to(far_neg,(T,2*T))
+        strip[:, 5*T:7*T]=jnp.broadcast_to(far_pos,(T,2*T))
+        for I in range(nb):
+            q=jnp.where(mine,q_ref[I*T:(I+1)*T,:],jnp.bfloat16(0))
+            s=dot_t(q,k)+(strip[:, (3-I)*T:(3-I)*T+seq]+mask)
+            m=jnp.max(s,axis=-1,keepdims=True)
+            e=jnp.exp(s-m)
+            tot=jnp.sum(e,axis=-1,keepdims=True)
+            p=(e*(1.0/tot)).astype(jnp.bfloat16)
+            p_ref[hh,I*T:(I+1)*T,:]=p
+            o=dot(p,v)
+            if hh==0:
+                o_ref[I*T:(I+1)*T,:]=o.astype(jnp.bfloat16)
+            else:
+                o_ref[I*T:(I+1)*T,:]=jnp.where(mine,o.astype(jnp.bfloat16),o_ref[I*T:(I+1)*T,:])
+
+def bwd_kernel(T, q_ref, k_ref, v_ref, do_ref, p_ref, dq_ref, dk_ref, dv_ref, db_ref, ds_ref):
+    seq=q_ref.shape[0]; nb=seq//T
+    lane=lax.broadcasted_iota(jnp.int32,(1,128),1)
+    k=k_ref[...]; v=v_ref[...]
+    dks=[];dvs=[]
+    for hh in range(2):
+        mine=(lane>=64) if hh else (lane<64)
+        acc=[None]*5
+        for I in range(nb):
+            sl=slice(I*T,(I+1)*T)
+            do=jnp.where(mine,do_ref[sl,:],jnp.bfloat16(0))
+            dp=dot_t(do,v)
+            p=p_ref[hh,sl,:].astype(jnp.float32)
+            t=p*dp
+            delta=jnp.sum(t,axis=-1,keepdims=True)
+            ds=(t-p*delta).astype(jnp.bfloat16)
+            ds_ref[sl,:]=ds
+            dsf=ds.astype(jnp.float32)
+            for J in range(nb):
+                d=min(2,max(-2,J-I))+2
+                x=dsf[:,J*T:(J+1)*T]
+                acc[d]=x if acc[d] is None else acc[d]+x
+            dq=dot(ds,k)
+            if hh==0: dq_ref[sl,:]=dq.astype(jnp.bfloat16)
+            else: dq_ref[sl,:]=jnp.where(mine,dq.astype(jnp.bfloat16),dq_ref[sl,:])
+        near=jnp.concatenate([acc[1],acc[2],acc[3],jnp.zeros((T,T),jnp.float32)],axis=1)
+        total=shear_sum(near,4*T)
+        far=jnp.concatenate([jnp.zeros((1,2*T),jnp.float32),jnp.sum(acc[4],axis=0,keepdims=True),jnp.sum(acc[0],axis=0,keepdims=True)],axis=1)
+        db_ref[hh:hh+1,:]=total+far
+        dk=dot_c(q_ref[...],ds_ref[...]).T; dv=dot_c(do_ref[...],p_ref[hh]).T
+        dks.append(dk); dvs.append(dv)
+    dk_ref[...]=jnp.where(lane<64,dks[0],dks[1]).astype(jnp.bfloat16)
+    dv_ref[...]=jnp.where(lane<64,dvs[0],dvs[1]).astype(jnp.bfloat16)
+
+def rel_hits(tile):
+    slot = jnp.arange(4 * tile, dtype=jnp.int32)
+    offset = jnp.where(slot < 3 * tile, slot - tile, slot - 5 * tile)
+    bucket_ids = jnp.arange(NB, dtype=jnp.int32)
+    return (bucket_of(offset)[None, :] == bucket_ids[:, None]).astype(jnp.bfloat16)
+
+
+def rel_vec(table, tile):
+    return dot_c(table, rel_hits(tile))
+
+
+def shear_sum(block, width):
+    rows = block.shape[0]
+    while rows > 8:
+        rows //= 2
+        block = block[:rows] + pltpu.roll(block[rows:], width - rows, axis=1)
+    total = block[0:1]
+    for r in range(1, 8):
+        total = total + pltpu.roll(block[r : r + 1], width - r, axis=1)
+    return total
+
+
+def att_fwd(q,k,v,rel,length,T=128):
+    seq,D=q.shape; H=rel.shape[0]
+    blk=pl.BlockSpec((seq,128),lambda h: (0,h))
+    return pl.pallas_call(functools.partial(fwd_kernel,T),grid=(H//2,),
+        in_specs=[pl.BlockSpec(memory_space=pltpu.SMEM),blk,blk,blk,pl.BlockSpec((None,2,4*T),lambda h:(h,0,0))],
+        out_specs=[blk,pl.BlockSpec((2,seq,seq),lambda h:(h,0,0))],
+        out_shape=[jax.ShapeDtypeStruct((seq,D),jnp.bfloat16),jax.ShapeDtypeStruct((H,seq,seq),jnp.bfloat16)],
+        scratch_shapes=[pltpu.VMEM((T,7*T),jnp.float32)],
+        compiler_params=pltpu.CompilerParams(vmem_limit_bytes=40*2**20))(length,q,k,v,rel.reshape(H//2,2,4*T))
+def att_bwd(q,k,v,do,p,T=128):
+    seq,D=q.shape; H=p.shape[0]
+    blk=pl.BlockSpec((seq,128),lambda h: (0,h))
+    o=jax.ShapeDtypeStruct((seq,D),jnp.bfloat16)
+    outs=pl.pallas_call(functools.partial(bwd_kernel,T),grid=(H//2,),
+        in_specs=[blk,blk,blk,blk,pl.BlockSpec((2,seq,seq),lambda h:(h,0,0))],
+        out_specs=[blk,blk,blk,pl.BlockSpec((None,2,4*T),lambda h:(h,0,0))],
+        out_shape=[o,o,o,jax.ShapeDtypeStruct((H//2,2,4*T),jnp.float32)],
+        scratch_shapes=[pltpu.VMEM((seq,seq),jnp.bfloat16)],
+        compiler_params=pltpu.CompilerParams(vmem_limit_bytes=40*2**20))(q,k,v,do,p)
+    return *outs[:3],outs[3].reshape(H,4*T)
 
 def contract_rows(left, right):
     return lax.dot_general(
@@ -156,32 +188,21 @@
         lax.all_gather(bias_table, "fsdp", axis=0, tiled=True),
     )
     head_count = full_table.shape[1]
-    head_size = model_width // head_count
-    per_item = math.gcd(head_count, 4)
-    groups = head_count // per_item
-    item_count = pairs_here * groups
-    layout = (pairs_here, seq_len, groups, per_item, head_size)
-    slot_ids = jnp.arange(2 * seq_len, dtype=jnp.int32)
-    offsets = jnp.where(slot_ids < seq_len, slot_ids, slot_ids - 2 * seq_len)
-    bucket_hits = (bucket_of(offsets)[:, None] == jnp.arange(NB, dtype=jnp.int32)[None, :]).astype(
-        jnp.float32
-    )
-    relative = jnp.dot(bucket_hits, full_table.astype(jnp.float32), precision=highest).T
-    relative_items = relative.reshape(1, groups, per_item, 2 * seq_len).reshape(
-        item_count, per_item, 2 * seq_len
-    )
-    length_items = jnp.repeat(lengths, groups)
+    tile = 128
+    relative = rel_vec(full_table, tile)
     flat_inputs = inputs.reshape(row_count, model_width).astype(jnp.float32)
     normed = rms_norm(flat_inputs, full_gain.astype(jnp.float32)).astype(jnp.bfloat16)
     joined = jnp.concatenate((full_query, full_key, full_value), axis=1)
     projected = jnp.dot(normed, joined, preferred_element_type=jnp.float32).astype(jnp.bfloat16)
-    queries = to_items(projected[:, :model_width], layout)
-    key_rows = to_items(projected[:, model_width : 2 * model_width], layout)
-    value_rows = to_items(projected[:, 2 * model_width :], layout)
-    attended_items, log_totals = lax.map(
-        item_forward, (queries, key_rows, value_rows, relative_items, length_items)
-    )
-    attended = from_items(attended_items, layout)
+    queries = projected[:, :model_width]
+    key_rows = projected[:, model_width : 2 * model_width]
+    value_rows = projected[:, 2 * model_width :]
+    pair_rows = [slice(n * seq_len, (n + 1) * seq_len) for n in range(pairs_here)]
+    forward_parts = [
+        att_fwd(queries[r], key_rows[r], value_rows[r], relative, lengths[n : n + 1], tile)
+        for n, r in enumerate(pair_rows)
+    ]
+    attended = jnp.concatenate([part[0] for part in forward_parts], axis=0)
     middle = flat_inputs + jnp.dot(attended, full_output, preferred_element_type=jnp.float32)
     full_inner, full_outer, full_ffn_gain = (
         lax.all_gather(inner_weight, "fsdp", axis=0, tiled=True),
@@ -224,33 +245,27 @@
     middle_low = grad_middle.astype(jnp.bfloat16)
     grad_attended = contract_cols(middle_low, full_output).astype(jnp.bfloat16)
     grad_output = contract_rows(attended, middle_low)
-    grad_query_items, grad_key_items, grad_value_items, grad_rel_items = lax.map(
-        item_backward,
-        (
-            queries,
-            key_rows,
-            value_rows,
-            relative_items,
-            length_items,
-            log_totals,
-            to_items(grad_attended, layout),
-        ),
-    )
+    backward_parts = [
+        att_bwd(
+            queries[r], key_rows[r], value_rows[r], grad_attended[r], forward_parts[n][1], tile
+        )
+        for n, r in enumerate(pair_rows)
+    ]
     grad_projected = jnp.concatenate(
-        (
-            from_items(grad_query_items, layout),
-            from_items(grad_key_items, layout),
-            from_items(grad_value_items, layout),
-        ),
-        axis=1,
+        [jnp.concatenate(part[:3], axis=1) for part in backward_parts], axis=0
     )
     grad_joined = contract_rows(normed, grad_projected)
     grad_normed = contract_cols(grad_projected, joined)
     attention_pull = jax.vjp(rms_norm, flat_inputs, full_gain.astype(jnp.float32))[1]
     grad_inputs_part, grad_attention_gain = attention_pull(grad_normed)
     input_grad = (grad_middle + grad_inputs_part).reshape(pairs_here, seq_len, model_width)
-    grad_relative = jnp.sum(grad_rel_items.reshape(pairs_here, head_count, 2 * seq_len), axis=0)
-    grad_table = jnp.dot(bucket_hits.T, grad_relative.T, precision=highest)
+    grad_relative = sum(part[3] for part in backward_parts)
+    grad_table = lax.dot_general(
+        rel_hits(tile).astype(jnp.float32),
+        grad_relative,
+        (((1,), (1,)), ((), ())),
+        precision=highest,
+    )
     gradients = (
         grad_joined[:, :model_width],
         grad_joined[:, model_width : 2 * model_width],

time: 1150 us -> 908 us (0.79)
  local copies, waits for them, and re-layouts: 386 us -> 21.2 us
  waiting for transfers between devices: 447 us -> 679 us
  matrix products: 129 us -> 64.1 us
  loops' own time: 39.5 us -> 0 us
  Pallas kernels: 0 us -> 36.3 us
  other arithmetic: 51.8 us -> 15.6 us
    while x54 -> x0, local copies, waits for them, and re-layouts: 163 us -> none
    reshape x10 -> x2, local copies, waits for them, and re-layouts: 113 us -> 0.04 us  [the longest x1 0.02 us: att_fwd(): rel.reshape(H // 2, 2, 4 * T)]
    all_gather x1, waiting for transfers between devices: 0.02 us -> 77.5 us  [local(): lax.all_gather(inner_weight, 'fsdp', axis=0, tiled=True)]
    slice x16 -> x1, local copies, waits for them, and re-layouts: 73.2 us -> 0.15 us  [local(): value_rows = projected[:, 2 * model_width:]]
    all_gather x1, waiting for transfers between devices: 0.01 us -> 71.9 us  [local(): lax.all_gather(outer_weight, 'fsdp', axis=0, tiled=True)]
    reduce_scatter x1, waiting for transfers between devices: 0.01 us -> 67 us  [local(): lax.psum_scatter(gradients[2].astype(jnp.bfloat16), 'fsdp', scatter_dimen...]
    reduce_scatter x1, waiting for transfers between devices: 66.3 us -> 0.01 us  [local(): lax.psum_scatter(gradients[0].astype(jnp.bfloat16), 'fsdp', scatter_dimen...]
    reduce_scatter x1, waiting for transfers between devices: 0.01 us -> 66.2 us  [local(): lax.psum_scatter(gradients[3].astype(jnp.bfloat16), 'fsdp', scatter_dimen...]
  transfers between devices with their start and end apart: 13 -> 13, of which waited for: 8 -> 12; matrix products, arithmetic and copies ran while one was open for 47% -> 7% of each run, Pallas kernels for 0% -> 2%
where the time goes in v1:
time: 908 us; the launch traced here: 907 us
  waiting for transfers between devices  679 us (75%)
  blocking collectives  73.1 us (8%)
  matrix products  64.1 us (7%)
  Pallas kernels  36.3 us (4%)
  local copies, waits for them, and re-layouts  21.2 us (2%)
  between operations  16.8 us (2%)
  other arithmetic  15.6 us (2%)
    reduce_scatter x1, waiting for transfers between devices, local(): lax.psum_scatter(gradients[6].astype(jnp.bfloat16), 'fsdp', scatter_dimen...  99.7 us
    reduce_scatter x1, waiting for transfers between devices, local(): lax.psum_scatter(gradients[7].astype(jnp.bfloat16), 'fsdp', scatter_dimen...  98.7 us
    all_gather x1, waiting for transfers between devices, local(): lax.all_gather(inner_weight, 'fsdp', axis=0, tiled=True)  77.5 us
    all_gather x1, waiting for transfers between devices, local(): lax.all_gather(outer_weight, 'fsdp', axis=0, tiled=True)  71.9 us
    reduce_scatter x1, waiting for transfers between devices, local(): lax.psum_scatter(gradients[2].astype(jnp.bfloat16), 'fsdp', scatter_dimen...  67 us
    reduce_scatter x1, waiting for transfers between devices, local(): lax.psum_scatter(gradients[3].astype(jnp.bfloat16), 'fsdp', scatter_dimen...  66.2 us
    reduce_scatter x1, waiting for transfers between devices, local(): lax.psum_scatter(gradients[1].astype(jnp.bfloat16), 'fsdp', scatter_dimen...  54.5 us
    unnamed x2, blocking collectives  47.1 us
  transfers between devices with their start and end apart: 13, of which 12 were waited for; matrix products, arithmetic and copies ran while one was open for 7% of the time, Pallas kernels for 2%

profile of v1, /device:TPU:1, one launch (start us, length us, event | category | flops | bytes accessed | tf_op | source)
XLA Modules:
  0.0 906.6 jit_solution(108727315203251714)
XLA Ops:
  11.8 1.3 fusion.34
  13.8 0.8 dynamic-update-slice
  14.7 0.8 dynamic-update-slice.1
  15.5 18.8 %all-reduce.6 = (bf16[768]{0:T(1024)(128)(2,1)S(1)}, bf16[768]{0:T(1024)(128)(2,1)S(1)}) all-reduce(bf16[768]{0:T(1024)(128)(2,1)S(1)} %dynamic-update-slice, bf16[768]{0:T(1024)(128)(2,1)S(1)} %dynamic-update-slice.1), channel_id=1, replica_groups=mesh['fsdp'=8,'rep'=4] {'fsdp'}, use_global_device_ids=true, to_apply=%add | all-reduce | flops 1536 | bytes 6144
  34.4 13.2 %all-gather = bf16[8,4,12]{2,1,0:T(4,128)(2,1)S(1)} all-gather(bf16[1,4,12]{2,1,0:T(4,128)(2,1)} %bitcast.46), channel_id=1, replica_groups=mesh['fsdp'=8,'rep'=4] {'fsdp'}, dimensions={0}, use_global_device_ids=true | all-gather | bytes 864 | tf_op jit(solution)/shard_map/all_gather | solution.py:188
  48.1 4.1 all-gather.8.cloned.1.call-done
  52.1 2.4 constant_dynamic-update-slice_fusion.2
  54.6 39.6 %all-gather.10.cloned.1.call-done = bf16[768,768]{1,0:T(8,128)(2,1)} async-done(((bf16[96,768]{1,0:T(8,128)(2,1)}), bf16[768,768]{1,0:T(8,128)(2,1)}) %all-gather.10.cloned.1.call-update) | async-done | bytes 1179664 | tf_op jit(solution)/shard_map/all_gather | solution.py:184
  94.1 2.4 constant_dynamic-update-slice_fusion.1
  96.5 39.6 %all-gather.12.cloned.1.call-done = bf16[768,768]{1,0:T(8,128)(2,1)} async-done(((bf16[96,768]{1,0:T(8,128)(2,1)}), bf16[768,768]{1,0:T(8,128)(2,1)}) %all-gather.12.cloned.1.call-update) | async-done | bytes 1179664 | tf_op jit(solution)/shard_map/all_gather | solution.py:185
  136.2 2.5 constant_dynamic-update-slice_fusion
  138.7 4.1 convolution_convert_fusion.3
  142.9 18.3 %shard_map.203 = (bf16[512,768]{1,0:T(8,128)(2,1)S(1)}, bf16[12,512,512]{2,1,0:T(8,128)(2,1)S(1)}) custom-call(s32[1]{0:T(128)} %copy.35.len_ref, bf16[512,768]{1,0:T(8,128)(2,1)S(1)} %get-tuple-element.46.q_ref, bf16[512,768]{1,0:T(8,128)(2,1)S(1)} %get-tuple-element.45.k_ref, bf16[512,768]{1,0:T(8,128)(2,1)S(1)} %get-tuple-element.44.v_ref, ...), custom_call_target="tpu_custom_call" | custom-call | tf_op jit(solution)/shard_map/pallas_call | solution.py:136
  161.2 2.6 copy-done
  163.8 14.3 %all-gather.14.cloned.1.call-done = bf16[768,768]{1,0:T(8,128)(2,1)} async-done(((bf16[96,768]{1,0:T(8,128)(2,1)}), bf16[768,768]{1,0:T(8,128)(2,1)}) %all-gather.14.cloned.1.call-update) | async-done | bytes 1179664 | tf_op jit(solution)/shard_map/all_gather | solution.py:186
  178.2 3.5 multiply_reduce_fusion.2
  181.6 77.5 %all-gather.16.cloned.1.call-done = bf16[768,3072]{1,0:T(8,128)(2,1)} async-done(((bf16[96,3072]{1,0:T(8,128)(2,1)}), bf16[768,3072]{1,0:T(8,128)(2,1)}) %all-gather.16.cloned.1.call-update) | async-done | bytes 4718608 | tf_op jit(solution)/shard_map/all_gather | solution.py:208
  259.1 8.2 fusion.31
  267.3 71.9 %all-gather.18.cloned.1.call-done = bf16[3072,768]{1,0:T(8,128)(2,1)} async-done(((bf16[384,768]{1,0:T(8,128)(2,1)}), bf16[3072,768]{1,0:T(8,128)(2,1)}) %all-gather.18.cloned.1.call-update) | async-done | bytes 4718608 | tf_op jit(solution)/shard_map/all_gather | solution.py:209
  339.2 9.8 %fusion.3 = bf16[512,3072]{1,0:T(8,128)(2,1)S(1)} fusion(f32[512,3072]{1,0:T(8,128)} %fusion.31, bf16[3072,768]{1,0:T(8,128)(2,1)} %all-gather.18.cloned.1.call-done, bf16[1,512,768]{2,1,0:T(8,128)(2,1)} %param.14, f32[512]{0:T(512)S(1)} %fusion.28), kind=kOutput, calls=%fused_computation.7 | convolution fusion | flops 2454847488 | bytes 14944256 | tf_op jit(solution)/shard_map/dot_general | solution.py:161
  349.1 2.8 multiply_reduce_fusion
  353.3 0.8 convolution_convert_fusion.5.do_ref
  354.4 2.8 copy-done.1
  357.2 18.0 %shard_map.204 = (bf16[512,768]{1,0:T(8,128)(2,1)S(1)}, bf16[512,768]{1,0:T(8,128)(2,1)S(1)}, bf16[512,768]{1,0:T(8,128)(2,1)S(1)}, f32[6,2,512]{2,1,0:T(2,128)S(1)}) custom-call(bf16[512,768]{1,0:T(8,128)(2,1)S(1)} %get-tuple-element.46.q_ref, bf16[512,768]{1,0:T(8,128)(2,1)S(1)} %get-tuple-element.45.k_ref, bf16[512,768]{1,0:T(8,128)(2,1)S(1)} %get-tuple-element.44.v_ref, ...), custom_call_target="tpu_custom_call" | custom-call | tf_op jit(solution)/shard_map/pallas_call | solution.py:146
  375.4 0.9 copy-done.8
  376.4 2.1 convolution_convert_fusion.2
  378.5 1.9 fusion.32
  381.9 1.9 convolution_convert_fusion.4
  383.9 7.3 convolution_convert_fusion.1
  391.3 1.1 copy-done.10
  392.4 8.4 convolution_convert_fusion
  402.5 6.1 fusion.9
  408.6 28.3 %all-reduce.5 = (bf16[768]{0:T(1024)(128)(2,1)S(1)}, bf16[32,12]{1,0:T(8,128)(2,1)S(1)}, bf16[768]{0:T(1024)(128)(2,1)S(1)}) all-reduce(bf16[768]{0:T(1024)(128)(2,1)S(1)} %get-tuple-element.25, bf16[32,12]{1,0:T(8,128)(2,1)S(1)} %convolution_convert_fusion.6, ...), channel_id=6, replica_groups=mesh['fsdp'=8,'rep'=4] {'fsdp'}, use_global_device_ids=true, to_apply=%region_13.14.clone | all-reduce | flops 1920 | bytes 7680
  437.0 12.8 %all-reduce.7 = (bf16[96]{0:T(256)(128)(2,1)S(1)}, bf16[4,12]{1,0:T(4,128)(2,1)S(1)}, bf16[96]{0:T(256)(128)(2,1)S(1)}) all-reduce(bf16[96]{0:T(256)(128)(2,1)S(1)} %dynamic-slice.3, bf16[4,12]{1,0:T(4,128)(2,1)S(1)} %constant_dynamic-slice_fusion, bf16[96]{0:T(256)(128)(2,1)S(1)} %dynamic-slice.7), channel_id=1, replica_groups=mesh['fsdp'=8,'rep'=4] {'rep'}, use_global_device_ids=true, to_apply=%region_14.15 | all-reduce | flops 240 | bytes 960 | tf_op jit(solution)/shard_map/psum | solution.py:316
  451.4 3.3 fusion.12
  454.7 54.5 %reduce-scatter.9.cloned.1.call-done = bf16[96,768]{1,0:T(8,128)(2,1)} async-done(((bf16[768,768]{1,0:T(8,128)(2,1)}), bf16[96,768]{1,0:T(8,128)(2,1)}) %reduce-scatter.9.cloned.1.call-update) | async-done | bytes 147472 | tf_op jit(solution)/shard_map/reduce_scatter | solution.py:295
  509.3 67.0 %reduce-scatter.11.cloned.1.call-done = bf16[96,768]{1,0:T(8,128)(2,1)} async-done(((bf16[768,768]{1,0:T(8,128)(2,1)}), bf16[96,768]{1,0:T(8,128)(2,1)}) %reduce-scatter.11.cloned.1.call-update) | async-done | bytes 147472 | tf_op jit(solution)/shard_map/reduce_scatter | solution.py:298
  576.3 66.2 %reduce-scatter.13.cloned.1.call-done = bf16[96,768]{1,0:T(8,128)(2,1)} async-done(((bf16[768,768]{1,0:T(8,128)(2,1)}), bf16[96,768]{1,0:T(8,128)(2,1)}) %reduce-scatter.13.cloned.1.call-update) | async-done | bytes 147472 | tf_op jit(solution)/shard_map/reduce_scatter | solution.py:301
  642.5 99.7 %reduce-scatter.15.cloned.1.call-done = bf16[96,3072]{1,0:T(8,128)(2,1)} async-done(((bf16[768,3072]{1,0:T(8,128)(2,1)}), bf16[96,3072]{1,0:T(8,128)(2,1)}) %reduce-scatter.15.cloned.1.call-update) | async-done | bytes 589840 | tf_op jit(solution)/shard_map/reduce_scatter | solution.py:281
  742.2 98.7 %reduce-scatter.17.cloned.1.call-done = bf16[384,768]{1,0:T(8,128)(2,1)} async-done(((bf16[3072,768]{1,0:T(8,128)(2,1)}), bf16[384,768]{1,0:T(8,128)(2,1)}) %reduce-scatter.17.cloned.1.call-update) | async-done | bytes 589840 | tf_op jit(solution)/shard_map/reduce_scatter | solution.py:284
  840.9 8.8 fusion.15
  849.7 40.5 %all-reduce.11.cloned.1.call-done = (bf16[96,768]{1,0:T(8,128)(2,1)}, bf16[96,768]{1,0:T(8,128)(2,1)}, bf16[96,768]{1,0:T(8,128)(2,1)}, bf16[96,768]{1,0:T(8,128...) async-done(((bf16[96,768]{1,0:T(8,128)(2,1)}, bf16[96,768]{1,0:T(8,128)(2,1)}, bf16[96,768]{1,0:T(8,128)(2,1)}, bf16[96,768]{1,0:T(8,128)(2,1)}, ...) | async-done | bytes 1769488 | tf_op jit(solution)/shard_map/psum | solution.py:312
  890.2 1.7 convert_element_type.214
  891.9 1.6 convert_element_type.215
  893.5 1.6 convert_element_type.216
  895.2 1.6 convert_element_type.218
  896.8 2.2 convert_element_type.224
  899.0 1.1 convert_element_type.226
  (79 shorter events, 10.2 us)
Async XLA Ops:
  7.2 40.6 %copy-start.7 = (bf16[1,512,768]{2,1,0:T(8,128)(2,1)S(1)}, bf16[1,512,768]{2,1,0:T(8,128)(2,1)}, u32[]{:S(2)}) copy-start(bf16[1,512,768]{2,1,0:T(8,128)(2,1)} %param.12) | copy-start | bytes 2359300
  7.2 44.9 %all-gather.8.cloned.1.call-start = ((), (), s32[]{:S(2)}) async-start(), calls=%async_computation.6 | async-start | bytes 1327104 | tf_op jit(solution)/shard_map/all_gather | solution.py:183
  7.9 86.2 %all-gather.10.cloned.1.call-start = ((), (), s32[]{:S(2)}) async-start(), calls=%async_computation.7 | async-start | bytes 1327104 | tf_op jit(solution)/shard_map/all_gather | solution.py:184
  8.7 127.5 %all-gather.12.cloned.1.call-start = ((), (), s32[]{:S(2)}) async-start(), calls=%async_computation.8 | async-start | bytes 1327104 | tf_op jit(solution)/shard_map/all_gather | solution.py:185
  9.4 168.8 %all-gather.14.cloned.1.call-start = ((), (), s32[]{:S(2)}) async-start(), calls=%async_computation.9 | async-start | bytes 1327104 | tf_op jit(solution)/shard_map/all_gather | solution.py:186
  10.0 249.2 %all-gather.16.cloned.1.call-start = ((), (), s32[]{:S(2)}) async-start(), calls=%async_computation.10 | async-start | bytes 5308416 | tf_op jit(solution)/shard_map/all_gather | solution.py:208
  10.6 328.7 %all-gather.18.cloned.1.call-start = ((), (), s32[]{:S(2)}) async-start(), calls=%async_computation.11 | async-start | bytes 5308416 | tf_op jit(solution)/shard_map/all_gather | solution.py:209
  11.1 443.6 %reduce-scatter.7.cloned.1.call-start = ((), (), s32[]{:S(2)}) async-start(), calls=%async_computation.12 | async-start | bytes 1327104 | tf_op jit(solution)/shard_map/reduce_scatter | solution.py:292
  161.2 2.6 copy-start
  339.2 9.8 %copy-start.4 = (f32[512,768]{1,0:T(8,128)S(1)}, f32[512,768]{1,0:T(8,128)}, u32[]{:S(2)}) copy-start(f32[512,768]{1,0:T(8,128)} %get-tuple-element.50) | copy-start | bytes 4718596
  339.2 9.9 %copy-start.6 = (bf16[768,3072]{1,0:T(8,128)(2,1)S(1)}, bf16[768,3072]{1,0:T(8,128)(2,1)}, u32[]{:S(2)}) copy-start(bf16[768,3072]{1,0:T(8,128)(2,1)} %all-gather.16.cloned.1.call-done) | copy-start | bytes 14155780
  349.1 2.9 copy-start.14
  349.1 2.9 copy-start.9
  352.0 1.3 copy-start.13
  353.3 1.1 copy-start.2
  354.4 2.8 copy-start.1
  375.2 1.1 copy-start.8
  376.4 2.1 copy-start.12
  380.4 1.6 copy-start.3
  380.4 128.9 %reduce-scatter.9.cloned.1.call-start = ((), (), s32[]{:S(2)}) async-start(), calls=%async_computation.13 | async-start | bytes 1327104 | tf_op jit(solution)/shard_map/reduce_scatter | solution.py:295
  381.2 195.1 %reduce-scatter.11.cloned.1.call-start = ((), (), s32[]{:S(2)}) async-start(), calls=%async_computation.14 | async-start | bytes 1327104 | tf_op jit(solution)/shard_map/reduce_scatter | solution.py:298
  381.9 260.6 %reduce-scatter.13.cloned.1.call-start = ((), (), s32[]{:S(2)}) async-start(), calls=%async_computation.15 | async-start | bytes 1327104 | tf_op jit(solution)/shard_map/reduce_scatter | solution.py:301
  383.9 358.3 %reduce-scatter.15.cloned.1.call-start = ((), (), s32[]{:S(2)}) async-start(), calls=%async_computation.16 | async-start | bytes 5308416 | tf_op jit(solution)/shard_map/reduce_scatter | solution.py:281
  391.2 1.1 copy-start.10
  391.3 449.6 %reduce-scatter.17.cloned.1.call-start = ((), (), s32[]{:S(2)}) async-start(), calls=%async_computation.17 | async-start | bytes 5308416 | tf_op jit(solution)/shard_map/reduce_scatter | solution.py:284
  400.8 489.4 %all-reduce.11.cloned.1.call-start = ((), (), s32[]{:S(2)}) async-start(), calls=%async_computation.18 | async-start | bytes 3538944 | tf_op jit(solution)/shard_map/psum | solution.py:312
  451.4 389.5 %copy-start.5 = (f32[512,768]{1,0:T(8,128)S(1)}, f32[512,768]{1,0:T(8,128)}, u32[]{:S(2)}) copy-start(f32[512,768]{1,0:T(8,128)} %get-tuple-element.50) | copy-start | bytes 4718596
  890.2 8.8 copy-start.11
Sparse Core Ops, SparseCore 0:
  10.2 41.8 all-gather.7
  54.3 39.7 all-gather.9
  96.3 39.8 all-gather.11
  138.2 39.9 all-gather.13
  180.2 78.9 all-gather.15
  261.2 78.0 all-gather.17
  380.5 61.7 reduce-scatter.6
  446.3 62.9 reduce-scatter.8
  513.2 62.9 reduce-scatter.10
  579.5 62.9 reduce-scatter.12
  646.2 95.9 reduce-scatter.14
  745.7 95.1 reduce-scatter.16
  843.7 46.4 all-reduce.10

commit v2 on v1

--- a/solution.py
+++ b/solution.py
@@ -163,30 +163,461 @@
     )
 
 
-def local(
-    inputs,
-    lengths,
-    cotangent,
-    query_weight,
-    key_weight,
-    value_weight,
-    output_weight,
-    attention_gain,
-    bias_table,
-    inner_weight,
-    outer_weight,
-    feedforward_gain,
+MESH = pl.DeviceIdType.MESH
+
+
+def coords():
+    shard = lax.axis_index("fsdp")
+    copy = lax.axis_index("rep")
+    return shard // 2, shard % 2, copy // 2, copy % 2
+
+
+def greet():
+    barrier = pltpu.get_barrier_semaphore()
+    shard = lax.axis_index("fsdp")
+    copy = lax.axis_index("rep")
+    for k in range(1, 8):
+        peer = (lax.rem(shard + k, 8), copy)
+        pl.semaphore_signal(barrier, inc=1, device_id=peer, device_id_type=MESH)
+    for k in range(1, 4):
+        peer = (shard, lax.rem(copy + k, 4))
+        pl.semaphore_signal(barrier, inc=1, device_id=peer, device_id_type=MESH)
+    pl.semaphore_wait(barrier, 10)
+
+
+def schedule(stages, count):
+    last = max(lag for _, lag in stages)
+
+    def step(t, carry):
+        for stage, lag in stages:
+            g = t - lag
+            pl.when((g >= 0) & (g < count))(functools.partial(stage, g))
+        return carry
+
+    lax.fori_loop(0, count + last, step, 0)
+
+
+class Links:
+    def __init__(self, rows, send_sems, recv_sems):
+        self.send_sems, self.recv_sems = send_sems, recv_sems
+        self.z, self.x, self.y, self.c = coords()
+        half = rows // 2
+        part = half // 3
+        at = lambda start, size: pl.ds(pl.multiple_of(start, part), size)
+        first = half * self.c
+        other = half * (1 - self.c)
+        self.half, self.other_half = at(first, half), at(other, half)
+        self.plane = at(first + part * self.y, 2 * part)
+        self.shared = at(first + part, part)
+        self.own_third = at(first + 2 * part * self.y, part)
+        self.other_third = at(first + 2 * part * (1 - self.y), part)
+        self.shared_in = at(part * self.y, part)
+        self.third_in = at(part * (1 - self.y), part)
+
+    def copy(self, src, dst, g, slot, device):
+        return pltpu.make_async_remote_copy(
+            src_ref=src,
+            dst_ref=dst,
+            send_sem=self.send_sems.at[g, slot],
+            recv_sem=self.recv_sems.at[g, slot],
+            device_id=device,
+            device_id_type=MESH,
+        )
+
+    def to_x(self):
+        return (self.z * 2 + 1 - self.x, self.y * 2 + self.c)
+
+    def to_y(self):
+        return (self.z * 2 + self.x, (1 - self.y) * 2 + self.c)
+
+    def to_core(self):
+        return (self.z * 2 + self.x, self.y * 2 + 1 - self.c)
+
+    def to_z(self, k):
+        return (lax.rem(self.z + k, 4) * 2 + self.x, self.y * 2 + self.c)
+
+    def z_before(self, k):
+        return lax.rem(self.z + 4 - k, 4)
+
+
+class Gather(Links):
+    slots = 15
+
+    def __init__(self, own, full, send_sems, recv_sems):
+        super().__init__(own.shape[1], send_sems, recv_sems)
+        self.own, self.full = own, full
+
+    def block(self, g, k, rows):
+        return self.full.at[self.z_before(k), self.x, g, rows]
+
+    def column(self, g, rows):
+        return self.full.at[:, 1 - self.x, g, rows]
+
+    def z_copy(self, g, k):
+        return self.copy(
+            self.own.at[g, self.plane],
+            self.full.at[self.z, self.x, g, self.plane],
+            g,
+            k - 1,
+            self.to_z(k),
+        )
+
+    def x_copy(self, g, k):
+        there = self.block(g, k, self.plane)
+        here = self.own.at[g, self.plane] if k == 0 else there
+        return self.copy(here, there, g, 3 + k, self.to_x())
+
+    def y_copy(self, g, k):
+        rows = self.own_third
+        part = self.block(g, k, rows) if k < 4 else self.column(g, rows)
+        return self.copy(part, part, g, 6 + k, self.to_y())
+
+    def core_copy(self, g, k):
+        part = self.block(g, k, self.half) if k < 4 else self.column(g, self.half)
+        return self.copy(part, part, g, 10 + k, self.to_core())
+
+    def arrived(self, part, g, slot, device):
+        self.copy(part, part, g, slot, device).wait_recv()
+
+    def start(self, g):
+        self.x_copy(g, 0).start()
+        for k in (1, 2, 3):
+            self.z_copy(g, k).start()
+
+    def after_z(self, g):
+        for k in (1, 2, 3):
+            self.arrived(self.block(g, k, self.plane), g, k - 1, self.to_z(k))
+            self.x_copy(g, k).start()
+            self.y_copy(g, k).start()
+
+    def after_x(self, g):
+        for k in range(4):
+            part = self.full.at[self.z_before(k), 1 - self.x, g, self.plane]
+            self.arrived(part, g, 3 + k, self.to_x())
+        self.y_copy(g, 4).start()
+
+    def after_y(self, g):
+        for k in (1, 2, 3):
+            self.arrived(self.block(g, k, self.other_third), g, 6 + k, self.to_y())
+            self.core_copy(g, k).start()
+        self.arrived(self.column(g, self.other_third), g, 10, self.to_y())
+        self.core_copy(g, 4).start()
+
+    def after_core(self, g):
+        for k in (1, 2, 3):
+            self.arrived(self.block(g, k, self.other_half), g, 10 + k, self.to_core())
+        self.arrived(self.column(g, self.other_half), g, 14, self.to_core())
+
+    def drain(self, g):
+        self.x_copy(g, 0).wait_send()
+        for k in (1, 2, 3):
+            self.z_copy(g, k).wait_send()
+            self.x_copy(g, k).wait_send()
+            self.y_copy(g, k).wait_send()
+            self.core_copy(g, k).wait_send()
+        self.y_copy(g, 4).wait_send()
+        self.core_copy(g, 4).wait_send()
+
+
+class Scatter(Links):
+    slots = 8
+
+    def __init__(self, full, own, from_core, from_y, from_x, from_z, send_sems, recv_sems):
+        super().__init__(own.shape[1], send_sems, recv_sems)
+        self.full, self.own = full, own
+        self.from_core, self.from_y, self.from_x, self.from_z = from_core, from_y, from_x, from_z
+
+    def core_copy(self, g):
+        part = self.full.at[:, :, g, self.other_half]
+        return self.copy(part, self.from_core.at[g], g, 0, self.to_core())
+
+    def y_copy(self, g):
+        part = self.full.at[:, :, g, self.other_third]
+        return self.copy(part, self.from_y.at[g], g, 1, self.to_y())
+
+    def x_copy(self, g):
+        part = self.full.at[:, 1 - self.x, g, self.plane]
+        return self.copy(part, self.from_x.at[g], g, 2, self.to_x())
+
+    def z_copy(self, g, k):
+        part = self.full.at[lax.rem(self.z + k, 4), self.x, g, self.plane]
+        return self.copy(part, self.from_z.at[g, k - 1], g, 2 + k, self.to_z(k))
+
+    def back_y_copy(self, g):
+        part = self.own.at[g, self.plane]
+        return self.copy(part, self.from_z.at[g, 3], g, 6, self.to_y())
+
+    def back_core_copy(self, g):
+        part = self.own.at[g, self.half]
+        return self.copy(part, part, g, 7, self.to_core())
+
+    def start(self, g):
+        self.core_copy(g).start()
+
+    def after_core(self, g):
+        self.core_copy(g).wait_recv()
+        for a in range(4):
+            for b in range(2):
+                self.full[a, b, g, self.half] += self.from_core[g, a, b]
+        self.y_copy(g).start()
+
+    def after_y(self, g):
+        self.y_copy(g).wait_recv()
+        for a in range(4):
+            for b in range(2):
+                self.full[a, b, g, self.own_third] += self.from_y[g, a, b]
+        self.x_copy(g).start()
+
+    def after_x(self, g):
+        self.x_copy(g).wait_recv()
+        for a in range(4):
+            self.full[a, self.x, g, self.plane] += self.from_x[g, a]
+        for k in (1, 2, 3):
+            self.z_copy(g, k).start()
+
+    def after_z(self, g):
+        total = self.full[self.z, self.x, g, self.plane].astype(jnp.float32)
+        for k in (1, 2, 3):
+            self.z_copy(g, k).wait_recv()
+            total = total + self.from_z[g, k - 1].astype(jnp.float32)
+        self.own[g, self.plane] = total.astype(jnp.bfloat16)
+        self.back_y_copy(g).start()
+
+    def after_back_y(self, g):
+        self.back_y_copy(g).wait_recv()
+        self.back_y_copy(g).wait_send()
+        got = self.from_z.at[g, 3]
+        self.own[g, self.shared] += got[self.shared_in]
+        self.own[g, self.other_third] = got[self.third_in]
+        self.back_core_copy(g).start()
+
+    def after_back_core(self, g):
+        part = self.own.at[g, self.other_half]
+        self.copy(part, part, g, 7, self.to_core()).wait_recv()
+
+    def drain(self, g):
+        self.core_copy(g).wait_send()
+        self.y_copy(g).wait_send()
+        self.x_copy(g).wait_send()
+        for k in (1, 2, 3):
+            self.z_copy(g, k).wait_send()
+        self.back_core_copy(g).wait_send()
+
+
+def small_gather(small, all_small, send_sems, recv_sems):
+    shard = lax.axis_index("fsdp")
+    copy = lax.axis_index("rep")
+    return [
+        pltpu.make_async_remote_copy(
+            src_ref=small,
+            dst_ref=all_small.at[shard],
+            send_sem=send_sems.at[k - 1],
+            recv_sem=recv_sems.at[k - 1],
+            device_id=(lax.rem(shard + k, 8), copy),
+            device_id_type=MESH,
+        )
+        for k in range(1, 8)
+    ]
+
+
+def gather_kernel(lags, own, small, full, all_small, sends, recvs, small_sends, small_recvs, sem):
+    shard = lax.axis_index("fsdp")
+    greet()
+    smalls = small_gather(small, all_small, small_sends, small_recvs)
+    for copy in smalls:
+        copy.start()
+    moves = Gather(own, full, sends, recvs)
+    keep = pltpu.make_async_copy(own, full.at[moves.z, moves.x], sem.at[0])
+    keep_small = pltpu.make_async_copy(small, all_small.at[shard], sem.at[1])
+    keep.start()
+    keep_small.start()
+    units = own.shape[0]
+    stages = (moves.after_y, moves.after_x, moves.after_z, moves.start, moves.after_core)
+    schedule(list(zip(stages, lags)), units)
+
+    def drain(g, carry):
+        moves.drain(g)
+        return carry
+
+    lax.fori_loop(0, units, drain, 0)
+    for copy in smalls:
+        copy.wait()
+    keep.wait()
+    keep_small.wait()
+
+
+def gather_call(own, small):
+    units = own.shape[0]
+    anywhere = pl.BlockSpec(memory_space=pl.ANY)
+    sems = pltpu.SemaphoreType.DMA
+    return pl.pallas_call(
+        functools.partial(gather_kernel, (6, 4, 2, 0, 7)),
+        out_shape=(
+            jax.ShapeDtypeStruct((4, 2) + own.shape, own.dtype),
+            jax.ShapeDtypeStruct((8,) + small.shape, small.dtype),
+        ),
+        in_specs=[anywhere, anywhere],
+        out_specs=[anywhere, anywhere],
+        scratch_shapes=[
+            sems((units, Gather.slots)),
+            sems((units, Gather.slots)),
+            sems((7,)),
+            sems((7,)),
+            sems((2,)),
+        ],
+        compiler_params=pltpu.CompilerParams(collective_id=0, has_side_effects=True),
+    )(own, small)
+
+
+def scatter_kernel(
+    lags, full_in, small, own_out, small_out, full, own, from_core, from_y, from_x, from_z,
+    small_in, small_rep, sends, recvs, load_sems, store_sems, small_sends, small_recvs, rep_sends,
+    rep_recvs,
 ):
+    units = own.shape[0]
+    shard = lax.axis_index("fsdp")
+    copy_id = lax.axis_index("rep")
+
+    def load(g):
+        return pltpu.make_async_copy(full_in.at[:, :, g], full.at[:, :, g], load_sems.at[g])
+
+    def store(g):
+        return pltpu.make_async_copy(own.at[g], own_out.at[g], store_sems.at[g])
+
+    def begin(g, carry):
+        load(g).start()
+        return carry
+
+    lax.fori_loop(0, units, begin, 0)
+    greet()
+    smalls = [
+        pltpu.make_async_remote_copy(
+            src_ref=small.at[lax.rem(shard + k, 8)],
+            dst_ref=small_in.at[k - 1],
+            send_sem=small_sends.at[k - 1],
+            recv_sem=small_recvs.at[k - 1],
+            device_id=(lax.rem(shard + k, 8), copy_id),
+            device_id_type=MESH,
+        )
+        for k in range(1, 8)
+    ]
+    for copy in smalls:
+        copy.start()
+    moves = Scatter(full, own, from_core, from_y, from_x, from_z, sends, recvs)
+
+    def first(g):
+        load(g).wait()
+        moves.start(g)
+
+    def last(g):
+        moves.after_back_core(g)
+        store(g).start()
+
+    stages = (
+        last, moves.after_back_y, moves.after_z, moves.after_x, moves.after_y, moves.after_core,
+        first,
+    )
+    schedule(list(zip(stages, lags)), units)
+    total = small[shard]
+    for k, copy in enumerate(smalls):
+        copy.wait_recv()
+        total = total + small_in[k]
+    small_rep[copy_id] = total
+    reps = [
+        pltpu.make_async_remote_copy(
+            src_ref=small_rep.at[copy_id],
+            dst_ref=small_rep.at[copy_id],
+            send_sem=rep_sends.at[k - 1],
+            recv_sem=rep_recvs.at[k - 1],
+            device_id=(shard, lax.rem(copy_id + k, 4)),
+            device_id_type=MESH,
+        )
+        for k in range(1, 4)
+    ]
+    for copy in reps:
+        copy.start()
+    for k in range(1, 4):
+        there = small_rep.at[lax.rem(copy_id + 4 - k, 4)]
+        pltpu.make_async_remote_copy(
+            src_ref=there,
+            dst_ref=there,
+            send_sem=rep_sends.at[k - 1],
+            recv_sem=rep_recvs.at[k - 1],
+            device_id=(shard, lax.rem(copy_id + k, 4)),
+            device_id_type=MESH,
+        ).wait_recv()
+    small_out[...] = (small_rep[0] + small_rep[1]) + (small_rep[2] + small_rep[3])
+
+    def drain(g, carry):
+        moves.drain(g)
+        store(g).wait()
+        return carry
+
+    lax.fori_loop(0, units, drain, 0)
+    for copy in smalls + reps:
+        copy.wait_send()
+
+
+def scatter_call(full, small):
+    units, rows, width = full.shape[2:]
+    half = rows // 2
+    part = half // 3
+    anywhere = pl.BlockSpec(memory_space=pl.ANY)
+    within = pl.BlockSpec(memory_space=pltpu.VMEM)
+    sems = pltpu.SemaphoreType.DMA
+    kind = full.dtype
+    return pl.pallas_call(
+        functools.partial(scatter_kernel, (9, 8, 7, 5, 3, 1, 0)),
+        out_shape=(
+            jax.ShapeDtypeStruct((units, rows, width), kind),
+            jax.ShapeDtypeStruct(small.shape[1:], small.dtype),
+        ),
+        in_specs=[anywhere, within],
+        out_specs=[anywhere, within],
+        scratch_shapes=[
+            pltpu.VMEM(full.shape, kind),
+            pltpu.VMEM((units, rows, width), kind),
+            pltpu.VMEM((units, 4, 2, half, width), kind),
+            pltpu.VMEM((units, 4, 2, part, width), kind),
+            pltpu.VMEM((units, 4, 2 * part, width), kind),
+            pltpu.VMEM((units, 4, 2 * part, width), kind),
+            pltpu.VMEM((7,) + small.shape[1:], small.dtype),
+            pltpu.VMEM((4,) + small.shape[1:], small.dtype),
+            sems((units, Scatter.slots)),
+            sems((units, Scatter.slots)),
+            sems((units,)),
+            sems((units,)),
+            sems((7,)),
+            sems((7,)),
+            sems((3,)),
+            sems((3,)),
+        ],
+        compiler_params=pltpu.CompilerParams(
+            collective_id=1, has_side_effects=True, vmem_limit_bytes=60 * 2**20
+        ),
+    )(full, small)
+
+
+def pack_small(gain_a, gain_f, table, kind, rows):
+    def put(part, rows_here):
+        part = part.reshape(part.shape[:-1] + (rows_here, -1)) if rows_here == 1 else part
+        lead = [(0, 0)] * (part.ndim - 1)
+        return jnp.pad(part, lead + [(0, 128 - part.shape[-1])])
+
+    block = jnp.concatenate(
+        (put(gain_a, 1), put(gain_f, 1), put(table, table.shape[-2])), axis=-2
+    ).astype(kind)
+    lead = [(0, 0)] * (block.ndim - 2)
+    return jnp.pad(block, lead + [(0, rows - block.shape[-2]), (0, 0)])
+
+
+def compute(inputs, lengths, cotangent, weights):
+    (
+        full_query, full_key, full_value, full_output, full_gain, full_table, full_inner,
+        full_outer, full_ffn_gain,
+    ) = weights
     pairs_here, seq_len, model_width = inputs.shape
     row_count = pairs_here * seq_len
-    full_query, full_key, full_value, full_output, full_gain, full_table = (
-        lax.all_gather(query_weight, "fsdp", axis=0, tiled=True),
-        lax.all_gather(key_weight, "fsdp", axis=0, tiled=True),
-        lax.all_gather(value_weight, "fsdp", axis=0, tiled=True),
-        lax.all_gather(output_weight, "fsdp", axis=0, tiled=True),
-        lax.all_gather(attention_gain, "fsdp", axis=0, tiled=True),
-        lax.all_gather(bias_table, "fsdp", axis=0, tiled=True),
-    )
     head_count = full_table.shape[1]
     tile = 128
     relative = rel_vec(full_table, tile)
@@ -204,11 +635,6 @@
     ]
     attended = jnp.concatenate([part[0] for part in forward_parts], axis=0)
     middle = flat_inputs + jnp.dot(attended, full_output, preferred_element_type=jnp.float32)
-    full_inner, full_outer, full_ffn_gain = (
-        lax.all_gather(inner_weight, "fsdp", axis=0, tiled=True),
-        lax.all_gather(outer_weight, "fsdp", axis=0, tiled=True),
-        lax.all_gather(feedforward_gain, "fsdp", axis=0, tiled=True),
-    )
     normed_ffn = rms_norm(middle, full_ffn_gain.astype(jnp.float32)).astype(jnp.bfloat16)
     raised = jnp.dot(normed_ffn, full_inner, preferred_element_type=jnp.float32)
     active = gelu(raised).astype(jnp.bfloat16)
@@ -219,11 +645,6 @@
     seed_rows = (cotangent.astype(jnp.float32) * row_live[:, :, None]).reshape(
         row_count, model_width
     )
-    full_inner, full_outer, full_ffn_gain = (
-        lax.all_gather(inner_weight, "fsdp", axis=0, tiled=True),
-        lax.all_gather(outer_weight, "fsdp", axis=0, tiled=True),
-        lax.all_gather(feedforward_gain, "fsdp", axis=0, tiled=True),
-    )
     seed_low = seed_rows.astype(jnp.bfloat16)
     grad_active = contract_cols(seed_low, full_outer)
     grad_outer = contract_rows(active, seed_low)
@@ -233,14 +654,6 @@
     ffn_pull = jax.vjp(rms_norm, middle, full_ffn_gain.astype(jnp.float32))[1]
     grad_middle_part, grad_ffn_gain = ffn_pull(grad_normed_ffn)
     grad_middle = seed_rows + grad_middle_part
-    full_query, full_key, full_value, full_output, full_gain, full_table = (
-        lax.all_gather(query_weight, "fsdp", axis=0, tiled=True),
-        lax.all_gather(key_weight, "fsdp", axis=0, tiled=True),
-        lax.all_gather(value_weight, "fsdp", axis=0, tiled=True),
-        lax.all_gather(output_weight, "fsdp", axis=0, tiled=True),
-        lax.all_gather(attention_gain, "fsdp", axis=0, tiled=True),
-        lax.all_gather(bias_table, "fsdp", axis=0, tiled=True),
-    )
     joined = jnp.concatenate((full_query, full_key, full_value), axis=1)
     middle_low = grad_middle.astype(jnp.bfloat16)
     grad_attended = contract_cols(middle_low, full_output).astype(jnp.bfloat16)
@@ -266,7 +679,7 @@
         (((1,), (1,)), ((), ())),
         precision=highest,
     )
-    gradients = (
+    return block_output, input_grad, (
         grad_joined[:, :model_width],
         grad_joined[:, model_width : 2 * model_width],
         grad_joined[:, 2 * model_width :],
@@ -277,61 +690,109 @@
         grad_outer,
         grad_ffn_gain,
     )
-    shard_inner, shard_outer, shard_ffn_gain = (
-        lax.psum_scatter(
-            gradients[6].astype(jnp.bfloat16), "fsdp", scatter_dimension=0, tiled=True
-        ).astype(jnp.float32),
-        lax.psum_scatter(
-            gradients[7].astype(jnp.bfloat16), "fsdp", scatter_dimension=0, tiled=True
-        ).astype(jnp.float32),
-        lax.psum_scatter(
-            gradients[8].astype(jnp.bfloat16), "fsdp", scatter_dimension=0, tiled=True
-        ).astype(jnp.float32),
-    )
-    shard_query, shard_key, shard_value, shard_output, shard_attention_gain, shard_table = (
-        lax.psum_scatter(
-            gradients[0].astype(jnp.bfloat16), "fsdp", scatter_dimension=0, tiled=True
-        ).astype(jnp.float32),
-        lax.psum_scatter(
-            gradients[1].astype(jnp.bfloat16), "fsdp", scatter_dimension=0, tiled=True
-        ).astype(jnp.float32),
-        lax.psum_scatter(
-            gradients[2].astype(jnp.bfloat16), "fsdp", scatter_dimension=0, tiled=True
-        ).astype(jnp.float32),
-        lax.psum_scatter(
-            gradients[3].astype(jnp.bfloat16), "fsdp", scatter_dimension=0, tiled=True
-        ).astype(jnp.float32),
-        lax.psum_scatter(
-            gradients[4].astype(jnp.bfloat16), "fsdp", scatter_dimension=0, tiled=True
-        ).astype(jnp.float32),
-        lax.psum_scatter(
-            gradients[5].astype(jnp.bfloat16), "fsdp", scatter_dimension=0, tiled=True
-        ).astype(jnp.float32),
-    )
-    summed = (
-        lax.psum(shard_query.astype(jnp.bfloat16), "rep").astype(jnp.float32),
-        lax.psum(shard_key.astype(jnp.bfloat16), "rep").astype(jnp.float32),
-        lax.psum(shard_value.astype(jnp.bfloat16), "rep").astype(jnp.float32),
-        lax.psum(shard_output.astype(jnp.bfloat16), "rep").astype(jnp.float32),
-        lax.psum(shard_attention_gain.astype(jnp.bfloat16), "rep").astype(jnp.float32),
-        lax.psum(shard_table.astype(jnp.bfloat16), "rep").astype(jnp.float32),
-        lax.psum(shard_inner.astype(jnp.bfloat16), "rep").astype(jnp.float32),
-        lax.psum(shard_outer.astype(jnp.bfloat16), "rep").astype(jnp.float32),
-        lax.psum(shard_ffn_gain.astype(jnp.bfloat16), "rep").astype(jnp.float32),
-    )
+
+
+def gather_all(query_weight, key_weight, value_weight, output_weight, attention_gain, bias_table,
+               inner_weight, outer_weight, feedforward_gain):
+    return tuple(
+        lax.all_gather(part, "fsdp", axis=0, tiled=True)
+        for part in (
+            query_weight, key_weight, value_weight, output_weight, attention_gain, bias_table,
+            inner_weight, outer_weight, feedforward_gain,
+        )
+    )
+
+
+def sum_all(gradients):
+    def one(part):
+        part = lax.psum_scatter(
+            part.astype(jnp.bfloat16), "fsdp", scatter_dimension=0, tiled=True
+        )
+        return lax.psum(part, "rep").astype(jnp.float32)
+
+    return tuple(one(part) for part in gradients)
+
+
+def gather_linked(query_weight, key_weight, value_weight, output_weight, attention_gain,
+                  bias_table, inner_weight, outer_weight, feedforward_gain):
+    rows, width = query_weight.shape
+    chunks = inner_weight.shape[1] // width
+    inner_units = jnp.transpose(inner_weight.reshape(rows, chunks, width), (1, 0, 2))
+    outer_units = outer_weight.reshape(chunks, rows, width)
+    own = jnp.concatenate(
+        (
+            jnp.stack((query_weight, key_weight, value_weight, output_weight)),
+            inner_units,
+            outer_units,
+        )
+    )
+    small = pack_small(attention_gain, feedforward_gain, bias_table, jnp.bfloat16, 16)
+    full, all_small = gather_call(own, small)
+    square = [full[:, :, u].reshape(8 * rows, width) for u in range(4)]
+    inner = jnp.concatenate(
+        [full[:, :, 4 + u].reshape(8 * rows, width) for u in range(chunks)], axis=1
+    )
+    outer = full[:, :, 4 + chunks :].reshape(8 * chunks * rows, width)
+    table_rows, heads = bias_table.shape
     return (
-        block_output,
-        input_grad,
-        summed[0],
-        summed[1],
-        summed[2],
-        summed[3],
-        summed[4],
-        summed[5],
-        summed[6],
-        summed[7],
-        summed[8],
-    )
+        *square,
+        all_small[:, 0, :rows].reshape(-1),
+        all_small[:, 2 : 2 + table_rows, :heads].reshape(8 * table_rows, heads),
+        inner,
+        outer,
+        all_small[:, 1, :rows].reshape(-1),
+    )
+
+
+def sum_linked(gradients):
+    query, key, value, output, gain, table, inner, outer, ffn_gain = gradients
+    width = query.shape[1]
+    rows = query.shape[0] // 8
+    chunks = inner.shape[1] // width
+    inner_units = jnp.transpose(inner.reshape(4, 2, rows, chunks, width), (0, 1, 3, 2, 4))
+    full = jnp.concatenate(
+        [part.reshape(4, 2, 1, rows, width).astype(jnp.bfloat16) for part in (query, key, value, output)]
+        + [
+            inner_units.astype(jnp.bfloat16),
+            outer.reshape(4, 2, chunks, rows, width).astype(jnp.bfloat16),
+        ],
+        axis=2,
+    )
+    table_rows = table.shape[0] // 8
+    heads = table.shape[1]
+    small = pack_small(
+        gain.reshape(8, rows), ffn_gain.reshape(8, rows), table.reshape(8, table_rows, heads),
+        jnp.float32, 8,
+    )
+    own, own_small = scatter_call(full, small)
+    own = own.astype(jnp.float32)
+    return (
+        own[0],
+        own[1],
+        own[2],
+        own[3],
+        own_small[0, :rows],
+        own_small[2 : 2 + table_rows, :heads],
+        jnp.transpose(own[4 : 4 + chunks], (1, 0, 2)).reshape(rows, chunks * width),
+        own[4 + chunks :].reshape(chunks * rows, width),
+        own_small[1, :rows],
+    )
+
+
+def local(linked, inputs, lengths, cotangent, query_weight, key_weight, value_weight,
+          output_weight, attention_gain, bias_table, inner_weight, outer_weight,
+          feedforward_gain):
+    gather, reduce = (gather_linked, sum_linked) if linked else (gather_all, sum_all)
+    weights = gather(
+        query_weight, key_weight, value_weight, output_weight, attention_gain, bias_table,
+        inner_weight, outer_weight, feedforward_gain,
+    )
+    block_output, input_grad, gradients = compute(inputs, lengths, cotangent, weights)
+    return (block_output, input_grad) + reduce(gradients)
+
+
+def can_link(mesh):
+    return mesh.shape["fsdp"] == 8 and mesh.shape["rep"] == 4
 
 
 def solution(mesh):
@@ -350,7 +811,7 @@
         P("fsdp"),
     )
     return jax.shard_map(
-        local,
+        functools.partial(local, can_link(mesh)),
         mesh=mesh,
         in_specs=placed,
         out_specs=(

time: 908 us -> 317 us (0.35)
  waiting for transfers between devices: 679 us -> 0 us
  Pallas kernels: 36.3 us -> 198 us
  blocking collectives: 73.1 us -> 0 us
  local copies, waits for them, and re-layouts: 21.2 us -> 54.8 us
  between operations: 16.8 us -> 2.03 us
  matrix products: 64.1 us -> 51.4 us
    reduce_scatter x6 -> x0, waiting for transfers between devices: 386 us -> none  [the longest x1 99.7 us: local(): lax.psum_scatter(gradients[6].astype(jnp.bfloat16), 'fsdp', scatter_dimen...]
    all_gather x6 -> x0, waiting for transfers between devices: 247 us -> none  [the longest x1 77.5 us: local(): lax.all_gather(inner_weight, 'fsdp', axis=0, tiled=True)]
    pallas_call x0 -> x2, Pallas kernels: none -> 162 us  [the longest x1 89.5 us: scatter_call(): pl.pallas_call(functools.partial(scatter_kernel, (9, 8, 7, 5, 3, 1, 0)),...]
    unnamed x2 -> x0, blocking collectives: 47.1 us -> none
    psum x1 -> x0, waiting for transfers between devices: 40.5 us -> none  [local(): lax.psum(shard_query.astype(jnp.bfloat16), 'rep').astype(jnp.float32)]
    convert_element_type x0 -> x4, local copies, waits for them, and re-layouts: none -> 14.7 us  [the longest x1 9.86 us: sum_linked(): inner_units.astype(jnp.bfloat16)]
    all_gather x1 -> x0, blocking collectives: 13.2 us -> none  [local(): lax.all_gather(bias_table, 'fsdp', axis=0, tiled=True)]
    psum x1 -> x0, blocking collectives: 12.8 us -> none  [local(): lax.psum(shard_attention_gain.astype(jnp.bfloat16), 'rep')]
  transfers between devices with their start and end apart: 13 -> 0, of which waited for: 12 -> 0; matrix products, arithmetic and copies ran while one was open for 7% -> 0% of each run, Pallas kernels for 2% -> 0%
where the time goes in v2:
time: 317 us; the launch traced here: 316 us
  Pallas kernels  198 us (62%)
  local copies, waits for them, and re-layouts  54.8 us (17%)
  matrix products  51.4 us (16%)
  other arithmetic  9.19 us (3%)
    pallas_call x1, Pallas kernels, scatter_call(): pl.pallas_call(functools.partial(scatter_kernel, (9, 8, 7, 5, 3, 1, 0)),...  89.5 us
    pallas_call x1, Pallas kernels, gather_call(): pl.pallas_call(functools.partial(gather_kernel, (6, 4, 2, 0, 7)), out_sha...  72.5 us
    unnamed x105, local copies, waits for them, and re-layouts  21.6 us
    pallas_call x1, Pallas kernels, att_fwd(): pl.pallas_call(functools.partial(fwd_kernel, T), grid=(H // 2,), in_specs...  18.1 us
    pallas_call x1, Pallas kernels, att_bwd(): pl.pallas_call(functools.partial(bwd_kernel, T), grid=(H // 2,), in_specs...  18 us
    dot_general x4, matrix products, contract_cols(): lax.dot_general(left, right, (((1,), (1,)), ((), ())), preferred_element_...  16.9 us
    dot_general x4, matrix products, contract_rows(): lax.dot_general(left, right, (((0,), (0,)), ((), ())), preferred_element_...  13 us
    convert_element_type x1, local copies, waits for them, and re-layouts, sum_linked(): inner_units.astype(jnp.bfloat16)  9.86 us

profile of v2, /device:TPU:1, one launch (start us, length us, event | category | flops | bytes accessed | tf_op | source)
XLA Modules:
  0.0 315.5 jit_solution(6542024576505958929)
XLA Ops:
  1.4 1.4 fusion.19
  2.8 0.7 fusion.51
  4.2 0.9 bitcast_dynamic-update-slice_fusion.4
  5.1 0.9 bitcast_dynamic-update-slice_fusion.3
  6.1 0.9 bitcast_dynamic-update-slice_fusion.2
  7.0 0.9 bitcast_dynamic-update-slice_fusion.1
  8.0 1.2 copy-done.15
  9.3 72.5 %shard_map.203 = (bf16[4,2,12,96,768]{4,3,2,1,0:T(8,128)(2,1)}, bf16[8,16,128]{2,1,0:T(8,128)(2,1)}) custom-call(bf16[12,96,768]{2,1,0:T(8,128)(2,1)} %copy-done.15, bf16[16,128]{1,0:T(8,128)(2,1)} %pad.33.small), custom_call_target="tpu_custom_call" | custom-call | tf_op jit(solution)/shard_map/pallas_call | solution.py:453
  81.8 0.7 slice.91
  82.5 0.8 convert_reduce_fusion
  83.8 4.8 %slice.98 = bf16[4,2,4,96,768]{4,3,2,1,0:T(8,128)(2,1)} slice(bf16[4,2,12,96,768]{4,3,2,1,0:T(8,128)(2,1)} %get-tuple-element.22), slice={[0:4], [0:2], [8:12], [0:96], [0:768]} | slice | bytes 9437184 | tf_op jit(solution)/shard_map/slice | solution.py:735
  88.6 4.2 %fusion.68 = (bf16[4,2,1,96,768]{4,3,2,1,0:T(8,128)(2,1)S(1)}, bf16[4,2,1,96,768]{4,3,2,1,0:T(8,128)(2,1)S(1)}, bf16[4,2,1,96,768]{4,3,2,1,0:T(8,128)(2,1)S(1)},...) fusion(bf16[4,2,12,96,768]{4,3,2,1,0:T(8,128)(2,1)} %get-tuple-, ...), kind=kLoop, calls=%fused_computation.134 | loop fusion | bytes 18874368 | tf_op jit(solution)/shard_map/slice | solution.py:733
  92.8 3.2 %convolution_convert_fusion.2 = bf16[512,2304]{1,0:T(8,128)(2,1)S(1)} fusion(bf16[768,768]{1,0:T(8,128)(2,1)S(1)} %bitcast.113, bf16[768,768]{1,0:T(8,128)(2,1)S(1)} %bitcast.115, bf16[768,768]{1,0:T(8,128)(2,1)S(1)} %bitcast.117, bf16[1,512,768]{2,1,0:T(8,128)(2,1)S(1)} %copy-done.13, f32[768]{0:T(1024)S(1)} %reshape.261, f32[512]{0:T(512)S(1)} %fusion.58), kind=kOutput, calls=%fused_computation.23 | convolution fusion | flops 1825308672 | bytes 6689792 | tf_op jit(solution)/shard_map/dot_general | solution.py:627
  96.3 18.1 %shard_map.204 = (bf16[512,768]{1,0:T(8,128)(2,1)S(1)}, bf16[12,512,512]{2,1,0:T(8,128)(2,1)S(1)}) custom-call(s32[1]{0:T(128)} %copy.57.len_ref, bf16[512,768]{1,0:T(8,128)(2,1)S(1)} %get-tuple-element.54.q_ref, bf16[512,768]{1,0:T(8,128)(2,1)S(1)} %get-tuple-element.53.k_ref, bf16[512,768]{1,0:T(8,128)(2,1)S(1)} %get-tuple-element.52.v_ref, ...), custom_call_target="tpu_custom_call" | custom-call | tf_op jit(solution)/shard_map/pallas_call | solution.py:136
  114.4 0.9 multiply_reduce_fusion.2
  115.4 7.7 %fusion.10 = (bf16[3072,512]{0,1:T(8,128)(2,1)}, f32[512,3072]{1,0:T(8,128)}) fusion(bf16[768,768]{1,0:T(8,128)(2,1)S(1)} %bitcast.123, bf16[768,768]{1,0:T(8,128)(2,1)S(1)} %bitcast.125, bf16[768,768]{1,0:T(8,128)(2,1)S(1)} %bitcast.127, bf16[768,768]{1,0:T(8,128)(2,1)S(1)} %bitcast.121, f32[512,768]{1,0:T(8,128)S(1)} %get-tuple-element.58, ...), kind=kOutput, calls=%fused_computation.15 | convolution fusion | flops 2450128896 | bytes 15733760 | tf_op jit(solution)/shard_map/dot_general | solution.py:639
  123.1 4.7 %copy.31 = bf16[3072,512]{1,0:T(8,128)(2,1)} copy(bf16[3072,512]{0,1:T(8,128)(2,1)} %get-tuple-element.61) | data formatting | bytes 6291456 | tf_op jit(solution)/shard_map/convert_element_type | solution.py:640
  127.7 9.4 %fusion.23 = bf16[1,512,768]{2,1,0:T(8,128)(2,1)} fusion(f32[512,768]{1,0:T(8,128)} %copy-done.16, bf16[3072,768]{1,0:T(8,128)(2,1)} %bitcast.110, f32[512,3072]{1,0:T(8,128)} %get-tuple-element.62), kind=kOutput, calls=%fused_computation.52 | convolution fusion | flops 2430861312 | bytes 13369344 | tf_op jit(solution)/shard_map/dot_general | solution.py:641
  137.2 8.8 %fusion.3 = bf16[512,3072]{1,0:T(8,128)(2,1)S(1)} fusion(f32[512,3072]{1,0:T(8,128)S(1)} %copy-done.43, bf16[3072,768]{1,0:T(8,128)(2,1)} %bitcast.111, bf16[1,512,768]{2,1,0:T(8,128)(2,1)S(1)} %copy-done.35, f32[512]{0:T(512)S(1)} %fusion.57), kind=kOutput, calls=%fused_computation.8 | convolution fusion | flops 2454847488 | bytes 14944256 | tf_op jit(solution)/shard_map/dot_general | solution.py:161
  146.1 3.9 %multiply_reduce_fusion = (f32[768]{0:T(1024)S(1)}, f32[512]{0:T(512)S(1)}, f32[512,768]{1,0:T(8,128)}) fusion(f32[512,768]{1,0:T(8,128)S(1)} %copy-done.17, f32[512]{0:T(512)S(1)} %fusion.59, f32[768]{0:T(1024)S(1)} %reshape.262, bf16[512,3072]{1,0:T(8,128)(2,1)S(1)} %fusion.3, bf16[768,768]{1,0:T(8,128)(2,1)S(1)} %bitcast.124, ...), kind=kOutput, calls=%fused_computation.42 | convolution fusion | flops 2437151488 | bytes 11020288 | tf_op jit(solution)/shard_map/dot_general | solution.py:161
  150.1 2.7 fusion.16
  152.8 1.2 copy-done.8
  153.9 0.8 convolution_convert_fusion.4.do_ref
  154.8 2.8 copy-done.1
  157.6 18.0 %shard_map.205 = (bf16[512,768]{1,0:T(8,128)(2,1)S(1)}, bf16[512,768]{1,0:T(8,128)(2,1)S(1)}, bf16[512,768]{1,0:T(8,128)(2,1)S(1)}, f32[6,2,512]{2,1,0:T(2,128)S(1)}) custom-call(bf16[512,768]{1,0:T(8,128)(2,1)S(1)} %get-tuple-element.54.q_ref, bf16[512,768]{1,0:T(8,128)(2,1)S(1)} %get-tuple-element.53.k_ref, bf16[512,768]{1,0:T(8,128)(2,1)S(1)} %get-tuple-element.52.v_ref, ...), custom_call_target="tpu_custom_call" | custom-call | tf_op jit(solution)/shard_map/pallas_call | solution.py:146
  175.6 0.9 copy-done.2
  176.5 1.0 copy-done.4
  177.4 0.9 copy-done.6
  178.3 4.6 %convolution_convert_fusion = bf16[768,3072]{1,0:T(8,128)(2,1)} fusion(bf16[512,3072]{1,0:T(8,128)(2,1)S(1)} %copy-done.42, f32[512,768]{1,0:T(8,128)S(1)} %copy-done.18, f32[768]{0:T(1024)S(1)} %reshape.262, f32[512]{0:T(512)S(1)} %fusion.59), kind=kOutput, calls=%fused_computation.18 | convolution fusion | flops 2419458048 | bytes 9442304 | tf_op jit(solution)/shard_map/dot_general | solution.py:155
  182.9 9.9 %convert_element_type.257 = bf16[4,2,96,4,768]{4,3,2,1,0:T(4,128)(2,1)} reshape(bf16[768,3072]{1,0:T(8,128)(2,1)} %convolution_convert_fusion) | data formatting | bytes 9437184 | tf_op jit(solution)/shard_map/convert_element_type | solution.py:756
  193.0 1.8 convolution_convert_fusion.3
  194.9 1.0 copy-done.3
  196.9 3.3 %fusion.15 = (f32[768]{0:T(1024)S(1)}, f32[512]{0:T(512)S(1)}, f32[512,768]{1,0:T(8,128)}) fusion(bf16[1,512,768]{2,1,0:T(8,128)(2,1)S(1)} %copy-done.14, f32[512]{0:T(512)S(1)} %fusion.58, f32[768]{0:T(1024)S(1)} %reshape.261, bf16[512,2304]{1,0:T(8,128)(2,1)S(1)} %constant_dynamic-update-slice_fusion.1, bf16[768,768]{1,0:T(8,128)(2,1)S(1)} %bitcast.114, ...), kind=kOutput, calls=%fused_computation.36 | convolution fusion | flops 1825307392 | bytes 8267776 | tf_op jit(solution)/shard_map/dot_general | solution.py:161
  200.3 3.1 fusion.18
  203.4 0.6 pad.37.small
  204.0 2.1 convolution_convert_fusion.1
  206.5 1.1 constant_dynamic-update-slice_fusion.7
  207.6 1.1 constant_dynamic-update-slice_fusion.6
  208.7 1.1 constant_dynamic-update-slice_fusion.5
  209.9 1.2 constant_dynamic-update-slice_fusion.4
  211.1 3.1 bitcast_dynamic-update-slice_fusion
  214.2 4.5 %convert_dynamic-update-slice_fusion.full_in = bf16[4,2,12,96,768]{4,3,2,1,0:T(8,128)(2,1)} fusion(bf16[4,2,12,96,768]{4,3,2,1,0:T(8,128)(2,1)} %bitcast_dynamic-update-slice_fusion, bf16[4,2,4,96,512]{4,3,2,1,0:T(8,128)(2,1)S(1)} %bitcast.112, bf16[1,512,768]{2,1,0:T(8,128)(2,1)S(1)} %copy-done.36, f32[512]{0:T(512)S(1)} %fusion.57), kind=kOutput, calls=%fused_computation.22 | convolution fusion | flops 2419458048 | bytes 8652800 | tf_op jit(solution)/shard_map/dot_general | solution.py:155
  218.7 89.5 %shard_map.206 = (bf16[12,96,768]{2,1,0:T(8,128)(2,1)}, f32[8,128]{1,0:T(8,128)}) custom-call(bf16[4,2,12,96,768]{4,3,2,1,0:T(8,128)(2,1)} %convert_dynamic-update-slice_fusion.full_in, f32[8,8,128]{2,1,0:T(8,128)} %pad.37.small), custom_call_target="tpu_custom_call" | custom-call | tf_op jit(solution)/shard_map/pallas_call | solution.py:569
  308.2 1.3 slice_bitcast_fusion.5
  309.5 1.2 slice.107
  310.7 2.2 slice.122
  313.3 1.0 slice_bitcast_fusion.1
  314.4 1.1 copy.38
  (115 shorter events, 3.7 us)
Async XLA Ops:
  0.6 7.3 %copy-start.38 = (bf16[384,768]{1,0:T(8,128)(2,1)S(1)}, bf16[384,768]{1,0:T(8,128)(2,1)}, u32[]{:S(2)}) copy-start(bf16[384,768]{1,0:T(8,128)(2,1)} %param.22) | copy-start | bytes 1769476
  0.7 7.3 %copy-start.37 = (bf16[96,3072]{1,0:T(8,128)(2,1)S(1)}, bf16[96,3072]{1,0:T(8,128)(2,1)}, u32[]{:S(2)}) copy-start(bf16[96,3072]{1,0:T(8,128)(2,1)} %param.21) | copy-start | bytes 1769476
  8.0 1.2 copy-start.15
  88.6 4.3 %copy-start.13 = (bf16[1,512,768]{2,1,0:T(8,128)(2,1)S(1)}, bf16[1,512,768]{2,1,0:T(8,128)(2,1)}, u32[]{:S(2)}) copy-start(bf16[1,512,768]{2,1,0:T(8,128)(2,1)} %param.12) | copy-start | bytes 2359300
  92.8 3.4 %copy-start.19 = (bf16[4,2,1,96,768]{4,3,2,1,0:T(8,128)(2,1)}, bf16[4,2,1,96,768]{4,3,2,1,0:T(8,128)(2,1)S(1)}, u32[]{:S(2)}) copy-start(bf16[4,2,1,96,768]{4,3,2,1,0:T(8,128)(2,1)S(1)} %get-tuple-element.42) | copy-start | bytes 3538948
  92.8 3.4 %copy-start.21 = (bf16[4,2,1,96,768]{4,3,2,1,0:T(8,128)(2,1)}, bf16[4,2,1,96,768]{4,3,2,1,0:T(8,128)(2,1)S(1)}, u32[]{:S(2)}) copy-start(bf16[4,2,1,96,768]{4,3,2,1,0:T(8,128)(2,1)S(1)} %get-tuple-element.43) | copy-start | bytes 3538948
  92.8 3.4 %copy-start.23 = (bf16[4,2,1,96,768]{4,3,2,1,0:T(8,128)(2,1)}, bf16[4,2,1,96,768]{4,3,2,1,0:T(8,128)(2,1)S(1)}, u32[]{:S(2)}) copy-start(bf16[4,2,1,96,768]{4,3,2,1,0:T(8,128)(2,1)S(1)} %get-tuple-element.44) | copy-start | bytes 3538948
  92.8 21.6 %copy-start.25 = (bf16[4,2,1,96,768]{4,3,2,1,0:T(8,128)(2,1)}, bf16[4,2,1,96,768]{4,3,2,1,0:T(8,128)(2,1)S(1)}, u32[]{:S(2)}) copy-start(bf16[4,2,1,96,768]{4,3,2,1,0:T(8,128)(2,1)S(1)} %get-tuple-element.41) | copy-start | bytes 3538948
  92.8 22.5 %copy-start.27 = (bf16[4,2,1,96,768]{4,3,2,1,0:T(8,128)(2,1)}, bf16[4,2,1,96,768]{4,3,2,1,0:T(8,128)(2,1)S(1)}, u32[]{:S(2)}) copy-start(bf16[4,2,1,96,768]{4,3,2,1,0:T(8,128)(2,1)S(1)} %get-tuple-element.37) | copy-start | bytes 3538948
  92.8 22.5 %copy-start.29 = (bf16[4,2,1,96,768]{4,3,2,1,0:T(8,128)(2,1)}, bf16[4,2,1,96,768]{4,3,2,1,0:T(8,128)(2,1)S(1)}, u32[]{:S(2)}) copy-start(bf16[4,2,1,96,768]{4,3,2,1,0:T(8,128)(2,1)S(1)} %get-tuple-element.38) | copy-start | bytes 3538948
  92.8 22.5 %copy-start.31 = (bf16[4,2,1,96,768]{4,3,2,1,0:T(8,128)(2,1)}, bf16[4,2,1,96,768]{4,3,2,1,0:T(8,128)(2,1)S(1)}, u32[]{:S(2)}) copy-start(bf16[4,2,1,96,768]{4,3,2,1,0:T(8,128)(2,1)S(1)} %get-tuple-element.39) | copy-start | bytes 3538948
  92.8 22.5 %copy-start.33 = (bf16[4,2,1,96,768]{4,3,2,1,0:T(8,128)(2,1)}, bf16[4,2,1,96,768]{4,3,2,1,0:T(8,128)(2,1)S(1)}, u32[]{:S(2)}) copy-start(bf16[4,2,1,96,768]{4,3,2,1,0:T(8,128)(2,1)S(1)} %get-tuple-element.40) | copy-start | bytes 3538948
  114.4 8.7 %copy-start = (bf16[12,512,512]{2,1,0:T(8,128)(2,1)}, bf16[12,512,512]{2,1,0:T(8,128)(2,1)S(1)}, u32[]{:S(2)}) copy-start(bf16[12,512,512]{2,1,0:T(8,128)(2,1)S(1)} %get-tuple-element.24.p_ref) | copy-start | bytes 18874372
  115.3 7.8 %copy-start.16 = (f32[512,768]{1,0:T(8,128)}, f32[512,768]{1,0:T(8,128)S(1)}, u32[]{:S(2)}) copy-start(f32[512,768]{1,0:T(8,128)S(1)} %get-tuple-element.58) | copy-start | bytes 4718596
  127.7 9.4 %copy-start.35 = (bf16[1,512,768]{2,1,0:T(8,128)(2,1)S(1)}, bf16[1,512,768]{2,1,0:T(8,128)(2,1)}, u32[]{:S(2)}) copy-start(bf16[1,512,768]{2,1,0:T(8,128)(2,1)} %param.14) | copy-start | bytes 2359300
  127.7 9.4 %copy-start.43 = (f32[512,3072]{1,0:T(8,128)S(1)}, f32[512,3072]{1,0:T(8,128)}, u32[]{:S(2)}) copy-start(f32[512,3072]{1,0:T(8,128)} %get-tuple-element.62) | copy-start | bytes 18874372
  137.1 8.9 %copy-start.17 = (f32[512,768]{1,0:T(8,128)S(1)}, f32[512,768]{1,0:T(8,128)}, u32[]{:S(2)}) copy-start(f32[512,768]{1,0:T(8,128)} %copy-done.16) | copy-start | bytes 4718596
  137.1 8.9 %copy-start.28 = (bf16[4,2,1,96,768]{4,3,2,1,0:T(8,128)(2,1)S(1)}, bf16[4,2,1,96,768]{4,3,2,1,0:T(8,128)(2,1)}, u32[]{:S(2)}) copy-start(bf16[4,2,1,96,768]{4,3,2,1,0:T(8,128)(2,1)} %copy-done.27) | copy-start | bytes 3538948
  137.1 8.9 %copy-start.30 = (bf16[4,2,1,96,768]{4,3,2,1,0:T(8,128)(2,1)S(1)}, bf16[4,2,1,96,768]{4,3,2,1,0:T(8,128)(2,1)}, u32[]{:S(2)}) copy-start(bf16[4,2,1,96,768]{4,3,2,1,0:T(8,128)(2,1)} %copy-done.29) | copy-start | bytes 3538948
  137.1 8.9 %copy-start.32 = (bf16[4,2,1,96,768]{4,3,2,1,0:T(8,128)(2,1)S(1)}, bf16[4,2,1,96,768]{4,3,2,1,0:T(8,128)(2,1)}, u32[]{:S(2)}) copy-start(bf16[4,2,1,96,768]{4,3,2,1,0:T(8,128)(2,1)} %copy-done.31) | copy-start | bytes 3538948
  137.2 8.9 %copy-start.34 = (bf16[4,2,1,96,768]{4,3,2,1,0:T(8,128)(2,1)S(1)}, bf16[4,2,1,96,768]{4,3,2,1,0:T(8,128)(2,1)}, u32[]{:S(2)}) copy-start(bf16[4,2,1,96,768]{4,3,2,1,0:T(8,128)(2,1)} %copy-done.33) | copy-start | bytes 3538948
  146.0 3.9 %copy-start.41 = (bf16[512,3072]{1,0:T(8,128)(2,1)}, bf16[512,3072]{1,0:T(8,128)(2,1)S(1)}, u32[]{:S(2)}) copy-start(bf16[512,3072]{1,0:T(8,128)(2,1)S(1)} %fusion.3) | copy-start | bytes 9437188
  150.1 3.9 %copy-start.26 = (bf16[4,2,1,96,768]{4,3,2,1,0:T(8,128)(2,1)S(1)}, bf16[4,2,1,96,768]{4,3,2,1,0:T(8,128)(2,1)}, u32[]{:S(2)}) copy-start(bf16[4,2,1,96,768]{4,3,2,1,0:T(8,128)(2,1)} %copy-done.25) | copy-start | bytes 3538948
  152.8 1.2 copy-start.8
  154.8 2.8 copy-start.1
  157.5 20.8 %copy-start.18 = (f32[512,768]{1,0:T(8,128)S(1)}, f32[512,768]{1,0:T(8,128)}, u32[]{:S(2)}) copy-start(f32[512,768]{1,0:T(8,128)} %copy-done.16) | copy-start | bytes 4718596
  157.5 20.8 %copy-start.42 = (bf16[512,3072]{1,0:T(8,128)(2,1)S(1)}, bf16[512,3072]{1,0:T(8,128)(2,1)}, u32[]{:S(2)}) copy-start(bf16[512,3072]{1,0:T(8,128)(2,1)} %copy-done.41) | copy-start | bytes 9437188
  175.6 0.9 copy-start.2
  176.5 1.0 copy-start.4
  177.4 0.9 copy-start.6
  182.9 10.1 %copy-start.9 = (f32[512,768]{1,0:T(8,128)S(1)}, f32[512,768]{1,0:T(8,128)}, u32[]{:S(2)}) copy-start(f32[512,768]{1,0:T(8,128)} %copy-done.8) | copy-start | bytes 4718596
  192.7 2.1 copy-start.7
  192.9 1.9 copy-start.5
  193.0 3.0 copy-start.24
  194.8 1.1 copy-start.3
  194.8 1.4 copy-start.14
  194.8 1.7 copy-start.20
  194.8 2.1 copy-start.22
  196.9 3.3 %copy-start.39 = (bf16[512,2304]{1,0:T(8,128)(2,1)}, bf16[512,2304]{1,0:T(8,128)(2,1)S(1)}, u32[]{:S(2)}) copy-start(bf16[512,2304]{1,0:T(8,128)(2,1)S(1)} %constant_dynamic-update-slice_fusion.1) | copy-start | bytes 7077892
  200.3 3.8 %copy-start.40 = (bf16[512,2304]{1,0:T(8,128)(2,1)S(1)}, bf16[512,2304]{1,0:T(8,128)(2,1)}, u32[]{:S(2)}) copy-start(bf16[512,2304]{1,0:T(8,128)(2,1)} %copy-done.39) | copy-start | bytes 7077892
  206.2 4.8 %slice-start = ((s8[4718592]{0:T(1024)(128)(4,1)}), s8[4194304]{0:T(1024)(128)(4,1)S(1)}, s32[]{:S(2)}) async-start(s8[4718592]{0:T(1024)(128)(4,1)} %bitcast.104), calls=%async_computation | async-start | bytes 8388608
  206.4 4.6 %slice-start.1 = ((s8[4718592]{0:T(1024)(128)(4,1)}), s8[524288]{0:T(1024)(128)(4,1)S(1)}, s32[]{:S(2)}) async-start(s8[4718592]{0:T(1024)(128)(4,1)} %bitcast.104), calls=%async_computation.1 | async-start | bytes 1048576
  207.6 2.3 copy-start.11
  211.0 3.2 copy-start.12
  211.0 3.1 copy-start.36
  308.2 4.7 %copy-start.10 = (bf16[12,96,768]{2,1,0:T(8,128)(2,1)S(1)}, bf16[12,96,768]{2,1,0:T(8,128)(2,1)}, u32[]{:S(2)}) copy-start(bf16[12,96,768]{2,1,0:T(8,128)(2,1)} %get-tuple-element.29) | copy-start | bytes 5308420

commit v3 on v2

--- a/solution.py
+++ b/solution.py
@@ -322,25 +322,25 @@
 class Scatter(Links):
     slots = 8
 
-    def __init__(self, full, own, from_core, from_y, from_x, from_z, send_sems, recv_sems):
+    def __init__(self, slot, full, own, from_core, from_y, from_x, from_z, send_sems, recv_sems):
         super().__init__(own.shape[1], send_sems, recv_sems)
-        self.full, self.own = full, own
+        self.slot, self.full, self.own = slot, full, own
         self.from_core, self.from_y, self.from_x, self.from_z = from_core, from_y, from_x, from_z
 
     def core_copy(self, g):
-        part = self.full.at[:, :, g, self.other_half]
+        part = self.full.at[:, :, self.slot(g), self.other_half]
         return self.copy(part, self.from_core.at[g], g, 0, self.to_core())
 
     def y_copy(self, g):
-        part = self.full.at[:, :, g, self.other_third]
+        part = self.full.at[:, :, self.slot(g), self.other_third]
         return self.copy(part, self.from_y.at[g], g, 1, self.to_y())
 
     def x_copy(self, g):
-        part = self.full.at[:, 1 - self.x, g, self.plane]
+        part = self.full.at[:, 1 - self.x, self.slot(g), self.plane]
         return self.copy(part, self.from_x.at[g], g, 2, self.to_x())
 
     def z_copy(self, g, k):
-        part = self.full.at[lax.rem(self.z + k, 4), self.x, g, self.plane]
+        part = self.full.at[lax.rem(self.z + k, 4), self.x, self.slot(g), self.plane]
         return self.copy(part, self.from_z.at[g, k - 1], g, 2 + k, self.to_z(k))
 
     def back_y_copy(self, g):
@@ -358,25 +358,25 @@
         self.core_copy(g).wait_recv()
         for a in range(4):
             for b in range(2):
-                self.full[a, b, g, self.half] += self.from_core[g, a, b]
+                self.full[a, b, self.slot(g), self.half] += self.from_core[g, a, b]
         self.y_copy(g).start()
 
     def after_y(self, g):
         self.y_copy(g).wait_recv()
         for a in range(4):
             for b in range(2):
-                self.full[a, b, g, self.own_third] += self.from_y[g, a, b]
+                self.full[a, b, self.slot(g), self.own_third] += self.from_y[g, a, b]
         self.x_copy(g).start()
 
     def after_x(self, g):
         self.x_copy(g).wait_recv()
         for a in range(4):
-            self.full[a, self.x, g, self.plane] += self.from_x[g, a]
+            self.full[a, self.x, self.slot(g), self.plane] += self.from_x[g, a]
         for k in (1, 2, 3):
             self.z_copy(g, k).start()
 
     def after_z(self, g):
-        total = self.full[self.z, self.x, g, self.plane].astype(jnp.float32)
+        total = self.full[self.z, self.x, self.slot(g), self.plane].astype(jnp.float32)
         for k in (1, 2, 3):
             self.z_copy(g, k).wait_recv()
             total = total + self.from_z[g, k - 1].astype(jnp.float32)
@@ -402,213 +402,6 @@
         for k in (1, 2, 3):
             self.z_copy(g, k).wait_send()
         self.back_core_copy(g).wait_send()
-
-
-def small_gather(small, all_small, send_sems, recv_sems):
-    shard = lax.axis_index("fsdp")
-    copy = lax.axis_index("rep")
-    return [
-        pltpu.make_async_remote_copy(
-            src_ref=small,
-            dst_ref=all_small.at[shard],
-            send_sem=send_sems.at[k - 1],
-            recv_sem=recv_sems.at[k - 1],
-            device_id=(lax.rem(shard + k, 8), copy),
-            device_id_type=MESH,
-        )
-        for k in range(1, 8)
-    ]
-
-
-def gather_kernel(lags, own, small, full, all_small, sends, recvs, small_sends, small_recvs, sem):
-    shard = lax.axis_index("fsdp")
-    greet()
-    smalls = small_gather(small, all_small, small_sends, small_recvs)
-    for copy in smalls:
-        copy.start()
-    moves = Gather(own, full, sends, recvs)
-    keep = pltpu.make_async_copy(own, full.at[moves.z, moves.x], sem.at[0])
-    keep_small = pltpu.make_async_copy(small, all_small.at[shard], sem.at[1])
-    keep.start()
-    keep_small.start()
-    units = own.shape[0]
-    stages = (moves.after_y, moves.after_x, moves.after_z, moves.start, moves.after_core)
-    schedule(list(zip(stages, lags)), units)
-
-    def drain(g, carry):
-        moves.drain(g)
-        return carry
-
-    lax.fori_loop(0, units, drain, 0)
-    for copy in smalls:
-        copy.wait()
-    keep.wait()
-    keep_small.wait()
-
-
-def gather_call(own, small):
-    units = own.shape[0]
-    anywhere = pl.BlockSpec(memory_space=pl.ANY)
-    sems = pltpu.SemaphoreType.DMA
-    return pl.pallas_call(
-        functools.partial(gather_kernel, (6, 4, 2, 0, 7)),
-        out_shape=(
-            jax.ShapeDtypeStruct((4, 2) + own.shape, own.dtype),
-            jax.ShapeDtypeStruct((8,) + small.shape, small.dtype),
-        ),
-        in_specs=[anywhere, anywhere],
-        out_specs=[anywhere, anywhere],
-        scratch_shapes=[
-            sems((units, Gather.slots)),
-            sems((units, Gather.slots)),
-            sems((7,)),
-            sems((7,)),
-            sems((2,)),
-        ],
-        compiler_params=pltpu.CompilerParams(collective_id=0, has_side_effects=True),
-    )(own, small)
-
-
-def scatter_kernel(
-    lags, full_in, small, own_out, small_out, full, own, from_core, from_y, from_x, from_z,
-    small_in, small_rep, sends, recvs, load_sems, store_sems, small_sends, small_recvs, rep_sends,
-    rep_recvs,
-):
-    units = own.shape[0]
-    shard = lax.axis_index("fsdp")
-    copy_id = lax.axis_index("rep")
-
-    def load(g):
-        return pltpu.make_async_copy(full_in.at[:, :, g], full.at[:, :, g], load_sems.at[g])
-
-    def store(g):
-        return pltpu.make_async_copy(own.at[g], own_out.at[g], store_sems.at[g])
-
-    def begin(g, carry):
-        load(g).start()
-        return carry
-
-    lax.fori_loop(0, units, begin, 0)
-    greet()
-    smalls = [
-        pltpu.make_async_remote_copy(
-            src_ref=small.at[lax.rem(shard + k, 8)],
-            dst_ref=small_in.at[k - 1],
-            send_sem=small_sends.at[k - 1],
-            recv_sem=small_recvs.at[k - 1],
-            device_id=(lax.rem(shard + k, 8), copy_id),
-            device_id_type=MESH,
-        )
-        for k in range(1, 8)
-    ]
-    for copy in smalls:
-        copy.start()
-    moves = Scatter(full, own, from_core, from_y, from_x, from_z, sends, recvs)
-
-    def first(g):
-        load(g).wait()
-        moves.start(g)
-
-    def last(g):
-        moves.after_back_core(g)
-        store(g).start()
-
-    stages = (
-        last, moves.after_back_y, moves.after_z, moves.after_x, moves.after_y, moves.after_core,
-        first,
-    )
-    schedule(list(zip(stages, lags)), units)
-    total = small[shard]
-    for k, copy in enumerate(smalls):
-        copy.wait_recv()
-        total = total + small_in[k]
-    small_rep[copy_id] = total
-    reps = [
-        pltpu.make_async_remote_copy(
-            src_ref=small_rep.at[copy_id],
-            dst_ref=small_rep.at[copy_id],
-            send_sem=rep_sends.at[k - 1],
-            recv_sem=rep_recvs.at[k - 1],
-            device_id=(shard, lax.rem(copy_id + k, 4)),
-            device_id_type=MESH,
-        )
-        for k in range(1, 4)
-    ]
-    for copy in reps:
-        copy.start()
-    for k in range(1, 4):
-        there = small_rep.at[lax.rem(copy_id + 4 - k, 4)]
-        pltpu.make_async_remote_copy(
-            src_ref=there,
-            dst_ref=there,
-            send_sem=rep_sends.at[k - 1],
-            recv_sem=rep_recvs.at[k - 1],
-            device_id=(shard, lax.rem(copy_id + k, 4)),
-            device_id_type=MESH,
-        ).wait_recv()
-    small_out[...] = (small_rep[0] + small_rep[1]) + (small_rep[2] + small_rep[3])
-
-    def drain(g, carry):
-        moves.drain(g)
-        store(g).wait()
-        return carry
-
-    lax.fori_loop(0, units, drain, 0)
-    for copy in smalls + reps:
-        copy.wait_send()
-
-
-def scatter_call(full, small):
-    units, rows, width = full.shape[2:]
-    half = rows // 2
-    part = half // 3
-    anywhere = pl.BlockSpec(memory_space=pl.ANY)
-    within = pl.BlockSpec(memory_space=pltpu.VMEM)
-    sems = pltpu.SemaphoreType.DMA
-    kind = full.dtype
-    return pl.pallas_call(
-        functools.partial(scatter_kernel, (9, 8, 7, 5, 3, 1, 0)),
-        out_shape=(
-            jax.ShapeDtypeStruct((units, rows, width), kind),
-            jax.ShapeDtypeStruct(small.shape[1:], small.dtype),
-        ),
-        in_specs=[anywhere, within],
-        out_specs=[anywhere, within],
-        scratch_shapes=[
-            pltpu.VMEM(full.shape, kind),
-            pltpu.VMEM((units, rows, width), kind),
-            pltpu.VMEM((units, 4, 2, half, width), kind),
-            pltpu.VMEM((units, 4, 2, part, width), kind),
-            pltpu.VMEM((units, 4, 2 * part, width), kind),
-            pltpu.VMEM((units, 4, 2 * part, width), kind),
-            pltpu.VMEM((7,) + small.shape[1:], small.dtype),
-            pltpu.VMEM((4,) + small.shape[1:], small.dtype),
-            sems((units, Scatter.slots)),
-            sems((units, Scatter.slots)),
-            sems((units,)),
-            sems((units,)),
-            sems((7,)),
-            sems((7,)),
-            sems((3,)),
-            sems((3,)),
-        ],
-        compiler_params=pltpu.CompilerParams(
-            collective_id=1, has_side_effects=True, vmem_limit_bytes=60 * 2**20
-        ),
-    )(full, small)
-
-
-def pack_small(gain_a, gain_f, table, kind, rows):
-    def put(part, rows_here):
-        part = part.reshape(part.shape[:-1] + (rows_here, -1)) if rows_here == 1 else part
-        lead = [(0, 0)] * (part.ndim - 1)
-        return jnp.pad(part, lead + [(0, 128 - part.shape[-1])])
-
-    block = jnp.concatenate(
-        (put(gain_a, 1), put(gain_f, 1), put(table, table.shape[-2])), axis=-2
-    ).astype(kind)
-    lead = [(0, 0)] * (block.ndim - 2)
-    return jnp.pad(block, lead + [(0, rows - block.shape[-2]), (0, 0)])
 
 
 def compute(inputs, lengths, cotangent, weights):
@@ -713,82 +506,627 @@
     return tuple(one(part) for part in gradients)
 
 
-def gather_linked(query_weight, key_weight, value_weight, output_weight, attention_gain,
-                  bias_table, inner_weight, outer_weight, feedforward_gain):
+def gelu_parts(z):
+    square = z * z
+    t = jnp.tanh(gelu_coeff * z * (1.0 + 0.044715 * square))
+    half = 0.5 * (1.0 + t)
+    slope = half + (0.5 * gelu_coeff) * z * (1.0 - t * t) * (1.0 + (3 * 0.044715) * square)
+    return z * half, slope
+
+
+def lanes(start, size):
+    return pl.ds(pl.multiple_of(start, 128), size)
+
+
+def rows_at(start, size):
+    return pl.ds(pl.multiple_of(start, size), size)
+
+
+def loop(count, body):
+    def step(n, carry):
+        body(n)
+        return carry
+
+    lax.fori_loop(0, count, step, 0)
+
+
+def norm_back(grad, gain, values):
+    inverse = lax.rsqrt(jnp.mean(values * values, axis=-1, keepdims=True) + epsilon)
+    scaled = grad * gain
+    centre = jnp.mean(scaled * values, axis=-1, keepdims=True)
+    back = inverse * scaled - values * (inverse * inverse * inverse * centre)
+    return back, jnp.sum(grad * values * inverse, axis=0, keepdims=True)
+
+
+class Layer:
+    def __init__(self, **refs):
+        self.__dict__.update(refs)
+        self.seq, self.width = self.x.shape
+        self.tile = 128
+        self.row_block = 128
+        self.shard_rows = self.bank.shape[3]
+
+    def unit(self, u, column=None, size=None):
+        if column is None:
+            block = self.bank[:, :, u]
+        else:
+            block = self.bank[:, :, u, :, lanes(column, size)]
+        return block.reshape(-1, block.shape[-1])
+
+    def row_chunks(self, body):
+        size = self.row_block
+        loop(self.seq // size, lambda n: body(rows_at(n * size, size)))
+
+    def small_arrays(self):
+        flat = self.all_small[...].reshape(-1, 128)
+        tile = self.tile
+        slot = lax.broadcasted_iota(jnp.int32, (flat.shape[0], 4 * tile), 1)
+        offset = jnp.where(slot < 3 * tile, slot - tile, slot - 5 * tile)
+        row = lax.broadcasted_iota(jnp.int32, (flat.shape[0], 4 * tile), 0)
+        per = NB // 8
+        inside = row % 16 - 2
+        wanted = jnp.where((inside >= 0) & (inside < per), (row // 16) * per + inside, -1)
+        hits = (bucket_of(offset) == wanted).astype(jnp.bfloat16)
+        self.rel[...] = dot_c(flat, hits)[: self.rel.shape[0]]
+        for index, ref in ((0, self.gain_a), (1, self.gain_f)):
+            total = jnp.zeros((1, self.width), jnp.float32)
+            for shard in range(8):
+                part = self.all_small[shard].astype(jnp.float32)[index : index + 1]
+                wide = jnp.concatenate(
+                    [part, jnp.zeros((1, self.width - 128), jnp.float32)], axis=1
+                )
+                total = total + (
+                    pltpu.roll(wide, shard * self.shard_rows, axis=1) if shard else wide
+                )
+            ref[...] = total
+
+    def norm_in(self):
+        gain = self.gain_a[...]
+
+        def body(r):
+            self.normed[r] = rms_norm(self.x[r].astype(jnp.float32), gain).astype(jnp.bfloat16)
+
+        self.row_chunks(body)
+
+    def mask_seed(self):
+        def body(r):
+            index = lax.broadcasted_iota(jnp.int32, (self.row_block, 1), 0) + r.start
+            live = index < self.length[0]
+            self.seed[r] = jnp.where(live, self.cot[r], jnp.bfloat16(0))
+
+        self.row_chunks(body)
+
+    def project(self, u):
+        def body(n):
+            self.qkv[u, :, lanes(n * 256, 256)] = dot(
+                self.normed[...], self.unit(u, n * 256, 256)
+            ).astype(jnp.bfloat16)
+
+        loop(self.width // 256, body)
+
+    def strip_for(self, head):
+        tile = self.tile
+        rel = self.rel[pl.ds(head, 1), :]
+        rolled = pltpu.roll(
+            jnp.broadcast_to(rel, (tile, 4 * tile)), 0, axis=1, stride=1, stride_axis=0
+        )
+        self.strip[:, 2 * tile : 5 * tile] = rolled[:, : 3 * tile]
+        self.strip[:, : 2 * tile] = jnp.broadcast_to(rel[:, :1], (tile, 2 * tile))
+        self.strip[:, 5 * tile :] = jnp.broadcast_to(
+            rel[:, 3 * tile - 1 : 3 * tile], (tile, 2 * tile)
+        )
+
+    def probs_store(self, pair, slot):
+        return pltpu.make_async_copy(
+            self.probs.at[slot], self.probs_far.at[pair], self.probs_sems.at[slot]
+        )
+
+    def probs_load(self, pair, slot):
+        return pltpu.make_async_copy(
+            self.probs_far.at[pair], self.probs.at[slot], self.probs_sems.at[slot]
+        )
+
+    def attend(self, pair):
+        tile, seq = self.tile, self.seq
+        slot = lax.rem(pair, 2)
+        pl.when(pair >= 2)(lambda: self.probs_store(pair, slot).wait())
+        lane = lax.broadcasted_iota(jnp.int32, (1, 128), 1)
+        key_at = lax.broadcasted_iota(jnp.int32, (1, seq), 1)
+        mask = jnp.where(key_at < self.length[0], 0.0, masked_score)
+        cols = lanes(pair * 128, 128)
+        k = self.qkv[1, :, cols]
+        v = self.qkv[2, :, cols]
+        for head in range(2):
+            mine = (lane >= 64) if head else (lane < 64)
+            self.strip_for(pair * 2 + head)
+            for block in range(seq // tile):
+                r = slice(block * tile, (block + 1) * tile)
+                q = jnp.where(mine, self.qkv[0, r, cols], jnp.bfloat16(0))
+                first = (seq // tile - 1 - block) * tile
+                scores = dot_t(q, k) + (self.strip[:, first : first + seq] + mask)
+                peak = jnp.max(scores, axis=-1, keepdims=True)
+                raised = jnp.exp(scores - peak)
+                total = jnp.sum(raised, axis=-1, keepdims=True)
+                probs = (raised * (1.0 / total)).astype(jnp.bfloat16)
+                self.probs[slot, head, r, :] = probs
+                out = dot(probs, v).astype(jnp.bfloat16)
+                if head:
+                    out = jnp.where(mine, out, self.attended[r, cols])
+                self.attended[r, cols] = out
+        self.probs_store(pair, slot).start()
+
+    def middle_rows(self):
+        def body(n):
+            c = lanes(n * 256, 256)
+            self.middle[:, c] = self.x[:, c].astype(jnp.float32) + dot(
+                self.attended[...], self.unit(3, n * 256, 256)
+            )
+
+        loop(self.width // 256, body)
+        gain = self.gain_f[...]
+
+        def norm(r):
+            self.normed_ffn[r] = rms_norm(self.middle[r], gain).astype(jnp.bfloat16)
+
+        self.row_chunks(norm)
+
+    def raise_unit(self, i):
+        def body(n):
+            raised = dot(self.normed_ffn[...], self.unit(4 + i, n * 256, 256))
+            active, slope = gelu_parts(raised)
+            c = lanes(i * self.width + n * 256, 256)
+            self.active[:, c] = active.astype(jnp.bfloat16)
+            self.slope[:, c] = slope.astype(jnp.bfloat16)
+
+        loop(self.width // 256, body)
+
+    def outer_grad(self, shard):
+        size = 4 * self.shard_rows
+        block = dot_c(self.active[:, lanes(shard * size, size)], self.seed[...])
+        self.bank[shard // 2, shard % 2, 12:16] = block.astype(jnp.bfloat16).reshape(
+            4, self.shard_rows, self.width
+        )
+
+    def lower(self):
+        def body(n):
+            outer = self.bank[:, :, 8:12, :, lanes(n * 256, 256)].reshape(-1, 256)
+            c = lanes(n * 256, 256)
+            self.block_out[:, c] = (self.middle[:, c] + dot(self.active[...], outer)).astype(
+                jnp.bfloat16
+            )
+
+        loop(self.width // 256, body)
+
+    def raised_grad(self, shard):
+        size = 4 * self.shard_rows
+        outer = self.bank[shard // 2, shard % 2, 8:12].reshape(size, self.width)
+        c = lanes(shard * size, size)
+        grad = dot_t(self.seed[...], outer) * self.slope[:, c].astype(jnp.float32)
+        self.slope[:, c] = grad.astype(jnp.bfloat16)
+
+    def inner_grad(self, i):
+        def body(n):
+            c = lanes(i * self.width + n * 256, 256)
+            block = dot_c(self.normed_ffn[...], self.slope[:, c]).astype(jnp.bfloat16)
+            self.bank[:, :, 16 + i, :, lanes(n * 256, 256)] = block.reshape(
+                4, 2, self.shard_rows, 256
+            )
+
+        loop(self.width // 256, body)
+
+    def middle_grad(self):
+        for part in range(2):
+            total = None
+            for i in range(4):
+                inner = self.bank[2 * part : 2 * part + 2, :, 4 + i]
+                inner = inner.reshape(-1, self.width)
+                term = dot_t(self.slope[:, i * self.width : (i + 1) * self.width], inner)
+                total = term if total is None else total + term
+            size = self.width // 2
+            self.grad_mid[:, part * size : (part + 1) * size] = total
+        gain = self.gain_f[...]
+        self.gain_f_grad[...] = jnp.zeros_like(self.gain_f_grad)
+
+        def body(r):
+            back, terms = norm_back(self.grad_mid[r], gain, self.middle[r])
+            total = self.seed[r].astype(jnp.float32) + back
+            self.gain_f_grad[...] += terms
+            self.grad_mid[r] = total
+            self.mid_low[r] = total.astype(jnp.bfloat16)
+
+        self.row_chunks(body)
+
+    def square_grad(self, left, right, slot):
+        def body(n):
+            block = dot_c(left[...], right(lanes(n * 256, 256))).astype(jnp.bfloat16)
+            self.bank[:, :, slot, :, lanes(n * 256, 256)] = block.reshape(
+                4, 2, self.shard_rows, 256
+            )
+
+        loop(self.width // 256, body)
+
+    def attended_grad(self):
+        size = self.width // 2
+        for part in range(2):
+            weight = self.bank[2 * part : 2 * part + 2, :, 3].reshape(size, self.width)
+            self.grad_att[:, part * size : (part + 1) * size] = dot_t(
+                self.mid_low[...], weight
+            ).astype(jnp.bfloat16)
+
+    def attend_back(self, pair):
+        tile, seq = self.tile, self.seq
+        slot = lax.rem(pair, 2)
+        self.probs_load(pair, slot).wait()
+        lane = lax.broadcasted_iota(jnp.int32, (1, 128), 1)
+        cols = lanes(pair * 128, 128)
+        k = self.qkv[1, :, cols]
+        v = self.qkv[2, :, cols]
+        blocks = seq // tile
+        grads = []
+        for head in range(2):
+            mine = (lane >= 64) if head else (lane < 64)
+            sums = [None] * 5
+            for block in range(blocks):
+                r = slice(block * tile, (block + 1) * tile)
+                grad_out = jnp.where(mine, self.grad_att[r, cols], jnp.bfloat16(0))
+                probs = self.probs[slot, head, r, :].astype(jnp.float32)
+                weighted = probs * dot_t(grad_out, v)
+                centre = jnp.sum(weighted, axis=-1, keepdims=True)
+                low = (weighted - probs * centre).astype(jnp.bfloat16)
+                self.grad_scores[r, :] = low
+                wide = low.astype(jnp.float32)
+                for other in range(blocks):
+                    apart = min(2, max(-2, other - block)) + 2
+                    part = wide[:, other * tile : (other + 1) * tile]
+                    sums[apart] = part if sums[apart] is None else sums[apart] + part
+                out = dot(low, k).astype(jnp.bfloat16)
+                if head:
+                    out = jnp.where(mine, out, self.grad_q[r, :])
+                self.grad_q[r, :] = out
+            zero = jnp.zeros((tile, tile), jnp.float32)
+            near = shear_sum(jnp.concatenate([sums[1], sums[2], sums[3], zero], axis=1), 4 * tile)
+            far = jnp.concatenate(
+                [
+                    jnp.zeros((1, 2 * tile), jnp.float32),
+                    jnp.sum(sums[4], axis=0, keepdims=True),
+                    jnp.sum(sums[0], axis=0, keepdims=True),
+                ],
+                axis=1,
+            )
+            self.rel_grad[pl.ds(pair * 2 + head, 1), :] = near + far
+            grads.append(
+                (
+                    dot_c(self.qkv[0, :, cols], self.grad_scores[...]).T,
+                    dot_c(self.grad_att[:, cols], self.probs[slot, head]).T,
+                )
+            )
+        first = lane < 64
+        self.qkv[0, :, cols] = self.grad_q[...]
+        self.qkv[1, :, cols] = jnp.where(first, grads[0][0], grads[1][0]).astype(jnp.bfloat16)
+        self.qkv[2, :, cols] = jnp.where(first, grads[0][1], grads[1][1]).astype(jnp.bfloat16)
+        pl.when(pair + 2 < self.probs_far.shape[0])(
+            lambda: self.probs_load(pair + 2, slot).start()
+        )
+
+    def input_grad(self):
+        size = self.width // 2
+        for part in range(2):
+            total = None
+            for u in range(3):
+                weight = self.bank[2 * part : 2 * part + 2, :, u].reshape(size, self.width)
+                term = dot_t(self.qkv[u], weight)
+                total = term if total is None else total + term
+            self.middle[:, part * size : (part + 1) * size] = total
+        gain = self.gain_a[...]
+        self.gain_a_grad[...] = jnp.zeros_like(self.gain_a_grad)
+
+        def body(r):
+            back, terms = norm_back(self.middle[r], gain, self.x[r].astype(jnp.float32))
+            self.gain_a_grad[...] += terms
+            self.grad_mid[r] += back
+
+        self.row_chunks(body)
+
+    def small_grads(self):
+        tile = self.tile
+        shape = (64, 4 * tile)
+        slot = lax.broadcasted_iota(jnp.int32, shape, 1)
+        offset = jnp.where(slot < 3 * tile, slot - tile, slot - 5 * tile)
+        row = lax.broadcasted_iota(jnp.int32, shape, 0)
+        per = NB // 8
+        inside = row % 8 - 2
+        wanted = jnp.where((inside >= 0) & (inside < per), (row // 8) * per + inside, -1)
+        hits = (bucket_of(offset) == wanted).astype(jnp.float32)
+        table = lax.dot_general(
+            hits,
+            self.rel_grad[...],
+            (((1,), (1,)), ((), ())),
+            precision=highest,
+            preferred_element_type=jnp.float32,
+        )
+        rows = lax.broadcasted_iota(jnp.int32, (8, 128), 0)
+        lane = lax.broadcasted_iota(jnp.int32, (8, 128), 1)
+        for shard in range(8):
+            block = table[8 * shard : 8 * shard + 8]
+            for index, ref in ((0, self.gain_a_grad), (1, self.gain_f_grad)):
+                wide = ref[...]
+                if shard:
+                    wide = pltpu.roll(wide, self.width - shard * self.shard_rows, axis=1)
+                here = (rows == index) & (lane < self.shard_rows)
+                block = jnp.where(here, jnp.broadcast_to(wide[:, :128], (8, 128)), block)
+            self.small_out[shard] = block
+
+
+def order_slot(n):
+    return jnp.where(n < 8, n + 12, jnp.where(n == 8, 7, n - 5))
+
+
+def fused_kernel(
+    length, x, cot, small, own, block_far, grad_far, own_far, small_result, probs_far,
+    bank, own_sum, from_core, from_y, from_x, from_z, all_small, small_out, small_in, small_rep,
+    probs, normed, qkv, attended, middle, normed_ffn, active, slope, seed, grad_mid, mid_low,
+    grad_att, block_out, rel, rel_grad, gain_a, gain_f, gain_a_grad, gain_f_grad, strip,
+    grad_scores, grad_q,
+    sends, recvs, sum_sends, sum_recvs, small_sends, small_recvs, back_sends, back_recvs,
+    rep_sends, rep_recvs, probs_sems, misc_sems, store_sems,
+):
+    shard = lax.axis_index("fsdp")
+    copy_id = lax.axis_index("rep")
+    layer = Layer(
+        length=length, x=x, cot=cot, bank=bank, all_small=all_small, small_out=small_out,
+        probs=probs, probs_far=probs_far, probs_sems=probs_sems, normed=normed, qkv=qkv,
+        attended=attended, middle=middle, normed_ffn=normed_ffn, active=active, slope=slope,
+        seed=seed, grad_mid=grad_mid, mid_low=mid_low, grad_att=grad_att, block_out=block_out,
+        rel=rel, rel_grad=rel_grad, gain_a=gain_a, gain_f=gain_f, gain_a_grad=gain_a_grad,
+        gain_f_grad=gain_f_grad, strip=strip, grad_scores=grad_scores, grad_q=grad_q,
+    )
+    units = own.shape[0]
+    gather = Gather(own, bank, sends, recvs)
+    scatter = Scatter(
+        order_slot, bank, own_sum, from_core, from_y, from_x, from_z, sum_sends, sum_recvs
+    )
+    pairs = probs_far.shape[0]
+
+    def remote(src, dst, send, recv, device):
+        return pltpu.make_async_remote_copy(
+            src_ref=src, dst_ref=dst, send_sem=send, recv_sem=recv, device_id=device,
+            device_id_type=MESH,
+        )
+
+    def peer(k):
+        return (lax.rem(shard + k, 8), copy_id)
+
+    def rep_peer(k):
+        return (shard, lax.rem(copy_id + k, 4))
+
+    greet()
+    small_copies = [
+        remote(small, all_small.at[shard], small_sends.at[k - 1], small_recvs.at[k - 1], peer(k))
+        for k in range(1, 8)
+    ]
+    for copy in small_copies:
+        copy.start()
+    keep = pltpu.make_async_copy(
+        own, bank.at[gather.z, gather.x, 0:units], misc_sems.at[0]
+    )
+    keep_small = pltpu.make_async_copy(small, all_small.at[shard], misc_sems.at[1])
+    keep.start()
+    keep_small.start()
+
+    stages = (
+        (gather.after_y, 6), (gather.after_x, 4), (gather.after_z, 2), (gather.start, 0),
+        (gather.after_core, 7),
+    )
+    schedule(stages, units)
+    keep.wait()
+    keep_small.wait()
+    for copy in small_copies:
+        copy.wait()
+    loop(units, gather.drain)
+
+    layer.small_arrays()
+    layer.mask_seed()
+    layer.norm_in()
+    loop(3, layer.project)
+    loop(pairs, layer.attend)
+    for pair in (pairs - 2, pairs - 1):
+        layer.probs_store(pair, pair % 2).wait()
+    layer.middle_rows()
+    loop(4, layer.raise_unit)
+    loop(8, layer.outer_grad)
+    layer.lower()
+    block_store = pltpu.make_async_copy(block_out, block_far, misc_sems.at[2])
+    block_store.start()
+    loop(8, layer.raised_grad)
+    loop(4, layer.inner_grad)
+    for pair in (0, 1):
+        layer.probs_load(pair, pair).start()
+    layer.middle_grad()
+    layer.square_grad(attended, lambda c: mid_low[:, c], 7)
+    layer.attended_grad()
+    rel_grad[...] = jnp.zeros_like(rel_grad)
+    loop(pairs, layer.attend_back)
+    for u in range(3):
+        layer.square_grad(normed, lambda c, u=u: qkv[u, :, c], 4 + u)
+    layer.input_grad()
+    grad_store = pltpu.make_async_copy(grad_mid, grad_far, misc_sems.at[3])
+    grad_store.start()
+    layer.small_grads()
+
+    back_copies = [
+        remote(
+            small_out.at[lax.rem(shard + k, 8)], small_in.at[k - 1], back_sends.at[k - 1],
+            back_recvs.at[k - 1], peer(k),
+        )
+        for k in range(1, 8)
+    ]
+    for copy in back_copies:
+        copy.start()
+
+    def store(n):
+        return pltpu.make_async_copy(own_sum.at[n], own_far.at[n], store_sems.at[n])
+
+    def last(n):
+        scatter.after_back_core(n)
+        store(n).start()
+
+    stages = (
+        (last, 9), (scatter.after_back_y, 8), (scatter.after_z, 7), (scatter.after_x, 5),
+        (scatter.after_y, 3), (scatter.after_core, 1), (scatter.start, 0),
+    )
+    schedule(stages, units)
+
+    total = small_out[shard]
+    for k, copy in enumerate(back_copies):
+        copy.wait_recv()
+        total = total + small_in[k]
+    small_rep[copy_id] = total
+    rep_copies = [
+        remote(
+            small_rep.at[copy_id], small_rep.at[copy_id], rep_sends.at[k - 1],
+            rep_recvs.at[k - 1], rep_peer(k),
+        )
+        for k in range(1, 4)
+    ]
+    for copy in rep_copies:
+        copy.start()
+    for k in range(1, 4):
+        there = small_rep.at[lax.rem(copy_id + 4 - k, 4)]
+        remote(there, there, rep_sends.at[k - 1], rep_recvs.at[k - 1], rep_peer(k)).wait_recv()
+    small_result[...] = (small_rep[0] + small_rep[1]) + (small_rep[2] + small_rep[3])
+
+    def drain(n):
+        scatter.drain(n)
+        store(n).wait()
+
+    loop(units, drain)
+    for copy in back_copies + rep_copies:
+        copy.wait_send()
+    block_store.wait()
+    grad_store.wait()
+
+
+def fused_call(length, x, cot, small, own, heads):
+    units, rows, width = own.shape
+    seq = x.shape[0]
+    half = rows // 2
+    part = half // 3
+    hidden = 4 * width
+    low, wide = jnp.bfloat16, jnp.float32
+    anywhere = pl.BlockSpec(memory_space=pl.ANY)
+    within = pl.BlockSpec(memory_space=pltpu.VMEM)
+    sems = pltpu.SemaphoreType.DMA
+    vm = pltpu.VMEM
+    head_rows = -(-heads // 8) * 8
+    return pl.pallas_call(
+        fused_kernel,
+        out_shape=(
+            jax.ShapeDtypeStruct((seq, width), low),
+            jax.ShapeDtypeStruct((seq, width), wide),
+            jax.ShapeDtypeStruct((units, rows, width), low),
+            jax.ShapeDtypeStruct((8, 128), wide),
+            jax.ShapeDtypeStruct((heads // 2, 2, seq, seq), low),
+        ),
+        in_specs=[pl.BlockSpec(memory_space=pltpu.SMEM), within, within, within, anywhere],
+        out_specs=[anywhere, anywhere, anywhere, within, anywhere],
+        scratch_shapes=[
+            vm((4, 2, units + 8, rows, width), low),
+            vm((units, rows, width), low),
+            vm((units, 4, 2, half, width), low),
+            vm((units, 4, 2, part, width), low),
+            vm((units, 4, 2 * part, width), low),
+            vm((units, 4, 2 * part, width), low),
+            vm((8, 16, 128), low),
+            vm((8, 8, 128), wide),
+            vm((7, 8, 128), wide),
+            vm((4, 8, 128), wide),
+            vm((2, 2, seq, seq), low),
+            vm((seq, width), low),
+            vm((3, seq, width), low),
+            vm((seq, width), low),
+            vm((seq, width), wide),
+            vm((seq, width), low),
+            vm((seq, hidden), low),
+            vm((seq, hidden), low),
+            vm((seq, width), low),
+            vm((seq, width), wide),
+            vm((seq, width), low),
+            vm((seq, width), low),
+            vm((seq, width), low),
+            vm((head_rows, 512), wide),
+            vm((128, 512), wide),
+            vm((1, width), wide),
+            vm((1, width), wide),
+            vm((1, width), wide),
+            vm((1, width), wide),
+            vm((128, 128 * 7), wide),
+            vm((seq, seq), low),
+            vm((seq, 128), low),
+            sems((units, Gather.slots)),
+            sems((units, Gather.slots)),
+            sems((units, Scatter.slots)),
+            sems((units, Scatter.slots)),
+            sems((7,)),
+            sems((7,)),
+            sems((7,)),
+            sems((7,)),
+            sems((3,)),
+            sems((3,)),
+            sems((2,)),
+            sems((4,)),
+            sems((units,)),
+        ],
+        compiler_params=pltpu.CompilerParams(
+            collective_id=0, has_side_effects=True, vmem_limit_bytes=63 * 2**20
+        ),
+    )(length, x, cot, small, own)
+
+
+def pack_small(gain_a, gain_f, table):
+    parts = (gain_a.reshape(1, -1), gain_f.reshape(1, -1), table)
+    block = jnp.concatenate(
+        [jnp.pad(part, ((0, 0), (0, 128 - part.shape[1]))) for part in parts]
+    )
+    return jnp.pad(block, ((0, 16 - block.shape[0]), (0, 0)))
+
+
+def local_linked(
+    inputs, lengths, cotangent, query_weight, key_weight, value_weight, output_weight,
+    attention_gain, bias_table, inner_weight, outer_weight, feedforward_gain,
+):
     rows, width = query_weight.shape
     chunks = inner_weight.shape[1] // width
-    inner_units = jnp.transpose(inner_weight.reshape(rows, chunks, width), (1, 0, 2))
-    outer_units = outer_weight.reshape(chunks, rows, width)
     own = jnp.concatenate(
         (
             jnp.stack((query_weight, key_weight, value_weight, output_weight)),
-            inner_units,
-            outer_units,
-        )
-    )
-    small = pack_small(attention_gain, feedforward_gain, bias_table, jnp.bfloat16, 16)
-    full, all_small = gather_call(own, small)
-    square = [full[:, :, u].reshape(8 * rows, width) for u in range(4)]
-    inner = jnp.concatenate(
-        [full[:, :, 4 + u].reshape(8 * rows, width) for u in range(chunks)], axis=1
-    )
-    outer = full[:, :, 4 + chunks :].reshape(8 * chunks * rows, width)
+            jnp.transpose(inner_weight.reshape(rows, chunks, width), (1, 0, 2)),
+            outer_weight.reshape(chunks, rows, width),
+        )
+    )
+    small = pack_small(attention_gain, feedforward_gain, bias_table)
     table_rows, heads = bias_table.shape
+    block_output, input_grad, sums, small_sum, _ = fused_call(
+        lengths, inputs[0], cotangent[0], small, own, heads
+    )
+    sums = sums.astype(jnp.float32)
     return (
-        *square,
-        all_small[:, 0, :rows].reshape(-1),
-        all_small[:, 2 : 2 + table_rows, :heads].reshape(8 * table_rows, heads),
-        inner,
-        outer,
-        all_small[:, 1, :rows].reshape(-1),
-    )
-
-
-def sum_linked(gradients):
-    query, key, value, output, gain, table, inner, outer, ffn_gain = gradients
-    width = query.shape[1]
-    rows = query.shape[0] // 8
-    chunks = inner.shape[1] // width
-    inner_units = jnp.transpose(inner.reshape(4, 2, rows, chunks, width), (0, 1, 3, 2, 4))
-    full = jnp.concatenate(
-        [part.reshape(4, 2, 1, rows, width).astype(jnp.bfloat16) for part in (query, key, value, output)]
-        + [
-            inner_units.astype(jnp.bfloat16),
-            outer.reshape(4, 2, chunks, rows, width).astype(jnp.bfloat16),
-        ],
-        axis=2,
-    )
-    table_rows = table.shape[0] // 8
-    heads = table.shape[1]
-    small = pack_small(
-        gain.reshape(8, rows), ffn_gain.reshape(8, rows), table.reshape(8, table_rows, heads),
-        jnp.float32, 8,
-    )
-    own, own_small = scatter_call(full, small)
-    own = own.astype(jnp.float32)
-    return (
-        own[0],
-        own[1],
-        own[2],
-        own[3],
-        own_small[0, :rows],
-        own_small[2 : 2 + table_rows, :heads],
-        jnp.transpose(own[4 : 4 + chunks], (1, 0, 2)).reshape(rows, chunks * width),
-        own[4 + chunks :].reshape(chunks * rows, width),
-        own_small[1, :rows],
-    )
-
-
-def local(linked, inputs, lengths, cotangent, query_weight, key_weight, value_weight,
-          output_weight, attention_gain, bias_table, inner_weight, outer_weight,
-          feedforward_gain):
-    gather, reduce = (gather_linked, sum_linked) if linked else (gather_all, sum_all)
-    weights = gather(
-        query_weight, key_weight, value_weight, output_weight, attention_gain, bias_table,
-        inner_weight, outer_weight, feedforward_gain,
-    )
-    block_output, input_grad, gradients = compute(inputs, lengths, cotangent, weights)
-    return (block_output, input_grad) + reduce(gradients)
+        block_output[None],
+        input_grad[None],
+        sums[9],
+        sums[10],
+        sums[11],
+        sums[8],
+        small_sum[0, :rows],
+        small_sum[2 : 2 + table_rows, :heads],
+        jnp.transpose(sums[4:8], (1, 0, 2)).reshape(rows, chunks * width),
+        sums[:4].reshape(chunks * rows, width),
+        small_sum[1, :rows],
+    )
+
+
+def local(inputs, lengths, cotangent, *shards):
+    block_output, input_grad, gradients = compute(inputs, lengths, cotangent, gather_all(*shards))
+    return (block_output, input_grad) + sum_all(gradients)
 
 
 def can_link(mesh):
@@ -811,7 +1149,7 @@
         P("fsdp"),
     )
     return jax.shard_map(
-        functools.partial(local, can_link(mesh)),
+        local_linked if can_link(mesh) else local,
         mesh=mesh,
         in_specs=placed,
         out_specs=(

time: 317 us -> 262 us (0.83)
  matrix products: 51.4 us -> 0 us
  Pallas kernels: 198 us -> 240 us
  local copies, waits for them, and re-layouts: 54.8 us -> 19 us
  other arithmetic: 9.19 us -> 1.03 us
    dot_general x14 -> x0, matrix products: 51.4 us -> none  [the longest x4 16.9 us: contract_cols(): lax.dot_general(left, right, (((1,), (1,)), ((), ())), preferred_element_...]
    pallas_call x4 -> x1, Pallas kernels: 198 us -> 240 us  [fused_call(): pl.pallas_call(fused_kernel, out_shape=(jax.ShapeDtypeStruct((seq, width)...]
    convert_element_type x4 -> x0, local copies, waits for them, and re-layouts: 14.7 us -> none  [the longest x1 9.86 us: sum_linked(): inner_units.astype(jnp.bfloat16)]
    unnamed x105 -> x16, local copies, waits for them, and re-layouts: 21.6 us -> 10.7 us
    slice x7 -> x2, local copies, waits for them, and re-layouts: 13.5 us -> 3.43 us  [the longest x1 2.17 us: local_linked(): sums[:4].reshape(chunks * rows, width)]
where the time goes in v3:
time: 262 us; the launch traced here: 261 us
  Pallas kernels  240 us (92%)
  local copies, waits for them, and re-layouts  19 us (7%)
    pallas_call x1, Pallas kernels, fused_call(): pl.pallas_call(fused_kernel, out_shape=(jax.ShapeDtypeStruct((seq, width)...  240 us
    unnamed x16, local copies, waits for them, and re-layouts  10.7 us

profile of v3, /device:TPU:1, one launch (start us, length us, event | category | flops | bytes accessed | tf_op | source)
XLA Modules:
  0.0 261.4 jit_solution(9826618959119776647)
XLA Ops:
  0.6 0.0 copy-start.3
  1.4 0.7 fusion.6
  2.1 0.6 pad.18.small
  2.7 1.6 bitcast_dynamic-update-slice_fusion.3
  4.3 1.6 bitcast_dynamic-update-slice_fusion.2
  5.9 1.6 bitcast_dynamic-update-slice_fusion.1
  7.4 1.6 bitcast_dynamic-update-slice_fusion
  9.0 2.0 fusion
  11.0 0.0 copy-done.3
  11.0 0.9 constant_dynamic-update-slice_fusion.own
  11.8 239.9 %shard_map.203 = (bf16[512,768]{1,0:T(8,128)(2,1)}, f32[512,768]{1,0:T(8,128)}, bf16[12,96,768]{2,1,0:T(8,128)(2,1)}, f32[8,128]{1,0:T(8,128)}, bf16[6,2,512,512]{3,2,1,0:T(8,128)(2,1)}) custom-call(s32[1]{0:T(128)S(6)} %copy.35.length, bf16[512,768]{1,0:T(8,128)(2,1)} %bitcast.45, bf16[512,768]{1,0:T(8,128)(2,1)} %bitcast.46, bf16[16,128]{1,0:T(8,128)(2,1)} %pad.18.small, ...), custom_call_target="tpu_custom_call" | custom-call | tf_op jit(solution)/shard_map/pallas_call | solution.py:1021
  251.7 0.0 copy-start
  251.8 1.3 slice_bitcast_fusion.5
  253.1 1.3 slice.32
  254.3 2.2 slice.41
  256.5 0.0 copy-done
  256.5 0.3 convert_element_type.10
  256.9 0.1 slice_bitcast_fusion
  257.0 1.0 slice_bitcast_fusion.1
  258.0 0.0 copy-start.2
  258.0 0.0 copy-start.1
  258.0 1.1 copy.26
  259.1 0.2 copy-done.2
  259.4 0.9 copy.36
  260.2 0.0 copy-done.1
  260.2 1.1 copy.37
Async XLA Ops:
  0.6 10.3 %copy-start.3 = (bf16[384,768]{1,0:T(8,128)(2,1)S(1)}, bf16[384,768]{1,0:T(8,128)(2,1)}, u32[]{:S(2)}) copy-start(bf16[384,768]{1,0:T(8,128)(2,1)} %param.22) | copy-start | bytes 1769476
  251.7 4.8 %copy-start = (bf16[12,96,768]{2,1,0:T(8,128)(2,1)S(1)}, bf16[12,96,768]{2,1,0:T(8,128)(2,1)}, u32[]{:S(2)}) copy-start(bf16[12,96,768]{2,1,0:T(8,128)(2,1)} %get-tuple-element.17) | copy-start | bytes 5308420
  258.0 1.4 copy-start.2
  258.0 2.2 copy-start.1

commit v4 on v3

--- a/solution.py
+++ b/solution.py
@@ -185,16 +185,17 @@
     pl.semaphore_wait(barrier, 10)
 
 
-def schedule(stages, count):
-    last = max(lag for _, lag in stages)
-
-    def step(t, carry):
+def stepper(stages, count):
+    def step(t):
         for stage, lag in stages:
             g = t - lag
-            pl.when((g >= 0) & (g < count))(functools.partial(stage, g))
-        return carry
-
-    lax.fori_loop(0, count + last, step, 0)
+            if isinstance(g, int):
+                if 0 <= g < count:
+                    stage(g)
+            else:
+                pl.when((g >= 0) & (g < count))(functools.partial(stage, g))
+
+    return step
 
 
 class Links:
@@ -243,9 +244,9 @@
 class Gather(Links):
     slots = 15
 
-    def __init__(self, own, full, send_sems, recv_sems):
-        super().__init__(own.shape[1], send_sems, recv_sems)
-        self.own, self.full = own, full
+    def __init__(self, full, send_sems, recv_sems):
+        super().__init__(full.shape[3], send_sems, recv_sems)
+        self.full = full
 
     def block(self, g, k, rows):
         return self.full.at[self.z_before(k), self.x, g, rows]
@@ -254,18 +255,12 @@
         return self.full.at[:, 1 - self.x, g, rows]
 
     def z_copy(self, g, k):
-        return self.copy(
-            self.own.at[g, self.plane],
-            self.full.at[self.z, self.x, g, self.plane],
-            g,
-            k - 1,
-            self.to_z(k),
-        )
+        part = self.block(g, 0, self.plane)
+        return self.copy(part, part, g, k - 1, self.to_z(k))
 
     def x_copy(self, g, k):
-        there = self.block(g, k, self.plane)
-        here = self.own.at[g, self.plane] if k == 0 else there
-        return self.copy(here, there, g, 3 + k, self.to_x())
+        part = self.block(g, k, self.plane)
+        return self.copy(part, part, g, 3 + k, self.to_x())
 
     def y_copy(self, g, k):
         rows = self.own_third
@@ -862,13 +857,15 @@
 
 
 def fused_kernel(
-    length, x, cot, small, own, block_far, grad_far, own_far, small_result, probs_far,
-    bank, own_sum, from_core, from_y, from_x, from_z, all_small, small_out, small_in, small_rep,
-    probs, normed, qkv, attended, middle, normed_ffn, active, slope, seed, grad_mid, mid_low,
-    grad_att, block_out, rel, rel_grad, gain_a, gain_f, gain_a_grad, gain_f_grad, strip,
-    grad_scores, grad_q,
+    length, x, cot, gain_a_own, gain_f_own, table_own, query_own, key_own, value_own, output_own,
+    inner_own, outer_own,
+    block_far, grad_far, own_far, small_result, probs_far,
+    bank, own_sum, from_core, from_y, from_x, from_z, small_wide, small, all_small, small_out,
+    small_in, small_rep, probs, normed, qkv, attended, middle, normed_ffn, active, slope, seed,
+    grad_mid, mid_low, grad_att, block_out, rel, rel_grad, gain_a, gain_f, gain_a_grad,
+    gain_f_grad, strip, grad_scores, grad_q,
     sends, recvs, sum_sends, sum_recvs, small_sends, small_recvs, back_sends, back_recvs,
-    rep_sends, rep_recvs, probs_sems, misc_sems, store_sems,
+    rep_sends, rep_recvs, probs_sems, misc_sems, store_sems, keep_sems,
 ):
     shard = lax.axis_index("fsdp")
     copy_id = lax.axis_index("rep")
@@ -880,8 +877,10 @@
         rel=rel, rel_grad=rel_grad, gain_a=gain_a, gain_f=gain_f, gain_a_grad=gain_a_grad,
         gain_f_grad=gain_f_grad, strip=strip, grad_scores=grad_scores, grad_q=grad_q,
     )
-    units = own.shape[0]
-    gather = Gather(own, bank, sends, recvs)
+    rows, width = query_own.shape
+    chunks = inner_own.shape[1] // width
+    units = 4 + 2 * chunks
+    gather = Gather(bank, sends, recvs)
     scatter = Scatter(
         order_slot, bank, own_sum, from_core, from_y, from_x, from_z, sum_sends, sum_recvs
     )
@@ -899,6 +898,24 @@
     def rep_peer(k):
         return (shard, lax.rem(copy_id + k, 4))
 
+    parts = [query_own, key_own, value_own, output_own]
+    parts += [inner_own.at[:, pl.ds(i * width, width)] for i in range(chunks)]
+    parts += [outer_own.at[pl.ds(i * rows, rows)] for i in range(chunks)]
+    keeps = [
+        pltpu.make_async_copy(part, bank.at[gather.z, gather.x, u], keep_sems.at[u])
+        for u, part in enumerate(parts)
+    ]
+    for copy in keeps:
+        copy.start()
+    small_wide[...] = jnp.zeros_like(small_wide)
+    small_wide[0:1, :rows] = gain_a_own[...].astype(jnp.float32)
+    small_wide[1:2, :rows] = gain_f_own[...].astype(jnp.float32)
+    per, heads = table_own.shape
+    small_wide[2 : 2 + per, :heads] = table_own[...].astype(jnp.float32)
+    small[...] = small_wide[...].astype(jnp.bfloat16)
+    all_small[shard] = small[...]
+    for copy in keeps:
+        copy.wait()
     greet()
     small_copies = [
         remote(small, all_small.at[shard], small_sends.at[k - 1], small_recvs.at[k - 1], peer(k))
@@ -906,53 +923,101 @@
     ]
     for copy in small_copies:
         copy.start()
-    keep = pltpu.make_async_copy(
-        own, bank.at[gather.z, gather.x, 0:units], misc_sems.at[0]
-    )
-    keep_small = pltpu.make_async_copy(small, all_small.at[shard], misc_sems.at[1])
-    keep.start()
-    keep_small.start()
-
-    stages = (
-        (gather.after_y, 6), (gather.after_x, 4), (gather.after_z, 2), (gather.start, 0),
-        (gather.after_core, 7),
-    )
-    schedule(stages, units)
-    keep.wait()
-    keep_small.wait()
+    gather_step = stepper(
+        (
+            (gather.after_y, 6), (gather.after_x, 4), (gather.after_z, 2), (gather.start, 0),
+            (gather.after_core, 7),
+        ),
+        units,
+    )
+    loop(2, gather_step)
+    layer.mask_seed()
     for copy in small_copies:
         copy.wait()
-    loop(units, gather.drain)
-
     layer.small_arrays()
-    layer.mask_seed()
     layer.norm_in()
-    loop(3, layer.project)
-    loop(pairs, layer.attend)
+
+    def early(n):
+        gather_step(n + 2)
+
+    loop(5, early)
+
+    def projects(u):
+        gather_step(u + 7)
+        layer.project(u)
+
+    loop(3, projects)
+
+    def attends(pair):
+        gather_step(pair + 10)
+        layer.attend(pair)
+
+    loop(pairs, attends)
+    layer.middle_rows()
+
+    def raises(i):
+        gather_step(i + 16)
+        layer.raise_unit(i)
+
+    loop(4, raises)
     for pair in (pairs - 2, pairs - 1):
         layer.probs_store(pair, pair % 2).wait()
-    layer.middle_rows()
-    loop(4, layer.raise_unit)
-    loop(8, layer.outer_grad)
-    layer.lower()
-    block_store = pltpu.make_async_copy(block_out, block_far, misc_sems.at[2])
-    block_store.start()
-    loop(8, layer.raised_grad)
-    loop(4, layer.inner_grad)
     for pair in (0, 1):
         layer.probs_load(pair, pair).start()
+    loop(8, layer.outer_grad)
+
+    def store(n):
+        return pltpu.make_async_copy(own_sum.at[n], own_far.at[n], store_sems.at[n])
+
+    def last(n):
+        scatter.after_back_core(n)
+        store(n).start()
+
+    sum_step = stepper(
+        (
+            (last, 9), (scatter.after_back_y, 8), (scatter.after_z, 7), (scatter.after_x, 5),
+            (scatter.after_y, 3), (scatter.after_core, 1), (scatter.start, 0),
+        ),
+        units,
+    )
+    sum_step(0)
+    layer.lower()
+    block_store = pltpu.make_async_copy(block_out, block_far, misc_sems.at[0])
+    block_store.start()
+    sum_step(1)
+    loop(8, layer.raised_grad)
+    sum_step(2)
+
+    def inners(i):
+        layer.inner_grad(2 * i)
+        layer.inner_grad(2 * i + 1)
+        sum_step(i + 3)
+        gather.drain(4 + 2 * i)
+        gather.drain(5 + 2 * i)
+
+    loop(2, inners)
     layer.middle_grad()
     layer.square_grad(attended, lambda c: mid_low[:, c], 7)
     layer.attended_grad()
     rel_grad[...] = jnp.zeros_like(rel_grad)
-    loop(pairs, layer.attend_back)
-    for u in range(3):
-        layer.square_grad(normed, lambda c, u=u: qkv[u, :, c], 4 + u)
+
+    def attend_backs(n):
+        sum_step(n + 5)
+        layer.attend_back(2 * n)
+        layer.attend_back(2 * n + 1)
+
+    loop(pairs // 2, attend_backs)
+    sum_step(8)
+
+    def square_grads(u):
+        layer.square_grad(normed, lambda c: qkv[u, :, c], 4 + u)
+        sum_step(u + 9)
+
+    loop(3, square_grads)
     layer.input_grad()
-    grad_store = pltpu.make_async_copy(grad_mid, grad_far, misc_sems.at[3])
+    grad_store = pltpu.make_async_copy(grad_mid, grad_far, misc_sems.at[1])
     grad_store.start()
     layer.small_grads()
-
     back_copies = [
         remote(
             small_out.at[lax.rem(shard + k, 8)], small_in.at[k - 1], back_sends.at[k - 1],
@@ -962,20 +1027,13 @@
     ]
     for copy in back_copies:
         copy.start()
-
-    def store(n):
-        return pltpu.make_async_copy(own_sum.at[n], own_far.at[n], store_sems.at[n])
-
-    def last(n):
-        scatter.after_back_core(n)
-        store(n).start()
-
-    stages = (
-        (last, 9), (scatter.after_back_y, 8), (scatter.after_z, 7), (scatter.after_x, 5),
-        (scatter.after_y, 3), (scatter.after_core, 1), (scatter.start, 0),
-    )
-    schedule(stages, units)
-
+    loop(4, gather.drain)
+    loop(units - 8, lambda n: gather.drain(n + 8))
+
+    def late(n):
+        sum_step(n + 12)
+
+    loop(5, late)
     total = small_out[shard]
     for k, copy in enumerate(back_copies):
         copy.wait_recv()
@@ -990,6 +1048,11 @@
     ]
     for copy in rep_copies:
         copy.start()
+
+    def later(n):
+        sum_step(n + 17)
+
+    loop(4, later)
     for k in range(1, 4):
         there = small_rep.at[lax.rem(copy_id + 4 - k, 4)]
         remote(there, there, rep_sends.at[k - 1], rep_recvs.at[k - 1], rep_peer(k)).wait_recv()
@@ -1006,12 +1069,14 @@
     grad_store.wait()
 
 
-def fused_call(length, x, cot, small, own, heads):
-    units, rows, width = own.shape
+def fused_call(length, x, cot, gain_a, gain_f, table, square, inner, outer):
+    rows, width = square[0].shape
+    units = 4 + 2 * (inner.shape[1] // width)
+    heads = table.shape[1]
     seq = x.shape[0]
     half = rows // 2
     part = half // 3
-    hidden = 4 * width
+    hidden = inner.shape[1]
     low, wide = jnp.bfloat16, jnp.float32
     anywhere = pl.BlockSpec(memory_space=pl.ANY)
     within = pl.BlockSpec(memory_space=pltpu.VMEM)
@@ -1027,7 +1092,7 @@
             jax.ShapeDtypeStruct((8, 128), wide),
             jax.ShapeDtypeStruct((heads // 2, 2, seq, seq), low),
         ),
-        in_specs=[pl.BlockSpec(memory_space=pltpu.SMEM), within, within, within, anywhere],
+        in_specs=[pl.BlockSpec(memory_space=pltpu.SMEM)] + [within] * 5 + [anywhere] * 6,
         out_specs=[anywhere, anywhere, anywhere, within, anywhere],
         scratch_shapes=[
             vm((4, 2, units + 8, rows, width), low),
@@ -1036,6 +1101,8 @@
             vm((units, 4, 2, part, width), low),
             vm((units, 4, 2 * part, width), low),
             vm((units, 4, 2 * part, width), low),
+            vm((16, 128), wide),
+            vm((16, 128), low),
             vm((8, 16, 128), low),
             vm((8, 8, 128), wide),
             vm((7, 8, 128), wide),
@@ -1073,54 +1140,76 @@
             sems((3,)),
             sems((3,)),
             sems((2,)),
-            sems((4,)),
+            sems((2,)),
+            sems((units,)),
             sems((units,)),
         ],
         compiler_params=pltpu.CompilerParams(
             collective_id=0, has_side_effects=True, vmem_limit_bytes=63 * 2**20
         ),
-    )(length, x, cot, small, own)
-
-
-def pack_small(gain_a, gain_f, table):
-    parts = (gain_a.reshape(1, -1), gain_f.reshape(1, -1), table)
-    block = jnp.concatenate(
-        [jnp.pad(part, ((0, 0), (0, 128 - part.shape[1]))) for part in parts]
-    )
-    return jnp.pad(block, ((0, 16 - block.shape[0]), (0, 0)))
+    )(length, x, cot, gain_a, gain_f, table, *square, inner, outer)
+
+
+def finish_kernel(
+    block_in, grad_in, sums, small, block_out, grad_out, query, key, value, output, gain_a, table,
+    inner, outer, gain_f, sems,
+):
+    copies = [
+        pltpu.make_async_copy(block_in, block_out, sems.at[0]),
+        pltpu.make_async_copy(grad_in, grad_out, sems.at[1]),
+    ]
+    for copy in copies:
+        copy.start()
+    rows, width = query.shape
+    chunks = inner.shape[1] // width
+    for i in range(chunks):
+        outer[i * rows : (i + 1) * rows, :] = sums[i].astype(jnp.float32)
+        inner[:, i * width : (i + 1) * width] = sums[chunks + i].astype(jnp.float32)
+    for n, ref in enumerate((output, query, key, value)):
+        ref[...] = sums[2 * chunks + n].astype(jnp.float32)
+    gain_a[...] = small[0:1, :rows]
+    gain_f[...] = small[1:2, :rows]
+    table[...] = small[2 : 2 + table.shape[0], : table.shape[1]]
+    for copy in copies:
+        copy.wait()
+
+
+def finish_call(block, grad, sums, small, table_shape, inner_shape, outer_shape):
+    rows, width = sums.shape[1:]
+    wide = jnp.float32
+    anywhere = pl.BlockSpec(memory_space=pl.ANY)
+    within = pl.BlockSpec(memory_space=pltpu.VMEM)
+    shapes = [(rows, width)] * 4 + [(1, rows), table_shape, inner_shape, outer_shape, (1, rows)]
+    return pl.pallas_call(
+        finish_kernel,
+        out_shape=[
+            jax.ShapeDtypeStruct(block.shape, block.dtype),
+            jax.ShapeDtypeStruct(grad.shape, grad.dtype),
+        ]
+        + [jax.ShapeDtypeStruct(shape, wide) for shape in shapes],
+        in_specs=[anywhere, anywhere, within, within],
+        out_specs=[anywhere, anywhere] + [within] * len(shapes),
+        scratch_shapes=[pltpu.SemaphoreType.DMA((2,))],
+        compiler_params=pltpu.CompilerParams(vmem_limit_bytes=32 * 2**20),
+    )(block, grad, sums, small)
 
 
 def local_linked(
     inputs, lengths, cotangent, query_weight, key_weight, value_weight, output_weight,
     attention_gain, bias_table, inner_weight, outer_weight, feedforward_gain,
 ):
-    rows, width = query_weight.shape
-    chunks = inner_weight.shape[1] // width
-    own = jnp.concatenate(
-        (
-            jnp.stack((query_weight, key_weight, value_weight, output_weight)),
-            jnp.transpose(inner_weight.reshape(rows, chunks, width), (1, 0, 2)),
-            outer_weight.reshape(chunks, rows, width),
-        )
-    )
-    small = pack_small(attention_gain, feedforward_gain, bias_table)
-    table_rows, heads = bias_table.shape
-    block_output, input_grad, sums, small_sum, _ = fused_call(
-        lengths, inputs[0], cotangent[0], small, own, heads
-    )
-    sums = sums.astype(jnp.float32)
+    rows = query_weight.shape[0]
+    square = (query_weight, key_weight, value_weight, output_weight)
+    block, grad, sums, small, _ = fused_call(
+        lengths, inputs[0], cotangent[0], attention_gain.reshape(1, rows),
+        feedforward_gain.reshape(1, rows), bias_table, square, inner_weight, outer_weight,
+    )
+    block, grad, query, key, value, output, gain_a, table, inner, outer, gain_f = finish_call(
+        block, grad, sums, small, bias_table.shape, inner_weight.shape, outer_weight.shape
+    )
     return (
-        block_output[None],
-        input_grad[None],
-        sums[9],
-        sums[10],
-        sums[11],
-        sums[8],
-        small_sum[0, :rows],
-        small_sum[2 : 2 + table_rows, :heads],
-        jnp.transpose(sums[4:8], (1, 0, 2)).reshape(rows, chunks * width),
-        sums[:4].reshape(chunks * rows, width),
-        small_sum[1, :rows],
+        block[None], grad[None], query, key, value, output, gain_a.reshape(rows), table, inner,
+        outer, gain_f.reshape(rows),
     )
 
 

time: 262 us -> 189 us (0.72)
  Pallas kernels: 240 us -> 181 us
  local copies, waits for them, and re-layouts: 19 us -> 4.68 us
    pallas_call x1, Pallas kernels: 240 us -> 178 us  [fused_call(): pl.pallas_call(fused_kernel, out_shape=(jax.ShapeDtypeStruct((seq, width)...]
    unnamed x16 -> x8, local copies, waits for them, and re-layouts: 10.7 us -> 4.68 us
    slice x2 -> x0, local copies, waits for them, and re-layouts: 3.43 us -> none  [the longest x1 2.17 us: local_linked(): sums[:4].reshape(chunks * rows, width)]
    pallas_call x0 -> x1, Pallas kernels: none -> 3.22 us  [finish_call(): pl.pallas_call(finish_kernel, out_shape=[jax.ShapeDtypeStruct(block.shape...]
where the time goes in v4:
time: 189 us; the launch traced here: 188 us
  Pallas kernels  181 us (96%)
  local copies, waits for them, and re-layouts  4.68 us (2%)
    pallas_call x1, Pallas kernels, fused_call(): pl.pallas_call(fused_kernel, out_shape=(jax.ShapeDtypeStruct((seq, width)...  178 us
    unnamed x8, local copies, waits for them, and re-layouts  4.68 us

profile of v4, /device:TPU:1, one launch (start us, length us, event | category | flops | bytes accessed | tf_op | source)
XLA Modules:
  0.0 187.6 jit_solution(3973433503412203891)
XLA Ops:
  1.3 178.2 %shard_map.203 = (bf16[512,768]{1,0:T(8,128)(2,1)}, f32[512,768]{1,0:T(8,128)}, bf16[12,96,768]{2,1,0:T(8,128)(2,1)}, f32[8,128]{1,0:T(8,128)}, bf16[6,2,512,512]{3,2,1,0:T(8,128)(2,1)}) custom-call(s32[1]{0:T(128)S(6)} %copy.23.length, bf16[512,768]{1,0:T(8,128)(2,1)} %bitcast.8, bf16[512,768]{1,0:T(8,128)(2,1)} %bitcast.9, bf16[1,96]{1,0:T(2,128)(2,1)} %bitcast.10, ...), custom_call_target="tpu_custom_call" | custom-call | tf_op jit(solution)/shard_map/pallas_call | solution.py:1086
  179.5 0.0 copy-start
  179.5 1.5 copy-done
  181.0 0.0 copy-start.1
  181.0 1.4 copy-done.1
  182.4 0.0 copy-start.2
  182.4 1.1 copy-done.2
  183.5 0.0 copy-start.3
  183.5 0.7 copy-done.3
  184.2 3.2 %shard_map.204 = (bf16[512,768]{1,0:T(8,128)(2,1)}, f32[512,768]{1,0:T(8,128)}, f32[96,768]{1,0:T(8,128)}, f32[96,768]{1,0:T(8,128)}, f32[96,768]{1,0:T(8,128)},...) custom-call(bf16[512,768]{1,0:T(8,128)(2,1)S(1)} %copy-done.2, ...), custom_call_target="tpu_custom_call" | custom-call | tf_op jit(solution)/shard_map/pallas_call | solution.py:1183
Async XLA Ops:
  179.5 1.5 copy-start
  181.0 1.4 copy-start.1
  182.4 1.1 copy-start.2
  183.5 0.7 copy-start.3

commit v5 on v4

--- a/solution.py
+++ b/solution.py
@@ -242,76 +242,115 @@
 
 
 class Gather(Links):
-    slots = 15
+    slots = 20
 
     def __init__(self, full, send_sems, recv_sems):
         super().__init__(full.shape[3], send_sems, recv_sems)
         self.full = full
-
-    def block(self, g, k, rows):
-        return self.full.at[self.z_before(k), self.x, g, rows]
+        self.beside = self.z + 1 - 2 * lax.rem(self.z, 2)
+        self.second = lax.rem(self.z + 2, 4)
+        self.across = 3 - self.z
+        self.at_end = (self.z == 0) | (self.z == 3)
+
+    def block(self, g, a, rows):
+        return self.full.at[a, self.x, g, rows]
 
     def column(self, g, rows):
         return self.full.at[:, 1 - self.x, g, rows]
 
-    def z_copy(self, g, k):
-        part = self.block(g, 0, self.plane)
-        return self.copy(part, part, g, k - 1, self.to_z(k))
-
-    def x_copy(self, g, k):
-        part = self.block(g, k, self.plane)
-        return self.copy(part, part, g, 3 + k, self.to_x())
-
-    def y_copy(self, g, k):
-        rows = self.own_third
-        part = self.block(g, k, rows) if k < 4 else self.column(g, rows)
-        return self.copy(part, part, g, 6 + k, self.to_y())
-
-    def core_copy(self, g, k):
-        part = self.block(g, k, self.half) if k < 4 else self.column(g, self.half)
-        return self.copy(part, part, g, 10 + k, self.to_core())
-
-    def arrived(self, part, g, slot, device):
-        self.copy(part, part, g, slot, device).wait_recv()
+    def move(self, part, g, send_slot, recv_slot, device):
+        return pltpu.make_async_remote_copy(
+            src_ref=part,
+            dst_ref=part,
+            send_sem=self.send_sems.at[g, send_slot],
+            recv_sem=self.recv_sems.at[g, recv_slot],
+            device_id=device,
+            device_id_type=MESH,
+        )
+
+    def at_z(self, a):
+        return (a * 2 + self.x, self.y * 2 + self.c)
+
+    def z_copy(self, g, to):
+        return self.move(self.block(g, self.z, self.plane), g, to, self.z, self.at_z(to))
+
+    def pass_copy(self, g):
+        return self.move(
+            self.block(g, self.second, self.plane), g, self.z, self.second, self.at_z(self.beside)
+        )
+
+    def x_copy(self, g, a):
+        return self.move(self.block(g, a, self.plane), g, 4 + a, 4 + a, self.to_x())
+
+    def y_copy(self, g, a):
+        return self.move(self.block(g, a, self.own_third), g, 8 + a, 8 + a, self.to_y())
+
+    def y_column_copy(self, g):
+        return self.move(self.column(g, self.own_third), g, 12, 12, self.to_y())
+
+    def core_copy(self, g, a):
+        return self.move(self.block(g, a, self.half), g, 13 + a, 13 + a, self.to_core())
+
+    def core_column_copy(self, g):
+        return self.move(self.column(g, self.half), g, 17, 17, self.to_core())
+
+    def arrived(self, part, g, slot):
+        self.move(part, g, slot, slot, self.to_x()).wait_recv()
+
+    def others(self):
+        return (self.beside, self.second, self.across)
 
     def start(self, g):
-        self.x_copy(g, 0).start()
-        for k in (1, 2, 3):
-            self.z_copy(g, k).start()
+        self.z_copy(g, self.second).start()
+        self.z_copy(g, self.beside).start()
+        pl.when(~self.at_end)(lambda: self.z_copy(g, self.across).start())
+        self.x_copy(g, self.z).start()
+
+    def spread(self, g, a):
+        self.arrived(self.block(g, a, self.plane), g, a)
+        self.x_copy(g, a).start()
+        self.y_copy(g, a).start()
 
     def after_z(self, g):
-        for k in (1, 2, 3):
-            self.arrived(self.block(g, k, self.plane), g, k - 1, self.to_z(k))
-            self.x_copy(g, k).start()
-            self.y_copy(g, k).start()
+        self.arrived(self.block(g, self.second, self.plane), g, self.second)
+        pl.when(~self.at_end)(lambda: self.pass_copy(g).start())
+        self.x_copy(g, self.second).start()
+        self.y_copy(g, self.second).start()
+        self.spread(g, self.beside)
+        pl.when(~self.at_end)(lambda: self.spread(g, self.across))
+
+    def after_pass(self, g):
+        pl.when(self.at_end)(lambda: self.spread(g, self.across))
 
     def after_x(self, g):
-        for k in range(4):
-            part = self.full.at[self.z_before(k), 1 - self.x, g, self.plane]
-            self.arrived(part, g, 3 + k, self.to_x())
-        self.y_copy(g, 4).start()
+        for a in range(4):
+            self.arrived(self.full.at[a, 1 - self.x, g, self.plane], g, 4 + a)
+        self.y_column_copy(g).start()
 
     def after_y(self, g):
-        for k in (1, 2, 3):
-            self.arrived(self.block(g, k, self.other_third), g, 6 + k, self.to_y())
-            self.core_copy(g, k).start()
-        self.arrived(self.column(g, self.other_third), g, 10, self.to_y())
-        self.core_copy(g, 4).start()
+        for a in self.others():
+            self.arrived(self.block(g, a, self.other_third), g, 8 + a)
+            self.core_copy(g, a).start()
+        self.arrived(self.column(g, self.other_third), g, 12)
+        self.core_column_copy(g).start()
 
     def after_core(self, g):
-        for k in (1, 2, 3):
-            self.arrived(self.block(g, k, self.other_half), g, 10 + k, self.to_core())
-        self.arrived(self.column(g, self.other_half), g, 14, self.to_core())
+        for a in self.others():
+            self.arrived(self.block(g, a, self.other_half), g, 13 + a)
+        self.arrived(self.column(g, self.other_half), g, 17)
 
     def drain(self, g):
-        self.x_copy(g, 0).wait_send()
-        for k in (1, 2, 3):
-            self.z_copy(g, k).wait_send()
-            self.x_copy(g, k).wait_send()
-            self.y_copy(g, k).wait_send()
-            self.core_copy(g, k).wait_send()
-        self.y_copy(g, 4).wait_send()
-        self.core_copy(g, 4).wait_send()
+        self.z_copy(g, self.second).wait_send()
+        self.z_copy(g, self.beside).wait_send()
+        pl.when(~self.at_end)(lambda: self.z_copy(g, self.across).wait_send())
+        pl.when(~self.at_end)(lambda: self.pass_copy(g).wait_send())
+        for a in range(4):
+            self.x_copy(g, a).wait_send()
+        for a in self.others():
+            self.y_copy(g, a).wait_send()
+            self.core_copy(g, a).wait_send()
+        self.y_column_copy(g).wait_send()
+        self.core_column_copy(g).wait_send()
 
 
 class Scatter(Links):
@@ -324,7 +363,8 @@
 
     def core_copy(self, g):
         part = self.full.at[:, :, self.slot(g), self.other_half]
-        return self.copy(part, self.from_core.at[g], g, 0, self.to_core())
+        ring = lax.rem(g, self.from_core.shape[0])
+        return self.copy(part, self.from_core.at[ring], g, 0, self.to_core())
 
     def y_copy(self, g):
         part = self.full.at[:, :, self.slot(g), self.other_third]
@@ -351,9 +391,10 @@
 
     def after_core(self, g):
         self.core_copy(g).wait_recv()
+        ring = lax.rem(g, self.from_core.shape[0])
         for a in range(4):
             for b in range(2):
-                self.full[a, b, self.slot(g), self.half] += self.from_core[g, a, b]
+                self.full[a, b, self.slot(g), self.half] += self.from_core[ring, a, b]
         self.y_copy(g).start()
 
     def after_y(self, g):
@@ -587,7 +628,7 @@
         def body(r):
             index = lax.broadcasted_iota(jnp.int32, (self.row_block, 1), 0) + r.start
             live = index < self.length[0]
-            self.seed[r] = jnp.where(live, self.cot[r], jnp.bfloat16(0))
+            self.seed[r] = jnp.where(live, self.seed[r], jnp.bfloat16(0))
 
         self.row_chunks(body)
 
@@ -599,17 +640,20 @@
 
         loop(self.width // 256, body)
 
-    def strip_for(self, head):
+    def strip_for(self, head, strip):
         tile = self.tile
         rel = self.rel[pl.ds(head, 1), :]
         rolled = pltpu.roll(
             jnp.broadcast_to(rel, (tile, 4 * tile)), 0, axis=1, stride=1, stride_axis=0
         )
-        self.strip[:, 2 * tile : 5 * tile] = rolled[:, : 3 * tile]
-        self.strip[:, : 2 * tile] = jnp.broadcast_to(rel[:, :1], (tile, 2 * tile))
-        self.strip[:, 5 * tile :] = jnp.broadcast_to(
-            rel[:, 3 * tile - 1 : 3 * tile], (tile, 2 * tile)
-        )
+        strip[:, 2 * tile : 5 * tile] = rolled[:, : 3 * tile]
+        strip[:, : 2 * tile] = jnp.broadcast_to(rel[:, :1], (tile, 2 * tile))
+        strip[:, 5 * tile :] = jnp.broadcast_to(rel[:, 3 * tile - 1 : 3 * tile], (tile, 2 * tile))
+
+    def pair_lanes(self, pair):
+        third = self.width // 3
+        first = lax.rem(pair, 2) * 128
+        return pair // 2, [lanes(first + n * third, 128) for n in range(3)]
 
     def probs_store(self, pair, slot):
         return pltpu.make_async_copy(
@@ -626,28 +670,31 @@
         slot = lax.rem(pair, 2)
         pl.when(pair >= 2)(lambda: self.probs_store(pair, slot).wait())
         lane = lax.broadcasted_iota(jnp.int32, (1, 128), 1)
+        own = (lane < 64, lane >= 64)
         key_at = lax.broadcasted_iota(jnp.int32, (1, seq), 1)
         mask = jnp.where(key_at < self.length[0], 0.0, masked_score)
-        cols = lanes(pair * 128, 128)
-        k = self.qkv[1, :, cols]
-        v = self.qkv[2, :, cols]
+        unit, (q_at, k_at, v_at) = self.pair_lanes(pair)
+        q = self.qkv[unit, :, q_at]
+        k = self.qkv[unit, :, k_at]
+        v = self.qkv[unit, :, v_at]
         for head in range(2):
-            mine = (lane >= 64) if head else (lane < 64)
-            self.strip_for(pair * 2 + head)
+            self.strip_for(pair * 2 + head, self.strip.at[head])
+            self.scores[head] = dot_t(jnp.where(own[head], q, jnp.bfloat16(0)), k)
+
+        def soften(head):
             for block in range(seq // tile):
                 r = slice(block * tile, (block + 1) * tile)
-                q = jnp.where(mine, self.qkv[0, r, cols], jnp.bfloat16(0))
                 first = (seq // tile - 1 - block) * tile
-                scores = dot_t(q, k) + (self.strip[:, first : first + seq] + mask)
+                bias = self.strip[head, :, first : first + seq]
+                scores = self.scores[head, r, :] + (bias + mask)
                 peak = jnp.max(scores, axis=-1, keepdims=True)
                 raised = jnp.exp(scores - peak)
                 total = jnp.sum(raised, axis=-1, keepdims=True)
-                probs = (raised * (1.0 / total)).astype(jnp.bfloat16)
-                self.probs[slot, head, r, :] = probs
-                out = dot(probs, v).astype(jnp.bfloat16)
-                if head:
-                    out = jnp.where(mine, out, self.attended[r, cols])
-                self.attended[r, cols] = out
+                self.probs[slot, head, r, :] = (raised * (1.0 / total)).astype(jnp.bfloat16)
+            return dot(self.probs[slot, head], v)
+
+        outs = [soften(head) for head in range(2)]
+        self.attended[:, lanes(pair * 128, 128)] = jnp.where(own[0], *outs).astype(jnp.bfloat16)
         self.probs_store(pair, slot).start()
 
     def middle_rows(self):
@@ -686,7 +733,7 @@
         def body(n):
             outer = self.bank[:, :, 8:12, :, lanes(n * 256, 256)].reshape(-1, 256)
             c = lanes(n * 256, 256)
-            self.block_out[:, c] = (self.middle[:, c] + dot(self.active[...], outer)).astype(
+            self.mid_low[:, c] = (self.middle[:, c] + dot(self.active[...], outer)).astype(
                 jnp.bfloat16
             )
 
@@ -744,7 +791,7 @@
         size = self.width // 2
         for part in range(2):
             weight = self.bank[2 * part : 2 * part + 2, :, 3].reshape(size, self.width)
-            self.grad_att[:, part * size : (part + 1) * size] = dot_t(
+            self.attended[:, part * size : (part + 1) * size] = dot_t(
                 self.mid_low[...], weight
             ).astype(jnp.bfloat16)
 
@@ -753,31 +800,29 @@
         slot = lax.rem(pair, 2)
         self.probs_load(pair, slot).wait()
         lane = lax.broadcasted_iota(jnp.int32, (1, 128), 1)
-        cols = lanes(pair * 128, 128)
-        k = self.qkv[1, :, cols]
-        v = self.qkv[2, :, cols]
+        own = (lane < 64, lane >= 64)
+        unit, (q_at, k_at, v_at) = self.pair_lanes(pair)
+        q = self.qkv[unit, :, q_at]
+        k = self.qkv[unit, :, k_at]
+        v = self.qkv[unit, :, v_at]
+        grad_out = self.attended[:, lanes(pair * 128, 128)]
         blocks = seq // tile
-        grads = []
         for head in range(2):
-            mine = (lane >= 64) if head else (lane < 64)
+            self.scores[head] = dot_t(jnp.where(own[head], grad_out, jnp.bfloat16(0)), v)
+
+        def back(head):
             sums = [None] * 5
             for block in range(blocks):
                 r = slice(block * tile, (block + 1) * tile)
-                grad_out = jnp.where(mine, self.grad_att[r, cols], jnp.bfloat16(0))
                 probs = self.probs[slot, head, r, :].astype(jnp.float32)
-                weighted = probs * dot_t(grad_out, v)
+                weighted = probs * self.scores[head, r, :]
                 centre = jnp.sum(weighted, axis=-1, keepdims=True)
-                low = (weighted - probs * centre).astype(jnp.bfloat16)
-                self.grad_scores[r, :] = low
-                wide = low.astype(jnp.float32)
+                grad = weighted - probs * centre
+                self.grad_scores[head, r, :] = grad.astype(jnp.bfloat16)
                 for other in range(blocks):
                     apart = min(2, max(-2, other - block)) + 2
-                    part = wide[:, other * tile : (other + 1) * tile]
+                    part = grad[:, other * tile : (other + 1) * tile]
                     sums[apart] = part if sums[apart] is None else sums[apart] + part
-                out = dot(low, k).astype(jnp.bfloat16)
-                if head:
-                    out = jnp.where(mine, out, self.grad_q[r, :])
-                self.grad_q[r, :] = out
             zero = jnp.zeros((tile, tile), jnp.float32)
             near = shear_sum(jnp.concatenate([sums[1], sums[2], sums[3], zero], axis=1), 4 * tile)
             far = jnp.concatenate(
@@ -789,16 +834,14 @@
                 axis=1,
             )
             self.rel_grad[pl.ds(pair * 2 + head, 1), :] = near + far
-            grads.append(
-                (
-                    dot_c(self.qkv[0, :, cols], self.grad_scores[...]).T,
-                    dot_c(self.grad_att[:, cols], self.probs[slot, head]).T,
-                )
+            return (
+                dot(self.grad_scores[head], k),
+                dot_c(q, self.grad_scores[head]).T,
+                dot_c(grad_out, self.probs[slot, head]).T,
             )
-        first = lane < 64
-        self.qkv[0, :, cols] = self.grad_q[...]
-        self.qkv[1, :, cols] = jnp.where(first, grads[0][0], grads[1][0]).astype(jnp.bfloat16)
-        self.qkv[2, :, cols] = jnp.where(first, grads[0][1], grads[1][1]).astype(jnp.bfloat16)
+
+        for at, first, second in zip((q_at, k_at, v_at), back(0), back(1)):
+            self.qkv[unit, :, at] = jnp.where(own[0], first, second).astype(jnp.bfloat16)
         pl.when(pair + 2 < self.probs_far.shape[0])(
             lambda: self.probs_load(pair + 2, slot).start()
         )
@@ -862,20 +905,20 @@
     block_far, grad_far, own_far, small_result, probs_far,
     bank, own_sum, from_core, from_y, from_x, from_z, small_wide, small, all_small, small_out,
     small_in, small_rep, probs, normed, qkv, attended, middle, normed_ffn, active, slope, seed,
-    grad_mid, mid_low, grad_att, block_out, rel, rel_grad, gain_a, gain_f, gain_a_grad,
-    gain_f_grad, strip, grad_scores, grad_q,
+    grad_mid, mid_low, scores, rel, rel_grad, gain_a, gain_f, gain_a_grad,
+    gain_f_grad, strip, grad_scores,
     sends, recvs, sum_sends, sum_recvs, small_sends, small_recvs, back_sends, back_recvs,
     rep_sends, rep_recvs, probs_sems, misc_sems, store_sems, keep_sems,
 ):
     shard = lax.axis_index("fsdp")
     copy_id = lax.axis_index("rep")
     layer = Layer(
-        length=length, x=x, cot=cot, bank=bank, all_small=all_small, small_out=small_out,
+        length=length, x=x, bank=bank, all_small=all_small, small_out=small_out,
         probs=probs, probs_far=probs_far, probs_sems=probs_sems, normed=normed, qkv=qkv,
         attended=attended, middle=middle, normed_ffn=normed_ffn, active=active, slope=slope,
-        seed=seed, grad_mid=grad_mid, mid_low=mid_low, grad_att=grad_att, block_out=block_out,
+        seed=seed, grad_mid=grad_mid, mid_low=mid_low, scores=scores,
         rel=rel, rel_grad=rel_grad, gain_a=gain_a, gain_f=gain_f, gain_a_grad=gain_a_grad,
-        gain_f_grad=gain_f_grad, strip=strip, grad_scores=grad_scores, grad_q=grad_q,
+        gain_f_grad=gain_f_grad, strip=strip, grad_scores=grad_scores,
     )
     rows, width = query_own.shape
     chunks = inner_own.shape[1] // width
@@ -898,13 +941,20 @@
     def rep_peer(k):
         return (shard, lax.rem(copy_id + k, 4))
 
-    parts = [query_own, key_own, value_own, output_own]
+    parts = [output_own]
     parts += [inner_own.at[:, pl.ds(i * width, width)] for i in range(chunks)]
     parts += [outer_own.at[pl.ds(i * rows, rows)] for i in range(chunks)]
+    third = width // 3
+    homes = [
+        (part.at[:, pl.ds(u * third, third)], bank.at[gather.z, gather.x, u, :, pl.ds(n * third, third)])
+        for u in range(3)
+        for n, part in enumerate((query_own, key_own, value_own))
+    ]
+    homes += [(part, bank.at[gather.z, gather.x, 3 + u]) for u, part in enumerate(parts)]
     keeps = [
-        pltpu.make_async_copy(part, bank.at[gather.z, gather.x, u], keep_sems.at[u])
-        for u, part in enumerate(parts)
+        pltpu.make_async_copy(part, home, keep_sems.at[u]) for u, (part, home) in enumerate(homes)
     ]
+    keeps.append(pltpu.make_async_copy(cot, seed, misc_sems.at[0]))
     for copy in keeps:
         copy.start()
     small_wide[...] = jnp.zeros_like(small_wide)
@@ -925,8 +975,8 @@
         copy.start()
     gather_step = stepper(
         (
-            (gather.after_y, 6), (gather.after_x, 4), (gather.after_z, 2), (gather.start, 0),
-            (gather.after_core, 7),
+            (gather.after_y, 7), (gather.after_x, 5), (gather.after_pass, 3), (gather.after_z, 2),
+            (gather.start, 0), (gather.after_core, 8),
         ),
         units,
     )
@@ -936,27 +986,20 @@
         copy.wait()
     layer.small_arrays()
     layer.norm_in()
-
-    def early(n):
-        gather_step(n + 2)
-
-    loop(5, early)
-
-    def projects(u):
-        gather_step(u + 7)
+    loop(6, lambda n: gather_step(n + 2))
+
+    def heads(u):
+        gather_step(u + 8)
         layer.project(u)
-
-    loop(3, projects)
-
-    def attends(pair):
-        gather_step(pair + 10)
-        layer.attend(pair)
-
-    loop(pairs, attends)
+        layer.attend(2 * u)
+        layer.attend(2 * u + 1)
+
+    loop(3, heads)
+    gather_step(11)
     layer.middle_rows()
 
     def raises(i):
-        gather_step(i + 16)
+        gather_step(i + 12)
         layer.raise_unit(i)
 
     loop(4, raises)
@@ -964,7 +1007,15 @@
         layer.probs_store(pair, pair % 2).wait()
     for pair in (0, 1):
         layer.probs_load(pair, pair).start()
-    loop(8, layer.outer_grad)
+
+    def outers(i):
+        gather_step(i + 16)
+        layer.outer_grad(4 * i)
+        layer.outer_grad(4 * i + 1)
+        layer.outer_grad(4 * i + 2)
+        layer.outer_grad(4 * i + 3)
+
+    loop(2, outers)
 
     def store(n):
         return pltpu.make_async_copy(own_sum.at[n], own_far.at[n], store_sems.at[n])
@@ -981,10 +1032,12 @@
         units,
     )
     sum_step(0)
+    gather_step(18)
+    sum_step(1)
+    gather_step(19)
     layer.lower()
-    block_store = pltpu.make_async_copy(block_out, block_far, misc_sems.at[0])
+    block_store = pltpu.make_async_copy(mid_low, block_far, misc_sems.at[0])
     block_store.start()
-    sum_step(1)
     loop(8, layer.raised_grad)
     sum_step(2)
 
@@ -996,24 +1049,20 @@
         gather.drain(5 + 2 * i)
 
     loop(2, inners)
+    block_store.wait()
     layer.middle_grad()
     layer.square_grad(attended, lambda c: mid_low[:, c], 7)
     layer.attended_grad()
     rel_grad[...] = jnp.zeros_like(rel_grad)
 
-    def attend_backs(n):
-        sum_step(n + 5)
-        layer.attend_back(2 * n)
-        layer.attend_back(2 * n + 1)
-
-    loop(pairs // 2, attend_backs)
-    sum_step(8)
-
-    def square_grads(u):
+    def heads_back(u):
+        sum_step(u + 5)
+        layer.attend_back(2 * u)
+        layer.attend_back(2 * u + 1)
         layer.square_grad(normed, lambda c: qkv[u, :, c], 4 + u)
-        sum_step(u + 9)
-
-    loop(3, square_grads)
+
+    loop(3, heads_back)
+    loop(4, lambda n: sum_step(n + 8))
     layer.input_grad()
     grad_store = pltpu.make_async_copy(grad_mid, grad_far, misc_sems.at[1])
     grad_store.start()
@@ -1065,7 +1114,6 @@
     loop(units, drain)
     for copy in back_copies + rep_copies:
         copy.wait_send()
-    block_store.wait()
     grad_store.wait()
 
 
@@ -1092,12 +1140,14 @@
             jax.ShapeDtypeStruct((8, 128), wide),
             jax.ShapeDtypeStruct((heads // 2, 2, seq, seq), low),
         ),
-        in_specs=[pl.BlockSpec(memory_space=pltpu.SMEM)] + [within] * 5 + [anywhere] * 6,
+        in_specs=[pl.BlockSpec(memory_space=pltpu.SMEM), within, anywhere]
+        + [within] * 3
+        + [anywhere] * 6,
         out_specs=[anywhere, anywhere, anywhere, within, anywhere],
         scratch_shapes=[
             vm((4, 2, units + 8, rows, width), low),
             vm((units, rows, width), low),
-            vm((units, 4, 2, half, width), low),
+            vm((4, 4, 2, half, width), low),
             vm((units, 4, 2, part, width), low),
             vm((units, 4, 2 * part, width), low),
             vm((units, 4, 2 * part, width), low),
@@ -1118,17 +1168,15 @@
             vm((seq, width), low),
             vm((seq, width), wide),
             vm((seq, width), low),
-            vm((seq, width), low),
-            vm((seq, width), low),
+            vm((2, seq, seq), wide),
             vm((head_rows, 512), wide),
             vm((128, 512), wide),
             vm((1, width), wide),
             vm((1, width), wide),
             vm((1, width), wide),
             vm((1, width), wide),
-            vm((128, 128 * 7), wide),
-            vm((seq, seq), low),
-            vm((seq, 128), low),
+            vm((2, 128, 128 * 7), wide),
+            vm((2, seq, seq), low),
             sems((units, Gather.slots)),
             sems((units, Gather.slots)),
             sems((units, Scatter.slots)),
@@ -1142,7 +1190,7 @@
             sems((2,)),
             sems((2,)),
             sems((units,)),
-            sems((units,)),
+            sems((units + 6,)),
         ],
         compiler_params=pltpu.CompilerParams(
             collective_id=0, has_side_effects=True, vmem_limit_bytes=63 * 2**20
@@ -1151,31 +1199,42 @@
 
 
 def finish_kernel(
-    block_in, grad_in, sums, small, block_out, grad_out, query, key, value, output, gain_a, table,
-    inner, outer, gain_f, sems,
+    block_in, grad_in, sums_far, small, block_out, grad_out, query, key, value, output, gain_a,
+    table, inner, outer, gain_f, sums, sems, sum_sems,
 ):
+    units, rows, width = sums.shape
+    loads = [pltpu.make_async_copy(sums_far.at[n], sums.at[n], sum_sems.at[n]) for n in range(units)]
     copies = [
         pltpu.make_async_copy(block_in, block_out, sems.at[0]),
         pltpu.make_async_copy(grad_in, grad_out, sems.at[1]),
     ]
-    for copy in copies:
+    for copy in loads + copies:
         copy.start()
-    rows, width = query.shape
-    chunks = inner.shape[1] // width
-    for i in range(chunks):
-        outer[i * rows : (i + 1) * rows, :] = sums[i].astype(jnp.float32)
-        inner[:, i * width : (i + 1) * width] = sums[chunks + i].astype(jnp.float32)
-    for n, ref in enumerate((output, query, key, value)):
-        ref[...] = sums[2 * chunks + n].astype(jnp.float32)
     gain_a[...] = small[0:1, :rows]
     gain_f[...] = small[1:2, :rows]
     table[...] = small[2 : 2 + table.shape[0], : table.shape[1]]
+    chunks = inner.shape[1] // width
+    third = width // 3
+    for i in range(chunks):
+        loads[i].wait()
+        outer[i * rows : (i + 1) * rows, :] = sums[i].astype(jnp.float32)
+    for i in range(chunks):
+        loads[chunks + i].wait()
+        inner[:, i * width : (i + 1) * width] = sums[chunks + i].astype(jnp.float32)
+    loads[2 * chunks].wait()
+    output[...] = sums[2 * chunks].astype(jnp.float32)
+    for u in range(3):
+        loads[2 * chunks + 1 + u].wait()
+        for n, ref in enumerate((query, key, value)):
+            ref[:, u * third : (u + 1) * third] = sums[
+                2 * chunks + 1 + u, :, n * third : (n + 1) * third
+            ].astype(jnp.float32)
     for copy in copies:
         copy.wait()
 
 
 def finish_call(block, grad, sums, small, table_shape, inner_shape, outer_shape):
-    rows, width = sums.shape[1:]
+    units, rows, width = sums.shape
     wide = jnp.float32
     anywhere = pl.BlockSpec(memory_space=pl.ANY)
     within = pl.BlockSpec(memory_space=pltpu.VMEM)
@@ -1187,10 +1246,14 @@
             jax.ShapeDtypeStruct(grad.shape, grad.dtype),
         ]
         + [jax.ShapeDtypeStruct(shape, wide) for shape in shapes],
-        in_specs=[anywhere, anywhere, within, within],
-        out_specs=[anywhere, anywhere] + [within] * len(shapes),
-        scratch_shapes=[pltpu.SemaphoreType.DMA((2,))],
-        compiler_params=pltpu.CompilerParams(vmem_limit_bytes=32 * 2**20),
+        in_specs=[anywhere, anywhere, anywhere, within],
+        out_specs=[within] * (2 + len(shapes)),
+        scratch_shapes=[
+            pltpu.VMEM(sums.shape, sums.dtype),
+            pltpu.SemaphoreType.DMA((2,)),
+            pltpu.SemaphoreType.DMA((units,)),
+        ],
+        compiler_params=pltpu.CompilerParams(vmem_limit_bytes=63 * 2**20),
     )(block, grad, sums, small)
 
 

time: 189 us -> 168 us (0.89)
  Pallas kernels: 181 us -> 165 us
  local copies, waits for them, and re-layouts: 4.68 us -> 0 us
    pallas_call x1, Pallas kernels: 178 us -> 160 us  [fused_call(): pl.pallas_call(fused_kernel, out_shape=(jax.ShapeDtypeStruct((seq, width)...]
    unnamed x8 -> x0, local copies, waits for them, and re-layouts: 4.68 us -> none
    pallas_call x1, Pallas kernels: 3.22 us -> 5.68 us  [finish_call(): pl.pallas_call(finish_kernel, out_shape=[jax.ShapeDtypeStruct(block.shape...]
where the time goes in v5:
time: 168 us; the launch traced here: 167 us
  Pallas kernels  165 us (98%)
    pallas_call x1, Pallas kernels, fused_call(): pl.pallas_call(fused_kernel, out_shape=(jax.ShapeDtypeStruct((seq, width)...  160 us
    pallas_call x1, Pallas kernels, finish_call(): pl.pallas_call(finish_kernel, out_shape=[jax.ShapeDtypeStruct(block.shape...  5.68 us

profile of v5, /device:TPU:1, one launch (start us, length us, event | category | flops | bytes accessed | tf_op | source)
XLA Modules:
  0.0 166.9 jit_solution(344794968101504114)
XLA Ops:
  1.3 159.8 %shard_map.203 = (bf16[512,768]{1,0:T(8,128)(2,1)}, f32[512,768]{1,0:T(8,128)}, bf16[12,96,768]{2,1,0:T(8,128)(2,1)}, f32[8,128]{1,0:T(8,128)}, bf16[6,2,512,512]{3,2,1,0:T(8,128)(2,1)}) custom-call(s32[1]{0:T(128)S(6)} %copy.23.length, bf16[512,768]{1,0:T(8,128)(2,1)} %bitcast.8, bf16[512,768]{1,0:T(8,128)(2,1)} %bitcast.9, bf16[1,96]{1,0:T(2,128)(2,1)} %bitcast.10, ...), custom_call_target="tpu_custom_call" | custom-call | tf_op jit(solution)/shard_map/pallas_call | solution.py:1134
  161.1 5.7 %shard_map.204 = (bf16[512,768]{1,0:T(8,128)(2,1)}, f32[512,768]{1,0:T(8,128)}, f32[96,768]{1,0:T(8,128)}, f32[96,768]{1,0:T(8,128)}, f32[96,768]{1,0:T(8,128)},...) custom-call(bf16[512,768]{1,0:T(8,128)(2,1)} %get-tuple-element.26.b, ...), custom_call_target="tpu_custom_call" | custom-call | tf_op jit(solution)/shard_map/pallas_call | solution.py:1242
